TPU v7x, 256 devices: a whole 4x4x8 slice. The times are simulated.
256 devices in a mesh: seq: 32 (over y_hi, z, core), chan: 8 (over y_lo, x).
Axes of the slice: x: 4, y: 4 (y_hi: 2, y_lo: 2; y = y_hi * 2 + y_lo), z: 8, core: 2. Of those that a mesh axis runs over, the one named last changes fastest.
Arguments:
- tokens: bfloat16 [131072, 1024], P('seq', 'chan'), may hold values from -9 to 9
- gain_in: float32 [1024], P('chan'), may hold values from 0.1 to 1.9
- right_in: bfloat16 [512, 512], replicated, may hold values from -0.25 to 0.25
- twiddle_in: float32 [256, 512], P('seq'), may hold values from -1.5 to 1.5
- left_in: bfloat16 [256, 256], replicated, may hold values from -0.375 to 0.375
- kernel: bfloat16 [256, 512, 1024], P(None, 'seq', 'chan'), may hold values from -5 to 5
- left_out: bfloat16 [256, 256], replicated, may hold values from -0.375 to 0.375
- right_out: bfloat16 [512, 512], replicated, may hold values from -0.25 to 0.25
- twiddle_out: float32 [256, 512], P('seq'), may hold values from -1.5 to 1.5
- gain_mlp: float32 [1024], replicated, may hold values from 0.1 to 1.9
- w_gate: bfloat16 [1024, 4096], P(None, 'chan'), may hold values from -0.1875 to 0.1875
- w_up: bfloat16 [1024, 4096], P(None, 'chan'), may hold values from -0.1875 to 0.1875
- w_down: bfloat16 [4096, 1024], P('chan'), may hold values from -0.09375 to 0.09375
Outputs:
- layer_out: bfloat16 [131072, 1024], P('seq', 'chan')
All inputs are finite; a program needn't handle non-finite values.
Results may differ from a plain program's by a relative error of at most 0.013.
Values may be sent and summed in bfloat16 or wider, within the bound.
No kernel may reach another device: no remote copies, remote signals or barrier semaphores. Data moves between devices by JAX's collectives and lax.ppermute only.
A program may use at most 128 MiB of HBM per device.

v0:
```python
import jax
import jax.numpy as jnp
from jax import lax
from jax.sharding import PartitionSpec as P

epsilon = 1e-06


def local(
    tokens,
    gain_in,
    right_in,
    twiddle_in,
    left_in,
    kernel,
    left_out,
    right_out,
    twiddle_out,
    gain_mlp,
    w_gate,
    w_up,
    w_down,
):
    tok_rows = tokens.shape[0]
    own_width = tokens.shape[1]
    inner_len = right_in.shape[0]
    full_width = own_width * lax.axis_size("chan")
    chan_index = lax.axis_index("chan")
    tok_float = tokens.astype(jnp.float32)
    energy_in = lax.psum(jnp.sum(tok_float * tok_float, axis=1), "chan")
    row_scale = lax.rsqrt(energy_in / full_width + epsilon)[:, None]
    normed_in = (tok_float * row_scale * gain_in).astype(jnp.bfloat16)
    normed_in = normed_in.reshape(tok_rows // inner_len, inner_len, own_width)
    factor_one = jnp.einsum("rq,pqd->prd", right_in, normed_in, preferred_element_type=jnp.float32)
    factor_one = (factor_one * twiddle_in[:, :, None]).astype(jnp.bfloat16)
    column_major = lax.all_to_all(factor_one, "seq", split_axis=1, concat_axis=0, tiled=True)
    factor_two = jnp.einsum(
        "sp,prd->srd", left_in, column_major, preferred_element_type=jnp.float32
    )
    factor_two = (factor_two * kernel.astype(jnp.float32)).astype(jnp.bfloat16)
    factor_three = jnp.einsum(
        "ts,srd->trd", left_out, factor_two, preferred_element_type=jnp.float32
    ).astype(jnp.bfloat16)
    returned = lax.all_to_all(factor_three, "seq", split_axis=0, concat_axis=1, tiled=True)
    mixed = jnp.einsum("ur,prd->pud", right_out, returned, preferred_element_type=jnp.float32)
    mixed = mixed * twiddle_out[:, :, None]
    stream = (tok_float + mixed.reshape(tok_rows, own_width)).astype(jnp.bfloat16)
    stream_float = stream.astype(jnp.float32)
    energy_mlp = lax.psum(jnp.sum(stream_float * stream_float, axis=1), "chan")
    scale_mlp = lax.rsqrt(energy_mlp / full_width + epsilon)[:, None]
    own_gain = lax.dynamic_slice_in_dim(gain_mlp, chan_index * own_width, own_width, 0)
    normed_mlp = (stream_float * scale_mlp * own_gain).astype(jnp.bfloat16)
    shard_part = lax.all_gather(normed_mlp, "chan", axis=1, tiled=True)
    gate_proj = jnp.dot(shard_part, w_gate, preferred_element_type=jnp.float32)
    up_proj = jnp.dot(shard_part, w_up, preferred_element_type=jnp.float32)
    hidden = (jax.nn.silu(gate_proj) * up_proj).astype(jnp.bfloat16)
    summed = (
        lax.psum_scatter(
            lax.dot_general(
                w_down, hidden, (((0,), (1,)), ((), ())), preferred_element_type=jnp.float32
            ).astype(jnp.bfloat16),
            "chan",
            scatter_dimension=0,
            tiled=True,
        )
        .astype(jnp.float32)
        .T
    )
    return (stream.astype(jnp.float32) + summed).astype(jnp.bfloat16)


def solution(mesh):
    in_specs = (
        P("seq", "chan"),
        P("chan"),
        P(),
        P("seq", None),
        P(),
        P(None, "seq", "chan"),
        P(),
        P(),
        P("seq", None),
        P(),
        P(None, "chan"),
        P(None, "chan"),
        P("chan", None),
    )
    out_specs = P("seq", "chan")
    return jax.shard_map(local, mesh=mesh, in_specs=in_specs, out_specs=out_specs, check_vma=False)
```

profile of v0, /device:TPU:1, one launch (start us, length us, event | category | flops | bytes accessed | tf_op | source)
XLA Modules:
  0.0 406.1 jit_solution(10960375884545051717)
XLA Ops:
  6.5 0.0 copy-start
  6.5 0.0 copy-start.10
  6.5 0.0 copy-start.7
  6.5 2.0 fusion.1
  8.5 28.1 %psum.14 = f32[4096]{0:T(1024)S(1)} all-reduce(f32[4096]{0:T(1024)S(1)} %fusion.1), channel_id=1, replica_groups=mesh['seq'=32,'chan'=8] {'chan'}, use_global_device_ids=true, to_apply=%region_1.0 | all-reduce | flops 4096 | bytes 32768 | tf_op jit(solution)/shard_map/psum | solution.py:30
  36.6 1.8 fusion.3
  38.4 0.0 copy-done.10
  38.4 0.0 copy-done.7
  38.4 0.8 fusion.11
  39.1 0.0 copy-start.2
  39.2 1.5 copy.26
  40.6 18.7 %all-to-all-start = ((bf16[8,512,128]{2,0,1:T(8,128)(2,1)}), bf16[8,512,128]{2,0,1:T(8,128)(2,1)S(1)}, u32[]{:S(2)}, u32[]{:S(2)}) async-start(bf16[8,512,128]{2,0,1:T(8,128)(2,1)} %copy.26), calls=%async_computation | async-start | bytes 2097152 | tf_op jit(solution)/shard_map/all_to_all | solution.py:36
  59.3 0.0 copy-done.2
  59.3 0.0 copy-start.8
  59.3 0.0 copy-start.9
  59.3 1.6 copy.30
  60.9 0.0 copy-start.3
  60.9 26.1 %all-to-all-done = bf16[8,512,128]{2,0,1:T(8,128)(2,1)S(1)} async-done(((bf16[8,512,128]{2,0,1:T(8,128)(2,1)}), bf16[8,512,128]{2,0,1:T(8,128)(2,1)S(1)}, u32[]{:S(2)}, u32[]{:S(2)}) %all-to-all-start) | async-done | bytes 1048608 | tf_op jit(solution)/shard_map/all_to_all | solution.py:36
  87.0 1.2 copy.28
  88.2 0.0 copy-done.8
  88.2 0.0 copy-done.9
  88.2 0.0 copy-done.3
  88.2 2.1 fusion.10
  90.3 1.8 copy.31
  92.1 0.0 copy-start.4
  92.1 0.0 copy-start.5
  92.1 6.3 %all-to-all-start.1 = ((bf16[256,16,128]{2,1,0:T(8,128)(2,1)}), bf16[256,16,128]{2,1,0:T(8,128)(2,1)S(1)}, u32[]{:S(2)}, u32[]{:S(2)}) async-start(bf16[256,16,128]{2,1,0:T(8,128)(2,1)} %copy.31), calls=%async_computation.1 | async-start | bytes 2097152 | tf_op jit(solution)/shard_map/all_to_all | solution.py:44
  98.5 0.0 all-gather.2.cloned.1.call-start
  98.5 0.8 dynamic_slice.3
  99.3 26.9 %all-to-all-done.1 = bf16[256,16,128]{2,1,0:T(8,128)(2,1)S(1)} async-done(((bf16[256,16,128]{2,1,0:T(8,128)(2,1)}), bf16[256,16,128]{2,1,0:T(8,128)(2,1)S(1)}, u32[]{:S(2)}, u32[]{:S(2)}) %all-to-all-start.1) | async-done | bytes 1048608 | tf_op jit(solution)/shard_map/all_to_all | solution.py:44
  126.2 0.2 copy.32
  126.4 0.0 copy-done.4
  126.4 0.0 copy-done.5
  126.4 2.1 multiply_bitcast_fusion
  128.5 0.0 copy-start.1
  128.5 3.0 copy.34
  131.5 0.0 copy-done.1
  131.5 2.2 fusion.5
  133.7 23.7 %psum.15 = f32[4096]{0:T(1024)S(1)} all-reduce(f32[4096]{0:T(1024)S(1)} %get-tuple-element.5), channel_id=1, replica_groups=mesh['seq'=32,'chan'=8] {'chan'}, use_global_device_ids=true, to_apply=%region_3.0 | all-reduce | flops 4096 | bytes 32768 | tf_op jit(solution)/shard_map/psum | solution.py:49
  157.4 1.5 fusion.7
  158.9 0.0 all-gather.2.cloned.1.call-update
  158.9 0.0 copy-start.6
  159.0 0.2 reduce-scatter.4.cloned.1.call-start
  159.2 99.2 %all-gather.2.cloned.1.call-done = bf16[4096,1024]{1,0:T(8,128)(2,1)} async-done(((bf16[4096,128]{1,0:T(8,128)(2,1)}), bf16[4096,1024]{1,0:T(8,128)(2,1)}) %all-gather.2.cloned.1.call-update) | async-done | bytes 8388624 | tf_op jit(solution)/shard_map/all_gather | solution.py:53
  258.4 11.4 %fusion.21 = f32[4096,512]{1,0:T(8,128)} fusion(bf16[4096,1024]{1,0:T(8,128)(2,1)} %all-gather.2.cloned.1.call-done, bf16[1024,512]{1,0:T(8,128)(2,1)} %param.23), kind=kOutput, calls=%fused_computation.32 | convolution fusion | flops 4294967296 | bytes 17825792 | tf_op jit(solution)/shard_map/dot_general | solution.py:54
  269.7 0.0 copy-done
  269.7 0.0 copy-done.6
  269.8 15.5 %convert_bitcast_fusion = bf16[1024,4096]{0,1:T(8,128)(2,1)} fusion(bf16[512,1024]{1,0:T(8,128)(2,1)S(1)} %copy-done, f32[4096,512]{1,0:T(8,128)} %fusion.21, bf16[4096,1024]{1,0:T(8,128)(2,1)} %all-gather.2.cloned.1.call-done, bf16[1024,512]{1,0:T(8,128)(2,1)S(1)} %copy-done.6), kind=kOutput, calls=%fused_computation | convolution fusion | flops 8606711808 | bytes 27262976 | tf_op jit(solution)/shard_map/dot_general | solution.py:59
  285.3 11.3 %copy.38 = bf16[1024,4096]{1,0:T(8,128)(2,1)} copy(bf16[1024,4096]{0,1:T(8,128)(2,1)} %convert_bitcast_fusion) | data formatting | bytes 16777216
  296.6 0.0 reduce-scatter.4.cloned.1.call-update
  296.6 99.8 %reduce-scatter.4.cloned.1.call-done = bf16[128,4096]{1,0:T(8,128)(2,1)} async-done(((bf16[1024,4096]{1,0:T(8,128)(2,1)}), bf16[128,4096]{1,0:T(8,128)(2,1)}) %reduce-scatter.4.cloned.1.call-update) | async-done | bytes 1048592
  396.4 1.6 copy.39
  398.0 1.2 fusion.8
  (2 shorter events, 0.0 us)
Async XLA Ops:
  6.5 263.2 %copy-start = (bf16[512,1024]{1,0:T(8,128)(2,1)S(1)}, bf16[512,1024]{1,0:T(8,128)(2,1)}, u32[]{:S(2)}) copy-start(bf16[512,1024]{1,0:T(8,128)(2,1)} %param.25) | copy-start | bytes 3145732
  6.5 31.8 %copy-start.10 = (f32[8,512]{1,0:T(8,128)S(1)}, f32[8,512]{1,0:T(8,128)}, u32[]{:S(2)}) copy-start(f32[8,512]{1,0:T(8,128)} %param.16) | copy-start | bytes 49156
  6.5 31.8 %copy-start.7 = (bf16[512,512]{1,0:T(8,128)(2,1)S(1)}, bf16[512,512]{1,0:T(8,128)(2,1)}, u32[]{:S(2)}) copy-start(bf16[512,512]{1,0:T(8,128)(2,1)} %param.15) | copy-start | bytes 1572868
  39.1 20.1 %copy-start.2 = (bf16[256,16,128]{2,1,0:T(8,128)(2,1)S(1)}, bf16[256,16,128]{2,1,0:T(8,128)(2,1)}, u32[]{:S(2)}) copy-start(bf16[256,16,128]{2,1,0:T(8,128)(2,1)} %param.18) | copy-start | bytes 3145732
  40.6 46.4 %all-to-all-start = ((bf16[8,512,128]{2,0,1:T(8,128)(2,1)}), bf16[8,512,128]{2,0,1:T(8,128)(2,1)S(1)}, u32[]{:S(2)}, u32[]{:S(2)}) async-start(bf16[8,512,128]{2,0,1:T(8,128)(2,1)} %copy.26), calls=%async_computation | async-start | bytes 2097152 | tf_op jit(solution)/shard_map/all_to_all | solution.py:36
  59.3 28.9 %copy-start.8 = (bf16[256,256]{1,0:T(8,128)(2,1)S(1)}, bf16[256,256]{1,0:T(8,128)(2,1)}, u32[]{:S(2)}) copy-start(bf16[256,256]{1,0:T(8,128)(2,1)} %param.19) | copy-start | bytes 393220
  59.3 28.9 %copy-start.9 = (bf16[256,256]{1,0:T(8,128)(2,1)S(1)}, bf16[256,256]{1,0:T(8,128)(2,1)}, u32[]{:S(2)}) copy-start(bf16[256,256]{1,0:T(8,128)(2,1)} %param.17) | copy-start | bytes 393220
  60.9 27.3 %copy-start.3 = (bf16[256,16,128]{0,2,1:T(8,128)(2,1)S(1)}, bf16[256,16,128]{0,2,1:T(8,128)(2,1)}, u32[]{:S(2)}) copy-start(bf16[256,16,128]{0,2,1:T(8,128)(2,1)} %copy.30) | copy-start | bytes 3145732
  92.1 34.3 %copy-start.4 = (bf16[512,512]{1,0:T(8,128)(2,1)S(1)}, bf16[512,512]{1,0:T(8,128)(2,1)}, u32[]{:S(2)}) copy-start(bf16[512,512]{1,0:T(8,128)(2,1)} %param.20) | copy-start | bytes 1572868
  92.1 34.3 %copy-start.5 = (f32[8,512]{1,0:T(8,128)S(1)}, f32[8,512]{1,0:T(8,128)}, u32[]{:S(2)}) copy-start(f32[8,512]{1,0:T(8,128)} %param.21) | copy-start | bytes 49156
  92.1 34.1 %all-to-all-start.1 = ((bf16[256,16,128]{2,1,0:T(8,128)(2,1)}), bf16[256,16,128]{2,1,0:T(8,128)(2,1)S(1)}, u32[]{:S(2)}, u32[]{:S(2)}) async-start(bf16[256,16,128]{2,1,0:T(8,128)(2,1)} %copy.31), calls=%async_computation.1 | async-start | bytes 2097152 | tf_op jit(solution)/shard_map/all_to_all | solution.py:44
  98.5 159.9 %all-gather.2.cloned.1.call-start = ((), (), s32[]{:S(2)}) async-start(), calls=%async_computation.3 | async-start | bytes 9437184 | tf_op jit(solution)/shard_map/all_gather | solution.py:53
  128.5 3.0 copy-start.1
  158.9 110.8 %copy-start.6 = (bf16[1024,512]{1,0:T(8,128)(2,1)S(1)}, bf16[1024,512]{1,0:T(8,128)(2,1)}, u32[]{:S(2)}) copy-start(bf16[1024,512]{1,0:T(8,128)(2,1)} %param.24) | copy-start | bytes 3145732
  159.0 237.4 %reduce-scatter.4.cloned.1.call-start = ((), (), s32[]{:S(2)}) async-start(), calls=%async_computation.4 | async-start | bytes 9437184
Sparse Core Ops, SparseCore 0:
  159.1 99.2 all-gather.1
  296.7 99.6 reduce-scatter.3
where the time goes:
time: 407 us; the launch traced here: 406 us
  waiting for transfers between devices  252 us (62%)
  blocking collectives  51.7 us (13%)
  matrix products  31.8 us (8%)
  starting transfers between devices  25.3 us (6%)
  local copies, waits for them, and re-layouts  22.9 us (6%)
  between operations  13.6 us (3%)
  other arithmetic  8.69 us (2%)
    unnamed x3, waiting for transfers between devices  99.8 us
    all_gather x1, waiting for transfers between devices, local(): shard_part = lax.all_gather(normed_mlp, 'chan', axis=1, tiled=True)  99.2 us
    psum x1, blocking collectives, local(): energy_in = lax.psum(jnp.sum(tok_float * tok_float, axis=1), 'chan')  28.1 us
    all_to_all x1, waiting for transfers between devices, local(): lax.all_to_all(factor_three, 'seq', split_axis=0, concat_axis=1, tiled=True)  26.9 us
    all_to_all x1, waiting for transfers between devices, local(): lax.all_to_all(factor_one, 'seq', split_axis=1, concat_axis=0, tiled=True)  26.1 us
    psum x1, blocking collectives, local(): energy_mlp = lax.psum(jnp.sum(stream_float * stream_float, axis=1), 'chan')  23.7 us
    all_to_all x1, starting transfers between devices, local(): lax.all_to_all(factor_one, 'seq', split_axis=1, concat_axis=0, tiled=True)  18.7 us
    dot_general x1, matrix products, local(): lax.dot_general(w_down, hidden, (((0,), (1,)), ((), ())), preferred_eleme...  15.5 us
  transfers between devices with their start and end apart: 4, of which 4 were waited for; matrix products, arithmetic and copies ran while one was open for 1% of the time, Pallas kernels for 0%

commit v1 on v0

v1 whole, which is shorter than its diff:
```python
import functools

import jax
import jax.numpy as jnp
from jax import lax
from jax.experimental import pallas as pl
from jax.experimental.pallas import tpu as pltpu
from jax.sharding import PartitionSpec as P

EPS = 1e-06
BOTH = ("seq", "chan")
Z, CORE, YLO, X = 8, 2, 2, 4
YHI = 2
BF, F32 = jnp.bfloat16, jnp.float32


def route(move):
    pairs = []
    for yhi in range(YHI):
        for z in range(Z):
            for core in range(CORE):
                for ylo in range(YLO):
                    for x in range(X):
                        a, b, c, d, e = move(yhi, z, core, ylo, x)
                        src = (((yhi * Z + z) * CORE + core) * YLO + ylo) * X + x
                        dst = (((a * Z + b) * CORE + c) * YLO + d) * X + e
                        pairs.append((src, dst))
    return pairs


def along_x(sign):
    def move(yhi, z, core, ylo, x):
        step = sign if core == 0 else -sign
        return yhi, z, core, ylo, (x + step) % X

    return route(move)


def along_y(yhi, z, core, ylo, x):
    y = (yhi * YLO + ylo + (1 if core == 0 else -1)) % (YHI * YLO)
    return y // YLO, z, core, y % YLO, x


def other_core(yhi, z, core, ylo, x):
    return yhi, z, 1 - core, ylo, x


def first_kernel(place, tok, right, tw, out):
    groups, rows, width = tok.shape
    energy = jnp.zeros((rows, 1), F32)
    for g in range(groups):
        t = tok[g].astype(F32)
        energy = energy + jnp.sum(t * t, axis=1, keepdims=True)
    scale = lax.rsqrt(energy / (groups * width) + EPS)
    turned = tw[...].T
    lane = lax.broadcasted_iota(jnp.int32, turned.shape, 1)
    twiddle = jnp.sum(jnp.where(lane == place[0], turned, 0.0), axis=1, keepdims=True)
    for g in range(0, groups, 2):
        pair = [(tok[g + k].astype(F32) * scale).astype(BF) for k in range(2)]
        f = jnp.dot(right[...], jnp.concatenate(pair, axis=1), preferred_element_type=F32)
        f = (f * twiddle).astype(BF)
        for k in range(2):
            part = f[:, k * width : (k + 1) * width]
            out[:, g + k] = part.reshape(out.shape[0], out.shape[2], width)


def middle_kernel(col, left_in, left_out, kern, gain, out, flat, kflat):
    blocks, inner, width = col.shape
    flat[...] = col[...].astype(F32).reshape(blocks * inner, width)
    kflat[...] = (kern[...].astype(F32) * gain[...][None]).reshape(blocks * inner, width)
    for r in range(0, inner, 2):
        at = [pl.ds(r + k, blocks, stride=inner) for k in range(2)]
        x = jnp.concatenate([flat[a, :].astype(BF) for a in at], axis=1)
        k = jnp.concatenate([kflat[a, :] for a in at], axis=1)
        two = jnp.dot(left_in[...], x, preferred_element_type=F32)
        two = (two * k).astype(BF)
        three = jnp.dot(left_out[...], two, preferred_element_type=F32)
        for i, a in enumerate(at):
            flat[a, :] = three[:, i * width : (i + 1) * width]
    out[...] = flat[...].reshape(blocks, inner, width).astype(BF)


def last_kernel(count, place, back, tok, right, tw, gain, *rest):
    packs, out = rest[:count], rest[count]
    weights, acc, normed, sems = rest[count + 1 :]
    for i in range(count):
        pltpu.make_async_copy(packs[i], weights.at[i], sems.at[i]).start()
    groups, rows, width = tok.shape
    full = groups * width
    turned = tw[...].T
    lane = lax.broadcasted_iota(jnp.int32, turned.shape, 1)
    twiddle = jnp.sum(jnp.where(lane == place[0], turned, 0.0), axis=1, keepdims=True)
    energy = jnp.zeros((rows, 1), F32)
    for g in range(0, groups, 2):
        pair = [back[:, g + k].reshape(rows, width) for k in range(2)]
        mixed = jnp.dot(right[...], jnp.concatenate(pair, axis=1), preferred_element_type=F32)
        mixed = mixed * twiddle
        for k in range(2):
            at = pl.ds((g + k) * width, width)
            s = (tok[g + k].astype(F32) + mixed[:, k * width : (k + 1) * width]).astype(BF).astype(F32)
            acc[:, at] = s
            energy = energy + jnp.sum(s * s, axis=1, keepdims=True)
    scale = lax.rsqrt(energy / full + EPS)
    normed[...] = (acc[...] * scale * gain[...]).astype(BF)
    hid = weights.shape[2] // 2

    @pl.loop(0, count)
    def _(i):
        pltpu.make_async_copy(packs[0], weights.at[i], sems.at[i]).wait()
        both = jnp.dot(normed[...], weights[i, :full, :], preferred_element_type=F32)
        gate, up = both[:, :hid], both[:, hid:]
        hidden = (gate * up / (1.0 + jnp.exp(-gate))).astype(BF)
        half = full // 2
        for k in range(2):
            down = weights[i, full + k * hid : full + (k + 1) * hid, :]
            acc[:, k * half : (k + 1) * half] += jnp.dot(hidden, down, preferred_element_type=F32)

    for g in range(groups):
        out[g] = acc[:, g * width : (g + 1) * width].astype(BF)


def local(tokens, gain_in, right_in, twiddle_in, left_in, kernel, left_out, right_out, twiddle_out, gain_mlp, w_gate, w_up, w_down):
    own = tokens.shape[1]
    inner = right_in.shape[0]
    n_chan = lax.axis_size("chan")
    n_seq = lax.axis_size("seq")
    blocks = left_in.shape[0]
    full = own * n_chan
    r_own = kernel.shape[1]
    hid = w_gate.shape[1] // 2
    place = lax.axis_index("chan").astype(jnp.int32)[None]
    core = lax.axis_index("seq") % CORE

    vmem = pl.BlockSpec(memory_space=pltpu.VMEM)
    smem = pl.BlockSpec(memory_space=pltpu.SMEM)
    any_ = pl.BlockSpec(memory_space=pl.ANY)

    tok = lax.all_to_all(tokens.reshape(n_chan, inner, own), "chan", 0, 0, tiled=True)

    def pack(side):
        at = side * hid
        cut = lambda w, axis: lax.dynamic_slice_in_dim(w, at, hid, axis)
        d = cut(w_down, 0)
        up = jnp.concatenate([cut(w_gate, 1), cut(w_up, 1)], axis=1)
        return jnp.concatenate([up, d[:, : full // 2], d[:, full // 2 :]], axis=0)

    mine, other = pack(core), pack(1 - core)
    mine, tok = lax.optimization_barrier((mine, tok))
    fwd, bwd, yy, swap = along_x(1), along_x(-1), route(along_y), route(other_core)
    go = lambda x, pairs: lax.ppermute(x, BOTH, pairs)
    a, b, y = go(mine, fwd), go(mine, bwd), go(mine, yy)
    aa, ya, yb = go(a, fwd), go(a, yy), go(b, yy)
    yaa = go(aa, yy)
    got = [y, a, b, ya, yb, aa, yaa]
    packs = [mine, other] + got + [go(g, swap) for g in got]

    f1 = pl.pallas_call(
        first_kernel,
        out_shape=jax.ShapeDtypeStruct((n_seq, n_chan, r_own, own), BF),
        in_specs=[smem] + [vmem] * 3,
        out_specs=vmem,
        compiler_params=pltpu.CompilerParams(vmem_limit_bytes=32 << 20),
        name="first",
    )(place, tok, right_in, twiddle_in)
    col = lax.all_to_all(f1.reshape(n_seq * n_chan, r_own, own), BOTH, 0, 0, tiled=True)
    f3 = pl.pallas_call(
        middle_kernel,
        out_shape=jax.ShapeDtypeStruct((blocks, r_own, own), BF),
        in_specs=[vmem] * 5,
        out_specs=vmem,
        scratch_shapes=[pltpu.VMEM((blocks * r_own, own), F32)] * 2,
        compiler_params=pltpu.CompilerParams(vmem_limit_bytes=32 << 20),
        name="middle",
    )(col, left_in, left_out, kernel, gain_in[None])
    back = lax.all_to_all(f3, BOTH, 0, 0, tiled=True).reshape(n_seq, n_chan, r_own, own)
    count = len(packs)


    done = pl.pallas_call(
        functools.partial(last_kernel, count),
        out_shape=jax.ShapeDtypeStruct((n_chan, inner, own), BF),
        in_specs=[smem] + [vmem] * 5 + [any_] * count,
        out_specs=vmem,
        scratch_shapes=[
            pltpu.VMEM((count,) + mine.shape, BF),
            pltpu.VMEM((inner, full), F32),
            pltpu.VMEM((inner, full), BF),
            pltpu.SemaphoreType.DMA((count,)),
        ],
        compiler_params=pltpu.CompilerParams(vmem_limit_bytes=56 << 20),
        name="last",
    )(place, back, tok, right_out, twiddle_out, gain_mlp[None], *packs)
    out = lax.all_to_all(done, "chan", 0, 0, tiled=True)
    return out.reshape(tokens.shape)


def solution(mesh):
    in_specs = (
        P("seq", "chan"),
        P("chan"),
        P(),
        P("seq", None),
        P(),
        P(None, "seq", "chan"),
        P(),
        P(),
        P("seq", None),
        P(),
        P(None, "chan"),
        P(None, "chan"),
        P("chan", None),
    )
    return jax.shard_map(local, mesh=mesh, in_specs=in_specs, out_specs=P("seq", "chan"), check_vma=False)
```

time: 407 us -> 200 us (0.49)
  waiting for transfers between devices: 252 us -> 101 us
  blocking collectives: 51.7 us -> 19.3 us
  matrix products: 31.8 us -> 0 us
  Pallas kernels: 0 us -> 25.6 us
  starting transfers between devices: 25.3 us -> 46.9 us
  local copies, waits for them, and re-layouts: 22.9 us -> 4.4 us
  between operations: 13.6 us -> 0.16 us
  other arithmetic: 8.69 us -> 2.64 us
    unnamed x3 -> x0, waiting for transfers between devices: 99.8 us -> none
    all_gather x1 -> x0, waiting for transfers between devices: 99.2 us -> none  [local(): shard_part = lax.all_gather(normed_mlp, 'chan', axis=1, tiled=True)]
    ppermute x0 -> x14, waiting for transfers between devices: none -> 64.8 us  [local(): go = lambda x, pairs: lax.ppermute(x, BOTH, pairs)]
    psum x2 -> x0, blocking collectives: 51.7 us -> none  [the longest x1 28.1 us: local(): energy_in = lax.psum(jnp.sum(tok_float * tok_float, axis=1), 'chan')]
    dot_general x5 -> x0, matrix products: 31.8 us -> none  [the longest x1 15.5 us: local(): lax.dot_general(w_down, hidden, (((0,), (1,)), ((), ())), preferred_eleme...]
    pallas_call x0 -> x3, Pallas kernels: none -> 25.6 us  [the longest x1 20.2 us: local(): pl.pallas_call(functools.partial(last_kernel, count), out_shape=jax.Shape...]
    all_to_all x0 -> x1, blocking collectives: none -> 19.3 us  [local(): out = lax.all_to_all(done, 'chan', 0, 0, tiled=True)]
    all_to_all x2 -> x3, waiting for transfers between devices: 53.1 us -> 35.7 us  [the longest x1 24.6 us: local(): lax.all_to_all(f1.reshape(n_seq * n_chan, r_own, own), BOTH, 0, 0, tiled=...]
  transfers between devices with their start and end apart: 4 -> 17, of which waited for: 4 -> 6; matrix products, arithmetic and copies ran while one was open for 1% -> 3% of each run, Pallas kernels for 0% -> 3%
where the time goes in v1:
time: 200 us
  waiting for transfers between devices  101 us (50%)
  starting transfers between devices  46.9 us (23%)
  Pallas kernels  25.6 us (13%)
  blocking collectives  19.3 us (10%)
  local copies, waits for them, and re-layouts  4.4 us (2%)
  other arithmetic  2.64 us (1%)
    ppermute x14, waiting for transfers between devices, local(): go = lambda x, pairs: lax.ppermute(x, BOTH, pairs)  64.8 us
    all_to_all x1, waiting for transfers between devices, local(): lax.all_to_all(f1.reshape(n_seq * n_chan, r_own, own), BOTH, 0, 0, tiled=...  24.6 us
    pallas_call x1, Pallas kernels, local(): pl.pallas_call(functools.partial(last_kernel, count), out_shape=jax.Shape...  20.2 us
    all_to_all x1, blocking collectives, local(): out = lax.all_to_all(done, 'chan', 0, 0, tiled=True)  19.3 us
    all_to_all x1, starting transfers between devices, local(): lax.all_to_all(f1.reshape(n_seq * n_chan, r_own, own), BOTH, 0, 0, tiled=...  18.2 us
    ppermute x14, starting transfers between devices, local(): go = lambda x, pairs: lax.ppermute(x, BOTH, pairs)  15.4 us
    all_to_all x1, waiting for transfers between devices, local(): lax.all_to_all(tokens.reshape(n_chan, inner, own), 'chan', 0, 0, tiled=True)  11.1 us
    all_to_all x1, starting transfers between devices, local(): lax.all_to_all(f3, BOTH, 0, 0, tiled=True)  7.43 us
  transfers between devices with their start and end apart: 17, of which 6 were waited for; matrix products, arithmetic and copies ran while one was open for 3% of the time, Pallas kernels for 3%

profile of v1, /device:TPU:1, one launch (start us, length us, event | category | flops | bytes accessed | tf_op | source)
XLA Modules:
  0.0 199.5 jit_solution(12494689763641332375)
XLA Ops:
  0.0 5.9 %all-to-all-start = ((bf16[8,512,128]{2,1,0:T(8,128)(2,1)}), bf16[8,512,128]{2,1,0:T(8,128)(2,1)S(1)}, u32[]{:S(2)}, u32[]{:S(2)}) async-start(bf16[8,512,128]{2,1,0:T(8,128)(2,1)} %bitcast.10), calls=%async_computation | async-start | bytes 2097152 | tf_op jit(solution)/shard_map/all_to_all | solution.py:138
  5.9 0.0 copy-start.10
  5.9 0.0 copy-start.11
  5.9 2.2 %constant_dynamic-slice_fusion.1 = (bf16[256,512]{1,0:T(8,128)(2,1)}, bf16[256,512]{1,0:T(8,128)(2,1)S(1)}, bf16[256,512]{1,0:T(8,128)(2,1)}, bf16[256,512]{1,0:T(8,128)(2,1)S(1)}) fusion(bf16[512,1024]{1,0:T(8,128)(2,1)} %param.25, s32[]{:T(128)S(6)} %select_n.19, s32[]{:T(128)S(6)} %select_n.18, s32[]{:T(128)S(6)} %add.17), kind=kLoop, calls=%fused_computation.3 | loop fusion | bytes 2097164 | tf_op jit(solution)/shard_map/slice | solution.py:145
  8.1 0.0 copy-done.10
  8.1 0.0 copy-done.11
  8.2 1.1 constant_dynamic-slice_fusion.2
  9.3 0.0 copy-start.2
  9.3 1.3 pad_maximum_fusion.rest_0_
  10.6 11.1 %all-to-all-done.tok = bf16[8,512,128]{2,1,0:T(8,128)(2,1)S(1)} async-done(((bf16[8,512,128]{2,1,0:T(8,128)(2,1)}), bf16[8,512,128]{2,1,0:T(8,128)(2,1)S(1)}, u32[]{:S(2)}, u32[]{:S(2)}) %all-to-all-start) | async-done | bytes 1048608 | tf_op jit(solution)/shard_map/all_to_all | solution.py:138
  21.7 0.0 copy-start
  21.7 0.6 collective-permute-start.1
  22.3 0.8 collective-permute-start.2
  23.1 1.7 collective-permute-start
  24.9 31.3 %collective-permute-done.1.rest_3_ = bf16[1536,512]{1,0:T(8,128)(2,1)} collective-permute-done((bf16[1536,512]{1,0:T(8,128)(2,1)}, bf16[1536,512]{1,0:T(8,128)(2,1)}, u32[]{:S(2)}, u32[]{:S(2)}) %collective-permute-start.1) | collective-permute-done | bytes 1572896 | tf_op jit(solution)/shard_map/ppermute | solution.py:150
  56.2 0.4 collective-permute-start.5
  56.6 0.0 copy-done.2
  56.6 0.0 copy-done.5
  56.6 2.2 %first.1 = bf16[32,8,16,128]{3,2,1,0:T(8,128)(2,1)} custom-call(s32[1]{0:T(128)} %bitcast.place, bf16[8,512,128]{2,1,0:T(8,128)(2,1)S(1)} %all-to-all-done.tok, bf16[512,512]{1,0:T(8,128)(2,1)S(1)} %copy-done.2, f32[8,512]{1,0:T(8,128)S(1)} %copy-done.5), custom_call_target="tpu_custom_call" | custom-call | tf_op jit(solution)/shard_map/first/pallas_call | solution.py:157
  58.7 0.0 copy-start.1
  58.7 0.0 copy-start.3
  58.7 0.0 copy-start.6
  58.7 0.0 copy-done
  58.7 18.2 %all-to-all-start.1 = ((bf16[256,16,128]{2,1,0:T(8,128)(2,1)}), bf16[256,16,128]{2,1,0:T(8,128)(2,1)S(1)}, u32[]{:S(2)}, u32[]{:S(2)}) async-start(bf16[256,16,128]{2,1,0:T(8,128)(2,1)} %bitcast.2), calls=%async_computation.1 | async-start | bytes 2097152 | tf_op jit(solution)/shard_map/all_to_all | solution.py:165
  76.9 0.0 collective-permute-done.2.rest_4_
  76.9 2.2 %collective-permute-start.9 = (bf16[1536,512]{1,0:T(8,128)(2,1)}, bf16[1536,512]{1,0:T(8,128)(2,1)}, u32[]{:S(2)}, u32[]{:S(2)}) collective-permute-start(bf16[1536,512]{1,0:T(8,128)(2,1)} %collective-permute-done.2.rest_4_), channel_id=1, source_target_pairs={{0,8},{1,9},{2,10},{3,11},{4,12},{5,13},{6,14},{7,15},{8,0},{9,1},... | collective-permute-start | bytes 4718600 | tf_op jit(solution)/shard_map/ppermute | solution.py:150
  79.2 0.9 collective-permute-start.4
  80.0 0.0 collective-permute-start.8
  80.0 0.0 collective-permute-done.rest_2_
  80.0 2.2 %collective-permute-start.3 = (bf16[1536,512]{1,0:T(8,128)(2,1)}, bf16[1536,512]{1,0:T(8,128)(2,1)}, u32[]{:S(2)}, u32[]{:S(2)}) collective-permute-start(bf16[1536,512]{1,0:T(8,128)(2,1)} %collective-permute-done.1.rest_3_), channel_id=1, source_target_pairs={{0,4},{1,5},{2,6},{3,7},{4,128},{5,129},{6,130},{7,131},{8,140},{9... | collective-permute-start | bytes 4718600 | tf_op jit(solution)/shard_map/ppermute | solution.py:150
  82.2 0.0 collective-permute-done.5.rest_7_
  82.2 0.1 collective-permute-start.6
  82.3 24.6 %all-to-all-done.1.col = bf16[256,16,128]{2,1,0:T(8,128)(2,1)S(1)} async-done(((bf16[256,16,128]{2,1,0:T(8,128)(2,1)}), bf16[256,16,128]{2,1,0:T(8,128)(2,1)S(1)}, u32[]{:S(2)}, u32[]{:S(2)}) %all-to-all-start.1) | async-done | bytes 1048608 | tf_op jit(solution)/shard_map/all_to_all | solution.py:165
  106.9 0.0 copy-done.1
  106.9 0.0 copy-done.3
  106.9 0.0 copy-done.4
  106.9 0.0 copy-done.6
  107.0 3.3 %middle.1 = bf16[256,16,128]{2,1,0:T(8,128)(2,1)} custom-call(bf16[256,16,128]{2,1,0:T(8,128)(2,1)S(1)} %all-to-all-done.1.col, bf16[256,256]{1,0:T(8,128)(2,1)S(1)} %copy-done.3, bf16[256,256]{1,0:T(8,128)(2,1)S(1)} %copy-done.4, bf16[256,16,128]{2,1,0:T(8,128)(2,1)S(1)} %copy-done.1, f32[1,128]{1,0:T(1,128)S(1)} %bitcast.7), custom_call_target="tpu_custom_call" | custom-call | tf_op jit(solution)/shard_map/middle/pallas_call | solution.py:166
  110.2 7.4 %all-to-all-start.2 = ((bf16[256,16,128]{2,1,0:T(8,128)(2,1)}), bf16[256,16,128]{2,1,0:T(8,128)(2,1)S(1)}, u32[]{:S(2)}, u32[]{:S(2)}) async-start(bf16[256,16,128]{2,1,0:T(8,128)(2,1)} %middle.1), calls=%async_computation.2 | async-start | bytes 2097152 | tf_op jit(solution)/shard_map/all_to_all | solution.py:175
  117.7 0.0 collective-permute-done.9.rest_11_
  117.7 2.4 %collective-permute-start.7 = (bf16[1536,512]{1,0:T(8,128)(2,1)}, bf16[1536,512]{1,0:T(8,128)(2,1)}, u32[]{:S(2)}, u32[]{:S(2)}) collective-permute-start(bf16[1536,512]{1,0:T(8,128)(2,1)} %collective-permute-done.rest_2_), channel_id=1, source_target_pairs={{0,8},{1,9},{2,10},{3,11},{4,12},{5,13},{6,14},{7,15},{8,0},{9,1},... | collective-permute-start | bytes 4718600 | tf_op jit(solution)/shard_map/ppermute | solution.py:150
  120.0 0.0 collective-permute-done.4.rest_6_
  120.0 0.1 collective-permute-start.12
  120.1 0.0 collective-permute-done.8.rest_10_
  120.1 0.4 collective-permute-start.11
  120.6 9.8 %collective-permute-done.3.rest_5_ = bf16[1536,512]{1,0:T(8,128)(2,1)} collective-permute-done((bf16[1536,512]{1,0:T(8,128)(2,1)}, bf16[1536,512]{1,0:T(8,128)(2,1)}, u32[]{:S(2)}, u32[]{:S(2)}) %collective-permute-start.3) | collective-permute-done | bytes 1572896 | tf_op jit(solution)/shard_map/ppermute | solution.py:150
  130.4 1.5 collective-permute-start.10
  131.8 21.7 %collective-permute-done.6.rest_8_ = bf16[1536,512]{1,0:T(8,128)(2,1)} collective-permute-done((bf16[1536,512]{1,0:T(8,128)(2,1)}, bf16[1536,512]{1,0:T(8,128)(2,1)}, u32[]{:S(2)}, u32[]{:S(2)}) %collective-permute-start.6) | collective-permute-done | bytes 1572896 | tf_op jit(solution)/shard_map/ppermute | solution.py:150
  153.6 2.1 %collective-permute-start.13 = (bf16[1536,512]{1,0:T(8,128)(2,1)}, bf16[1536,512]{1,0:T(8,128)(2,1)}, u32[]{:S(2)}, u32[]{:S(2)}) collective-permute-start(bf16[1536,512]{1,0:T(8,128)(2,1)} %collective-permute-done.6.rest_8_), channel_id=1, source_target_pairs={{0,8},{1,9},{2,10},{3,11},{4,12},{5,13},{6,14},{7,15},{8,0},{9,1},... | collective-permute-start | bytes 4718600 | tf_op jit(solution)/shard_map/ppermute | solution.py:150
  155.7 0.0 copy-done.8
  155.7 0.0 copy-done.9
  155.7 0.0 copy-done.12
  155.7 0.0 copy-done.13
  155.7 1.4 pad_maximum_fusion.1.rest_1_
  157.1 0.0 collective-permute-done.7.rest_9_
  157.1 0.0 all-to-all-done.2
  157.1 0.0 collective-permute-done.11.rest_13_
  157.1 0.0 collective-permute-done.12.rest_14_
  157.1 0.0 collective-permute-done.10.rest_12_
  157.1 2.0 collective-permute-done.13.rest_15_
  159.1 0.0 copy-done.7
  159.1 20.2 %last.1 = bf16[8,512,128]{2,1,0:T(8,128)(2,1)} custom-call(s32[1]{0:T(128)} %bitcast.place, bf16[32,8,16,128]{3,2,1,0:T(8,128)(2,1)} %bitcast.8, bf16[8,512,128]{2,1,0:T(8,128)(2,1)} %copy-done, bf16[512,512]{1,0:T(8,128)(2,1)} %right.3, f32[8,512]{1,0:T(8,128)} %tw.3, f32[1,1024]{1,0:T(1,128)} %bitcast.11, bf16[1536,512]{1,0:T(8,128)(2,1)} %pad_maximum_fusion.rest_0_, ...), custom_call_target="tpu_custom_call" | custom-call | tf_op jit(solution)/shard_map/last/pallas_call | solution.py:179
  179.2 19.3 %all_to_all.20 = bf16[8,512,128]{2,1,0:T(8,128)(2,1)S(1)} all-to-all(bf16[8,512,128]{2,1,0:T(8,128)(2,1)} %last.1), channel_id=1, replica_groups=mesh['seq'=32,'chan'=8] {'chan'}, dimensions={0} | all-to-all | bytes 2097152 | tf_op jit(solution)/shard_map/all_to_all | solution.py:193
  198.6 1.0 copy.15
  (7 shorter events, 0.0 us)
Async XLA Ops:
  0.0 21.7 %all-to-all-start = ((bf16[8,512,128]{2,1,0:T(8,128)(2,1)}), bf16[8,512,128]{2,1,0:T(8,128)(2,1)S(1)}, u32[]{:S(2)}, u32[]{:S(2)}) async-start(bf16[8,512,128]{2,1,0:T(8,128)(2,1)} %bitcast.10), calls=%async_computation | async-start | bytes 2097152 | tf_op jit(solution)/shard_map/all_to_all | solution.py:138
  5.9 2.3 %copy-start.10 = (bf16[1024,512]{1,0:T(8,128)(2,1)S(1)}, bf16[1024,512]{1,0:T(8,128)(2,1)}, u32[]{:S(2)}) copy-start(bf16[1024,512]{1,0:T(8,128)(2,1)} %param.24) | copy-start | bytes 3145732
  5.9 2.3 %copy-start.11 = (bf16[1024,512]{1,0:T(8,128)(2,1)S(1)}, bf16[1024,512]{1,0:T(8,128)(2,1)}, u32[]{:S(2)}) copy-start(bf16[1024,512]{1,0:T(8,128)(2,1)} %param.23) | copy-start | bytes 3145732
  9.3 47.3 %copy-start.2 = (bf16[512,512]{1,0:T(8,128)(2,1)S(1)}, bf16[512,512]{1,0:T(8,128)(2,1)}, u32[]{:S(2)}) copy-start(bf16[512,512]{1,0:T(8,128)(2,1)} %right.2) | copy-start | bytes 1572868
  9.3 47.3 %copy-start.5 = (f32[8,512]{1,0:T(8,128)S(1)}, f32[8,512]{1,0:T(8,128)}, u32[]{:S(2)}) copy-start(f32[8,512]{1,0:T(8,128)} %tw.2) | copy-start | bytes 49156
  21.7 37.1 %copy-start = (bf16[8,512,128]{2,1,0:T(8,128)(2,1)}, bf16[8,512,128]{2,1,0:T(8,128)(2,1)S(1)}, u32[]{:S(2)}) copy-start(bf16[8,512,128]{2,1,0:T(8,128)(2,1)S(1)} %all-to-all-done.tok) | copy-start | bytes 3145732
  21.7 34.5 %collective-permute-start.1 = (bf16[1536,512]{1,0:T(8,128)(2,1)}, bf16[1536,512]{1,0:T(8,128)(2,1)}, u32[]{:S(2)}, u32[]{:S(2)}) collective-permute-start(bf16[1536,512]{1,0:T(8,128)(2,1)} %pad_maximum_fusion.rest_0_), channel_id=1, source_target_pairs={{0,1},{1,2},{2,3},{3,0},{4,5},{5,6},{6,7},{7,4},{8,11},{9,8},{10,9... | collective-permute-start | bytes 4718600 | tf_op jit(solution)/shard_map/ppermute | solution.py:150
  22.3 54.6 %collective-permute-start.2 = (bf16[1536,512]{1,0:T(8,128)(2,1)}, bf16[1536,512]{1,0:T(8,128)(2,1)}, u32[]{:S(2)}, u32[]{:S(2)}) collective-permute-start(bf16[1536,512]{1,0:T(8,128)(2,1)} %pad_maximum_fusion.rest_0_), channel_id=1, source_target_pairs={{0,3},{1,0},{2,1},{3,2},{4,7},{5,4},{6,5},{7,6},{8,9},{9,10},{10,1... | collective-permute-start | bytes 4718600 | tf_op jit(solution)/shard_map/ppermute | solution.py:150
  23.1 56.9 %collective-permute-start = (bf16[1536,512]{1,0:T(8,128)(2,1)}, bf16[1536,512]{1,0:T(8,128)(2,1)}, u32[]{:S(2)}, u32[]{:S(2)}) collective-permute-start(bf16[1536,512]{1,0:T(8,128)(2,1)} %pad_maximum_fusion.rest_0_), channel_id=1, source_target_pairs={{0,4},{1,5},{2,6},{3,7},{4,128},{5,129},{6,130},{7,131},{8,140},{9... | collective-permute-start | bytes 4718600 | tf_op jit(solution)/shard_map/ppermute | solution.py:150
  56.2 26.0 %collective-permute-start.5 = (bf16[1536,512]{1,0:T(8,128)(2,1)}, bf16[1536,512]{1,0:T(8,128)(2,1)}, u32[]{:S(2)}, u32[]{:S(2)}) collective-permute-start(bf16[1536,512]{1,0:T(8,128)(2,1)} %collective-permute-done.1.rest_3_), channel_id=1, source_target_pairs={{0,1},{1,2},{2,3},{3,0},{4,5},{5,6},{6,7},{7,4},{8,11},{9,8},{10,9... | collective-permute-start | bytes 4718600 | tf_op jit(solution)/shard_map/ppermute | solution.py:150
  58.7 48.2 %copy-start.1 = (bf16[256,16,128]{2,1,0:T(8,128)(2,1)S(1)}, bf16[256,16,128]{2,1,0:T(8,128)(2,1)}, u32[]{:S(2)}) copy-start(bf16[256,16,128]{2,1,0:T(8,128)(2,1)} %kern.1) | copy-start | bytes 3145732
  58.7 48.2 %copy-start.3 = (bf16[256,256]{1,0:T(8,128)(2,1)S(1)}, bf16[256,256]{1,0:T(8,128)(2,1)}, u32[]{:S(2)}) copy-start(bf16[256,256]{1,0:T(8,128)(2,1)} %left_in.1) | copy-start | bytes 393220
  58.7 48.2 %copy-start.4 = (bf16[256,256]{1,0:T(8,128)(2,1)S(1)}, bf16[256,256]{1,0:T(8,128)(2,1)}, u32[]{:S(2)}) copy-start(bf16[256,256]{1,0:T(8,128)(2,1)} %left_out.1) | copy-start | bytes 393220
  58.7 48.2 %copy-start.6 = (f32[128]{0:T(128)S(1)}, f32[128]{0:T(128)}, u32[]{:S(2)}) copy-start(f32[128]{0:T(128)} %param.14) | copy-start | bytes 1540
  58.7 48.2 %all-to-all-start.1 = ((bf16[256,16,128]{2,1,0:T(8,128)(2,1)}), bf16[256,16,128]{2,1,0:T(8,128)(2,1)S(1)}, u32[]{:S(2)}, u32[]{:S(2)}) async-start(bf16[256,16,128]{2,1,0:T(8,128)(2,1)} %bitcast.2), calls=%async_computation.1 | async-start | bytes 2097152 | tf_op jit(solution)/shard_map/all_to_all | solution.py:165
  76.9 40.7 %collective-permute-start.9 = (bf16[1536,512]{1,0:T(8,128)(2,1)}, bf16[1536,512]{1,0:T(8,128)(2,1)}, u32[]{:S(2)}, u32[]{:S(2)}) collective-permute-start(bf16[1536,512]{1,0:T(8,128)(2,1)} %collective-permute-done.2.rest_4_), channel_id=1, source_target_pairs={{0,8},{1,9},{2,10},{3,11},{4,12},{5,13},{6,14},{7,15},{8,0},{9,1},... | collective-permute-start | bytes 4718600 | tf_op jit(solution)/shard_map/ppermute | solution.py:150
  79.2 40.9 %collective-permute-start.4 = (bf16[1536,512]{1,0:T(8,128)(2,1)}, bf16[1536,512]{1,0:T(8,128)(2,1)}, u32[]{:S(2)}, u32[]{:S(2)}) collective-permute-start(bf16[1536,512]{1,0:T(8,128)(2,1)} %collective-permute-done.2.rest_4_), channel_id=1, source_target_pairs={{0,4},{1,5},{2,6},{3,7},{4,128},{5,129},{6,130},{7,131},{8,140},{9... | collective-permute-start | bytes 4718600 | tf_op jit(solution)/shard_map/ppermute | solution.py:150
  80.0 40.1 %collective-permute-start.8 = (bf16[1536,512]{1,0:T(8,128)(2,1)}, bf16[1536,512]{1,0:T(8,128)(2,1)}, u32[]{:S(2)}, u32[]{:S(2)}) collective-permute-start(bf16[1536,512]{1,0:T(8,128)(2,1)} %collective-permute-done.1.rest_3_), channel_id=1, source_target_pairs={{0,8},{1,9},{2,10},{3,11},{4,12},{5,13},{6,14},{7,15},{8,0},{9,1},... | collective-permute-start | bytes 4718600 | tf_op jit(solution)/shard_map/ppermute | solution.py:150
  80.0 50.3 %collective-permute-start.3 = (bf16[1536,512]{1,0:T(8,128)(2,1)}, bf16[1536,512]{1,0:T(8,128)(2,1)}, u32[]{:S(2)}, u32[]{:S(2)}) collective-permute-start(bf16[1536,512]{1,0:T(8,128)(2,1)} %collective-permute-done.1.rest_3_), channel_id=1, source_target_pairs={{0,4},{1,5},{2,6},{3,7},{4,128},{5,129},{6,130},{7,131},{8,140},{9... | collective-permute-start | bytes 4718600 | tf_op jit(solution)/shard_map/ppermute | solution.py:150
  82.2 71.3 %collective-permute-start.6 = (bf16[1536,512]{1,0:T(8,128)(2,1)}, bf16[1536,512]{1,0:T(8,128)(2,1)}, u32[]{:S(2)}, u32[]{:S(2)}) collective-permute-start(bf16[1536,512]{1,0:T(8,128)(2,1)} %collective-permute-done.5.rest_7_), channel_id=1, source_target_pairs={{0,4},{1,5},{2,6},{3,7},{4,128},{5,129},{6,130},{7,131},{8,140},{9... | collective-permute-start | bytes 4718600 | tf_op jit(solution)/shard_map/ppermute | solution.py:150
  110.2 45.5 %copy-start.8 = (bf16[1024,256]{1,0:T(8,128)(2,1)S(1)}, bf16[1024,256]{1,0:T(8,128)(2,1)}, u32[]{:S(2)}) copy-start(bf16[1024,256]{1,0:T(8,128)(2,1)} %get-tuple-element.11) | copy-start | bytes 1572868
  110.2 45.5 %copy-start.9 = (bf16[1024,256]{1,0:T(8,128)(2,1)S(1)}, bf16[1024,256]{1,0:T(8,128)(2,1)}, u32[]{:S(2)}) copy-start(bf16[1024,256]{1,0:T(8,128)(2,1)} %get-tuple-element.18) | copy-start | bytes 1572868
  110.2 45.5 %copy-start.12 = (bf16[256,512]{1,0:T(8,128)(2,1)S(1)}, bf16[256,512]{1,0:T(8,128)(2,1)}, u32[]{:S(2)}) copy-start(bf16[256,512]{1,0:T(8,128)(2,1)} %get-tuple-element.13) | copy-start | bytes 786436
  110.2 45.5 %copy-start.13 = (bf16[256,512]{1,0:T(8,128)(2,1)S(1)}, bf16[256,512]{1,0:T(8,128)(2,1)}, u32[]{:S(2)}) copy-start(bf16[256,512]{1,0:T(8,128)(2,1)} %get-tuple-element.15) | copy-start | bytes 786436
  110.2 46.9 %all-to-all-start.2 = ((bf16[256,16,128]{2,1,0:T(8,128)(2,1)}), bf16[256,16,128]{2,1,0:T(8,128)(2,1)S(1)}, u32[]{:S(2)}, u32[]{:S(2)}) async-start(bf16[256,16,128]{2,1,0:T(8,128)(2,1)} %middle.1), calls=%async_computation.2 | async-start | bytes 2097152 | tf_op jit(solution)/shard_map/all_to_all | solution.py:175
  117.7 39.4 %collective-permute-start.7 = (bf16[1536,512]{1,0:T(8,128)(2,1)}, bf16[1536,512]{1,0:T(8,128)(2,1)}, u32[]{:S(2)}, u32[]{:S(2)}) collective-permute-start(bf16[1536,512]{1,0:T(8,128)(2,1)} %collective-permute-done.rest_2_), channel_id=1, source_target_pairs={{0,8},{1,9},{2,10},{3,11},{4,12},{5,13},{6,14},{7,15},{8,0},{9,1},... | collective-permute-start | bytes 4718600 | tf_op jit(solution)/shard_map/ppermute | solution.py:150
  120.0 37.0 %collective-permute-start.12 = (bf16[1536,512]{1,0:T(8,128)(2,1)}, bf16[1536,512]{1,0:T(8,128)(2,1)}, u32[]{:S(2)}, u32[]{:S(2)}) collective-permute-start(bf16[1536,512]{1,0:T(8,128)(2,1)} %collective-permute-done.5.rest_7_), channel_id=1, source_target_pairs={{0,8},{1,9},{2,10},{3,11},{4,12},{5,13},{6,14},{7,15},{8,0},{9,1},... | collective-permute-start | bytes 4718600 | tf_op jit(solution)/shard_map/ppermute | solution.py:150
  120.1 36.9 %collective-permute-start.11 = (bf16[1536,512]{1,0:T(8,128)(2,1)}, bf16[1536,512]{1,0:T(8,128)(2,1)}, u32[]{:S(2)}, u32[]{:S(2)}) collective-permute-start(bf16[1536,512]{1,0:T(8,128)(2,1)} %collective-permute-done.4.rest_6_), channel_id=1, source_target_pairs={{0,8},{1,9},{2,10},{3,11},{4,12},{5,13},{6,14},{7,15},{8,0},{9,1},... | collective-permute-start | bytes 4718600 | tf_op jit(solution)/shard_map/ppermute | solution.py:150
  130.4 26.7 %collective-permute-start.10 = (bf16[1536,512]{1,0:T(8,128)(2,1)}, bf16[1536,512]{1,0:T(8,128)(2,1)}, u32[]{:S(2)}, u32[]{:S(2)}) collective-permute-start(bf16[1536,512]{1,0:T(8,128)(2,1)} %collective-permute-done.3.rest_5_), channel_id=1, source_target_pairs={{0,8},{1,9},{2,10},{3,11},{4,12},{5,13},{6,14},{7,15},{8,0},{9,1},... | collective-permute-start | bytes 4718600 | tf_op jit(solution)/shard_map/ppermute | solution.py:150
  153.6 5.5 %collective-permute-start.13 = (bf16[1536,512]{1,0:T(8,128)(2,1)}, bf16[1536,512]{1,0:T(8,128)(2,1)}, u32[]{:S(2)}, u32[]{:S(2)}) collective-permute-start(bf16[1536,512]{1,0:T(8,128)(2,1)} %collective-permute-done.6.rest_8_), channel_id=1, source_target_pairs={{0,8},{1,9},{2,10},{3,11},{4,12},{5,13},{6,14},{7,15},{8,0},{9,1},... | collective-permute-start | bytes 4718600 | tf_op jit(solution)/shard_map/ppermute | solution.py:150
  157.1 2.0 %copy-start.7 = (bf16[256,16,128]{2,1,0:T(8,128)(2,1)}, bf16[256,16,128]{2,1,0:T(8,128)(2,1)S(1)}, u32[]{:S(2)}) copy-start(bf16[256,16,128]{2,1,0:T(8,128)(2,1)S(1)} %all-to-all-done.2) | copy-start | bytes 3145732

commit v2 on v1

--- a/solution.py
+++ b/solution.py
@@ -43,6 +43,21 @@
 
 def other_core(yhi, z, core, ylo, x):
     return yhi, z, 1 - core, ylo, x
+
+
+def touch_kernel(count, *rest):
+    rest[count][...] = jnp.zeros_like(rest[count])
+
+
+def touch(arrays, flops):
+    return pl.pallas_call(
+        functools.partial(touch_kernel, len(arrays)),
+        out_shape=jax.ShapeDtypeStruct((8, 128), F32),
+        in_specs=[pl.BlockSpec(memory_space=pl.ANY)] * len(arrays),
+        out_specs=pl.BlockSpec(memory_space=pltpu.VMEM),
+        cost_estimate=pl.CostEstimate(flops=flops, bytes_accessed=1, transcendentals=0),
+        name="touch",
+    )(*arrays)
 
 
 def first_kernel(place, tok, right, tw, out):
@@ -80,41 +95,86 @@
     out[...] = flat[...].reshape(blocks, inner, width).astype(BF)
 
 
-def last_kernel(count, place, back, tok, right, tw, gain, *rest):
-    packs, out = rest[:count], rest[count]
-    weights, acc, normed, sems = rest[count + 1 :]
-    for i in range(count):
-        pltpu.make_async_copy(packs[i], weights.at[i], sems.at[i]).start()
-    groups, rows, width = tok.shape
-    full = groups * width
-    turned = tw[...].T
-    lane = lax.broadcasted_iota(jnp.int32, turned.shape, 1)
-    twiddle = jnp.sum(jnp.where(lane == place[0], turned, 0.0), axis=1, keepdims=True)
-    energy = jnp.zeros((rows, 1), F32)
-    for g in range(0, groups, 2):
-        pair = [back[:, g + k].reshape(rows, width) for k in range(2)]
-        mixed = jnp.dot(right[...], jnp.concatenate(pair, axis=1), preferred_element_type=F32)
-        mixed = mixed * twiddle
-        for k in range(2):
-            at = pl.ds((g + k) * width, width)
-            s = (tok[g + k].astype(F32) + mixed[:, k * width : (k + 1) * width]).astype(BF).astype(F32)
-            acc[:, at] = s
-            energy = energy + jnp.sum(s * s, axis=1, keepdims=True)
-    scale = lax.rsqrt(energy / full + EPS)
-    normed[...] = (acc[...] * scale * gain[...]).astype(BF)
-    hid = weights.shape[2] // 2
-
-    @pl.loop(0, count)
-    def _(i):
-        pltpu.make_async_copy(packs[0], weights.at[i], sems.at[i]).wait()
-        both = jnp.dot(normed[...], weights[i, :full, :], preferred_element_type=F32)
+def mlp_over(packs, weights, sems, first, second, normed, acc, prepare):
+    full = normed.shape[1]
+    hid, half = weights.shape[2] // 2, full // 2
+    count, tall = weights.shape[:2]
+    rows = packs[0].shape[1]
+    per = tall // rows
+    copies = []
+    for pack in packs:
+        for k in range(pack.shape[0]):
+            i = len(copies)
+            place = weights.at[i // per, pl.ds(i % per * rows, rows)]
+            copies.append(pltpu.make_async_copy(pack.at[k], place, sems.at[i]))
+            copies[i].start()
+    prepare()
+
+    def up_to(i, to):
+        for copy in copies[i * per : (i + 1) * per]:
+            copy.wait()
+        to[...] = jnp.dot(normed[...], weights[i, :full, :], preferred_element_type=F32)
+
+    def down_from(i, both):
         gate, up = both[:, :hid], both[:, hid:]
         hidden = (gate * up / (1.0 + jnp.exp(-gate))).astype(BF)
-        half = full // 2
         for k in range(2):
             down = weights[i, full + k * hid : full + (k + 1) * hid, :]
             acc[:, k * half : (k + 1) * half] += jnp.dot(hidden, down, preferred_element_type=F32)
 
+    held = (first, second)
+    up_to(0, first)
+    for i in range(count):
+        if i + 1 < count:
+            up_to(i + 1, held[(i + 1) % 2])
+        down_from(i, held[i % 2])
+
+
+def third_kernel(count, place, back, tok, right_hbm, tw, gain, *rest):
+    packs, (acc, normed, right, sem, weights, sems, one, two) = rest[:count], rest[count:]
+    load = pltpu.make_async_copy(right_hbm, right, sem)
+    load.start()
+
+    def prepare():
+        groups, rows, width = tok.shape
+        turned = tw[...].T
+        lane = lax.broadcasted_iota(jnp.int32, turned.shape, 1)
+        twiddle = jnp.sum(jnp.where(lane == place[0], turned, 0.0), axis=1, keepdims=True)
+        energy = jnp.zeros((rows, 1), F32)
+        load.wait()
+        for g in range(0, groups, 2):
+            pair = [back[:, g + k].reshape(rows, width) for k in range(2)]
+            mixed = jnp.dot(right[...], jnp.concatenate(pair, axis=1), preferred_element_type=F32)
+            mixed = mixed * twiddle
+            for k in range(2):
+                at = pl.ds((g + k) * width, width)
+                s = tok[g + k].astype(F32) + mixed[:, k * width : (k + 1) * width]
+                s = s.astype(BF).astype(F32)
+                acc[:, at] = s
+                energy = energy + jnp.sum(s * s, axis=1, keepdims=True)
+        scale = lax.rsqrt(energy / (groups * width) + EPS)
+        normed[...] = (acc[...] * scale * gain[...]).astype(BF)
+
+    mlp_over(packs, weights, sems, one, two, normed, acc, prepare)
+
+
+def more_kernel(count, before, normed, *rest):
+    packs, (acc, weights, sems, one, two) = rest[:count], rest[count:]
+
+    def prepare():
+        acc[...] = before[...]
+
+    mlp_over(packs, weights, sems, one, two, normed, acc, prepare)
+
+
+def last_kernel(count, before, normed, *rest):
+    packs, (out, acc, weights, sems, one, two) = rest[:count], rest[count:]
+
+    def prepare():
+        acc[...] = before[...]
+
+    mlp_over(packs, weights, sems, one, two, normed, acc, prepare)
+    groups, _, width = out.shape
     for g in range(groups):
         out[g] = acc[:, g * width : (g + 1) * width].astype(BF)
 
@@ -134,62 +194,81 @@
     vmem = pl.BlockSpec(memory_space=pltpu.VMEM)
     smem = pl.BlockSpec(memory_space=pltpu.SMEM)
     any_ = pl.BlockSpec(memory_space=pl.ANY)
+    hbm = pl.BlockSpec(memory_space=pltpu.HBM)
 
     tok = lax.all_to_all(tokens.reshape(n_chan, inner, own), "chan", 0, 0, tiled=True)
 
-    def pack(side):
-        at = side * hid
-        cut = lambda w, axis: lax.dynamic_slice_in_dim(w, at, hid, axis)
-        d = cut(w_down, 0)
-        up = jnp.concatenate([cut(w_gate, 1), cut(w_up, 1)], axis=1)
-        return jnp.concatenate([up, d[:, : full // 2], d[:, full // 2 :]], axis=0)
-
-    mine, other = pack(core), pack(1 - core)
+    halves = []
+    for k in range(2):
+        cut = slice(k * hid, (k + 1) * hid)
+        d = w_down[cut]
+        gate_up = jnp.concatenate([w_gate[:, cut], w_up[:, cut]], axis=1)
+        halves.append(jnp.concatenate([gate_up, d[:, : full // 2], d[:, full // 2 :]], axis=0))
+    mine = jnp.stack(halves)
+    half = lambda w: lax.dynamic_slice_in_dim(w, core, 1, 0)
+    fwd, yy, swap = along_x(1), route(along_y), route(other_core)
+    go = lambda x, pairs: lax.ppermute(x, BOTH, pairs)
     mine, tok = lax.optimization_barrier((mine, tok))
-    fwd, bwd, yy, swap = along_x(1), along_x(-1), route(along_y), route(other_core)
-    go = lambda x, pairs: lax.ppermute(x, BOTH, pairs)
-    a, b, y = go(mine, fwd), go(mine, bwd), go(mine, yy)
-    aa, ya, yb = go(a, fwd), go(a, yy), go(b, yy)
-    yaa = go(aa, yy)
-    got = [y, a, b, ya, yb, aa, yaa]
-    packs = [mine, other] + got + [go(g, swap) for g in got]
+    ab, y = go(mine, fwd), go(half(mine), yy)
 
     f1 = pl.pallas_call(
         first_kernel,
         out_shape=jax.ShapeDtypeStruct((n_seq, n_chan, r_own, own), BF),
         in_specs=[smem] + [vmem] * 3,
         out_specs=vmem,
-        compiler_params=pltpu.CompilerParams(vmem_limit_bytes=32 << 20),
+        compiler_params=pltpu.CompilerParams(vmem_limit_bytes=60 << 20),
+        cost_estimate=pl.CostEstimate(flops=1, bytes_accessed=1, transcendentals=0),
         name="first",
     )(place, tok, right_in, twiddle_in)
     col = lax.all_to_all(f1.reshape(n_seq * n_chan, r_own, own), BOTH, 0, 0, tiled=True)
+    ab, y, col = lax.optimization_barrier((ab, y, col))
+    cut = mine.shape[1] // 2
+    quarter = lambda w, k: lax.dynamic_slice(w, (core, k * cut, 0), (1, cut, w.shape[2]))
+    yab, a0, a1 = go(ab, yy), go(quarter(ab, 0), fwd), go(quarter(ab, 1), fwd)
     f3 = pl.pallas_call(
         middle_kernel,
         out_shape=jax.ShapeDtypeStruct((blocks, r_own, own), BF),
         in_specs=[vmem] * 5,
         out_specs=vmem,
         scratch_shapes=[pltpu.VMEM((blocks * r_own, own), F32)] * 2,
-        compiler_params=pltpu.CompilerParams(vmem_limit_bytes=32 << 20),
+        compiler_params=pltpu.CompilerParams(vmem_limit_bytes=60 << 20),
+        cost_estimate=pl.CostEstimate(flops=1, bytes_accessed=1, transcendentals=0),
         name="middle",
     )(col, left_in, left_out, kernel, gain_in[None])
     back = lax.all_to_all(f3, BOTH, 0, 0, tiled=True).reshape(n_seq, n_chan, r_own, own)
-    count = len(packs)
-
-
-    done = pl.pallas_call(
-        functools.partial(last_kernel, count),
-        out_shape=jax.ShapeDtypeStruct((n_chan, inner, own), BF),
-        in_specs=[smem] + [vmem] * 5 + [any_] * count,
-        out_specs=vmem,
-        scratch_shapes=[
-            pltpu.VMEM((count,) + mine.shape, BF),
-            pltpu.VMEM((inner, full), F32),
-            pltpu.VMEM((inner, full), BF),
-            pltpu.SemaphoreType.DMA((count,)),
-        ],
-        compiler_params=pltpu.CompilerParams(vmem_limit_bytes=56 << 20),
-        name="last",
-    )(place, back, tok, right_out, twiddle_out, gain_mlp[None], *packs)
+    back, mark = lax.optimization_barrier((back, touch([yab, a0, a1], 10**11)))
+    yab, a0, a1, _ = lax.optimization_barrier((yab, a0, a1, mark))
+    ya0, ya1 = go(a0, yy), go(quarter(yab, 1), fwd)
+    both = lambda g: [g, go(g, swap)]
+    shape = (inner, full)
+    rows_f32, rows_bf = jax.ShapeDtypeStruct(shape, F32), jax.ShapeDtypeStruct(shape, BF)
+
+    def mlp(body, name, inputs, specs, packs, outs, scratch):
+        pieces = sum(p.shape[0] for p in packs)
+        count = pieces * packs[0].shape[1] // mine.shape[1]
+        return pl.pallas_call(
+            functools.partial(body, len(packs)),
+            out_shape=outs,
+            in_specs=specs + [any_] * len(packs),
+            out_specs=jax.tree.map(lambda _: vmem, outs),
+            scratch_shapes=scratch
+            + [
+                pltpu.VMEM((count,) + mine.shape[1:], BF),
+                pltpu.SemaphoreType.DMA((pieces,)),
+                pltpu.VMEM((inner, 2 * hid), F32),
+                pltpu.VMEM((inner, 2 * hid), F32),
+            ],
+            compiler_params=pltpu.CompilerParams(vmem_limit_bytes=32 << 20),
+            cost_estimate=pl.CostEstimate(flops=10**11, bytes_accessed=1, transcendentals=0),
+            name=name,
+        )(*inputs, *packs)
+
+    start = [place, back, tok, right_out, twiddle_out, gain_mlp[None]]
+    extra = [pltpu.VMEM(right_out.shape, BF), pltpu.SemaphoreType.DMA]
+    acc, normed = mlp(third_kernel, "third", start, [smem, vmem, vmem, hbm, vmem, vmem], [mine] + both(ab) + both(y), (rows_f32, rows_bf), extra)
+    acc = mlp(more_kernel, "more", [acc, normed], [vmem] * 2, both(yab), rows_f32, [])
+    done = jax.ShapeDtypeStruct((n_chan, inner, own), BF)
+    done = mlp(last_kernel, "last", [acc, normed], [vmem] * 2, [a0, a1, go(a0, swap), go(a1, swap), ya0, ya1, go(ya0, swap), go(ya1, swap)], done, [pltpu.VMEM(shape, F32)])
     out = lax.all_to_all(done, "chan", 0, 0, tiled=True)
     return out.reshape(tokens.shape)
 

time: 200 us -> 176 us (0.88)
  waiting for transfers between devices: 101 us -> 65.3 us
  Pallas kernels: 25.6 us -> 30.4 us
  local copies, waits for them, and re-layouts: 4.4 us -> 7.55 us
  other arithmetic: 2.64 us -> 4.78 us
    ppermute x14, waiting for transfers between devices: 64.8 us -> 28.1 us  [local(): go = lambda x, pairs: lax.ppermute(x, BOTH, pairs)]
    all_to_all x1, waiting for transfers between devices: 0.01 us -> 25.5 us  [local(): lax.all_to_all(f3, BOTH, 0, 0, tiled=True)]
    all_to_all x1, waiting for transfers between devices: 24.6 us -> 2.32 us  [local(): lax.all_to_all(f1.reshape(n_seq * n_chan, r_own, own), BOTH, 0, 0, tiled=...]
    all_to_all x1, starting transfers between devices: 7.43 us -> 12.8 us  [local(): lax.all_to_all(f3, BOTH, 0, 0, tiled=True)]
    another operation x0 -> x2, other arithmetic: none -> 4.78 us  [local(): mine = jnp.stack(halves)]
    dynamic_slice x1 -> x3, local copies, waits for them, and re-layouts: 1.13 us -> 3.93 us  [the longest x2 3.82 us: local(): lax.dynamic_slice(w, (core, k * cut, 0), (1, cut, w.shape[2]))]
    concatenate x2 -> x0, other arithmetic: 2.64 us -> none  [pack(): return jnp.concatenate([up, d[:, :full // 2], d[:, full // 2:]], axis=0)]
    all_to_all x1, starting transfers between devices: 18.2 us -> 15.9 us  [local(): lax.all_to_all(f1.reshape(n_seq * n_chan, r_own, own), BOTH, 0, 0, tiled=...]
  transfers between devices with their start and end apart: 17 -> 17, of which waited for: 6 -> 5; matrix products, arithmetic and copies ran while one was open for 3% -> 6% of each run, Pallas kernels for 3% -> 14%
where the time goes in v2:
time: 176 us
  waiting for transfers between devices  65.3 us (37%)
  starting transfers between devices  48.2 us (27%)
  Pallas kernels  30.4 us (17%)
  blocking collectives  19 us (11%)
  local copies, waits for them, and re-layouts  7.55 us (4%)
  other arithmetic  4.78 us (3%)
    ppermute x14, waiting for transfers between devices, local(): go = lambda x, pairs: lax.ppermute(x, BOTH, pairs)  28.1 us
    all_to_all x1, waiting for transfers between devices, local(): lax.all_to_all(f3, BOTH, 0, 0, tiled=True)  25.5 us
    pallas_call x3, Pallas kernels, mlp(): pl.pallas_call(functools.partial(body, len(packs)), out_shape=outs, in_sp...  22.1 us
    all_to_all x1, blocking collectives, local(): out = lax.all_to_all(done, 'chan', 0, 0, tiled=True)  19 us
    all_to_all x1, starting transfers between devices, local(): lax.all_to_all(f1.reshape(n_seq * n_chan, r_own, own), BOTH, 0, 0, tiled=...  15.9 us
    ppermute x14, starting transfers between devices, local(): go = lambda x, pairs: lax.ppermute(x, BOTH, pairs)  13.5 us
    all_to_all x1, starting transfers between devices, local(): lax.all_to_all(f3, BOTH, 0, 0, tiled=True)  12.8 us
    all_to_all x1, waiting for transfers between devices, local(): lax.all_to_all(tokens.reshape(n_chan, inner, own), 'chan', 0, 0, tiled=True)  9.47 us
  transfers between devices with their start and end apart: 17, of which 5 were waited for; matrix products, arithmetic and copies ran while one was open for 6% of the time, Pallas kernels for 14%

profile of v2, /device:TPU:1, one launch (start us, length us, event | category | flops | bytes accessed | tf_op | source)
XLA Modules:
  0.0 175.5 jit_solution(5587918120526832089)
XLA Ops:
  0.0 0.0 copy-start.3
  0.0 6.0 %all-to-all-start = ((bf16[8,512,128]{2,1,0:T(8,128)(2,1)}), bf16[8,512,128]{2,1,0:T(8,128)(2,1)}, u32[]{:S(2)}, u32[]{:S(2)}) async-start(bf16[8,512,128]{2,1,0:T(8,128)(2,1)} %bitcast.14), calls=%async_computation | async-start | bytes 2097152 | tf_op jit(solution)/shard_map/all_to_all | solution.py:199
  6.0 0.0 copy-start.4
  6.0 1.4 fusion.1
  7.4 0.0 copy-done.3
  7.4 0.1 fusion
  7.5 0.1 copy-done.4
  7.5 0.1 fusion.2
  7.6 4.5 %maximum_bitcast_fusion = (bf16[1,1536,512]{2,1,0:T(8,128)(2,1)S(1)}, bf16[1,1536,512]{2,1,0:T(8,128)(2,1)S(1)}) fusion(bf16[256,512]{1,0:T(8,128)(2,1)S(1)} %get-tuple-element.32, bf16[256,512]{1,0:T(8,128)(2,1)S(1)} %get-tuple-element.31, bf16[1024,256]{1,0:T(8,128)(2,1)S(1)} %get-tuple-element.29, bf16[1024,256]{1,0:T(8,128)(2,1)S(1)} %get-tuple-element.27, ...), kind=kLoop, calls=%fused_computation.1 | loop fusion | flops 12582912 | bytes 6291456 | tf_op jit(solution)/shard_map/stack | solution.py:207
  12.1 0.3 pad_maximum_fusion.rest_0_
  12.4 9.5 %all-to-all-done.tok = bf16[8,512,128]{2,1,0:T(8,128)(2,1)} async-done(((bf16[8,512,128]{2,1,0:T(8,128)(2,1)}), bf16[8,512,128]{2,1,0:T(8,128)(2,1)}, u32[]{:S(2)}, u32[]{:S(2)}) %all-to-all-start) | async-done | bytes 1048608 | tf_op jit(solution)/shard_map/all_to_all | solution.py:199
  21.9 0.0 collective-permute-start
  21.9 3.6 %first.1 = bf16[32,8,16,128]{3,2,1,0:T(8,128)(2,1)} custom-call(s32[1]{0:T(128)} %bitcast.place, bf16[8,512,128]{2,1,0:T(8,128)(2,1)} %all-to-all-done.tok, bf16[512,512]{1,0:T(8,128)(2,1)} %right.1, f32[8,512]{1,0:T(8,128)} %tw.2), custom_call_target="tpu_custom_call" | custom-call | flops 1 | bytes 1 | tf_op jit(solution)/shard_map/first/pallas_call | solution.py:214
  25.5 15.9 %all-to-all-start.1 = ((bf16[256,16,128]{2,1,0:T(8,128)(2,1)}), bf16[256,16,128]{2,1,0:T(8,128)(2,1)}, u32[]{:S(2)}, u32[]{:S(2)}) async-start(bf16[256,16,128]{2,1,0:T(8,128)(2,1)} %bitcast.12), calls=%async_computation.1 | async-start | bytes 2097152 | tf_op jit(solution)/shard_map/all_to_all | solution.py:223
  41.4 0.1 constant_dynamic-slice_fusion.3
  41.5 2.7 %collective-permute-start.1 = (bf16[1,1536,512]{2,1,0:T(8,128)(2,1)S(1)}, bf16[1,1536,512]{2,1,0:T(8,128)(2,1)}, u32[]{:S(2)}, u32[]{:S(2)}) collective-permute-start(bf16[1,1536,512]{2,1,0:T(8,128)(2,1)S(1)} %constant_dynamic-slice_fusion.3), channel_id=1, source_target_pairs={{0,4},{1,5},{2,6},{3,7},{4,128},{5,129},{6,130},{7,131},{8,140},{9... | collective-permute-start | bytes 4718600 | tf_op jit(solution)/shard_map/ppermute | solution.py:210
  44.3 27.5 %collective-permute-done.1.rest_3_ = bf16[1,1536,512]{2,1,0:T(8,128)(2,1)} collective-permute-done((bf16[1,1536,512]{2,1,0:T(8,128)(2,1)S(1)}, bf16[1,1536,512]{2,1,0:T(8,128)(2,1)}, u32[]{:S(2)}, u32[]{:S(2)}) %collective-permute-start.1) | collective-permute-done | bytes 1572896 | tf_op jit(solution)/shard_map/ppermute | solution.py:210
  71.7 2.3 %all-to-all-done.1.col = bf16[256,16,128]{2,1,0:T(8,128)(2,1)} async-done(((bf16[256,16,128]{2,1,0:T(8,128)(2,1)}), bf16[256,16,128]{2,1,0:T(8,128)(2,1)}, u32[]{:S(2)}, u32[]{:S(2)}) %all-to-all-start.1) | async-done | bytes 1048608 | tf_op jit(solution)/shard_map/all_to_all | solution.py:223
  74.1 0.0 collective-permute-done.rest_1_
  74.1 0.7 collective-permute-start.4
  74.8 0.5 collective-permute-start.2
  75.3 4.8 %middle.1 = bf16[256,16,128]{2,1,0:T(8,128)(2,1)} custom-call(bf16[256,16,128]{2,1,0:T(8,128)(2,1)} %all-to-all-done.1.col, bf16[256,256]{1,0:T(8,128)(2,1)} %left_in.1, bf16[256,256]{1,0:T(8,128)(2,1)} %left_out.1, bf16[256,16,128]{2,1,0:T(8,128)(2,1)} %kern.1, f32[1,128]{1,0:T(1,128)} %bitcast.15), custom_call_target="tpu_custom_call" | custom-call | flops 1 | bytes 1 | tf_op jit(solution)/shard_map/middle/pallas_call | solution.py:228
  80.1 0.0 copy-start.1
  80.1 0.0 copy-start.2
  80.1 12.8 %all-to-all-start.2 = ((bf16[256,16,128]{2,1,0:T(8,128)(2,1)}), bf16[256,16,128]{2,1,0:T(8,128)(2,1)}, u32[]{:S(2)}, u32[]{:S(2)}) async-start(bf16[256,16,128]{2,1,0:T(8,128)(2,1)} %middle.1), calls=%async_computation.2 | async-start | bytes 2097152 | tf_op jit(solution)/shard_map/all_to_all | solution.py:238
  92.9 2.5 %collective-permute-start.3 = (bf16[1,1536,512]{2,1,0:T(8,128)(2,1)}, bf16[1,1536,512]{2,1,0:T(8,128)(2,1)}, u32[]{:S(2)}, u32[]{:S(2)}) collective-permute-start(bf16[1,1536,512]{2,1,0:T(8,128)(2,1)} %collective-permute-done.1.rest_3_), channel_id=1, source_target_pairs={{0,8},{1,9},{2,10},{3,11},{4,12},{5,13},{6,14},{7,15},{8,0},{9,1},... | collective-permute-start | bytes 4718600 | tf_op jit(solution)/shard_map/ppermute | solution.py:210
  95.4 2.6 %constant_dynamic-slice_fusion.1 = (bf16[1,768,512]{2,1,0:T(8,128)(2,1)}, bf16[1,768,512]{2,1,0:T(8,128)(2,1)}) fusion(bf16[2,1536,512]{2,1,0:T(8,128)(2,1)} %collective-permute-done.rest_1_, s32[]{:T(128)S(6)} %select_n.14), kind=kLoop, calls=%fused_computation.4 | loop fusion | bytes 3145732 | tf_op jit(solution)/shard_map/dynamic_slice | solution.py:226
  98.0 0.7 collective-permute-start.5
  98.8 0.6 collective-permute-start.6
  99.3 25.5 %all-to-all-done.2 = bf16[256,16,128]{2,1,0:T(8,128)(2,1)} async-done(((bf16[256,16,128]{2,1,0:T(8,128)(2,1)}), bf16[256,16,128]{2,1,0:T(8,128)(2,1)}, u32[]{:S(2)}, u32[]{:S(2)}) %all-to-all-start.2) | async-done | bytes 1048608 | tf_op jit(solution)/shard_map/all_to_all | solution.py:238
  124.8 0.0 collective-permute-done.5.rest_0_
  124.8 0.6 collective-permute-done.6.rest_1_
  125.4 0.0 collective-permute-done.4.rest_0_
  125.4 2.1 %collective-permute-start.8 = (bf16[1,768,512]{2,1,0:T(8,128)(2,1)}, bf16[1,768,512]{2,1,0:T(8,128)(2,1)}, u32[]{:S(2)}, u32[]{:S(2)}) collective-permute-start(bf16[1,768,512]{2,1,0:T(8,128)(2,1)} %collective-permute-done.5.rest_0_), channel_id=1, source_target_pairs={{0,8},{1,9},{2,10},{3,11},{4,12},{5,13},{6,14},{7,15},{8,0},{9,1},... | collective-permute-start | bytes 2359304 | tf_op jit(solution)/shard_map/ppermute | solution.py:210
  127.5 1.7 collective-permute-start.10
  129.1 0.0 collective-permute-start.7
  129.1 1.2 constant_dynamic-slice_fusion
  130.3 0.0 collective-permute-done.3.rest_4_
  130.3 0.6 collective-permute-start.9
  130.9 0.0 collective-permute-done.2.rest_2_
  130.9 0.8 collective-permute-start.11
  131.7 0.0 copy-done.1
  131.7 0.0 copy-done.2
  131.7 0.0 copy-start
  131.7 1.0 copy-done
  132.8 11.2 %third.1 = (f32[512,1024]{1,0:T(8,128)S(1)}, bf16[512,1024]{1,0:T(8,128)(2,1)S(1)}) custom-call(s32[1]{0:T(128)} %bitcast.place, bf16[32,8,16,128]{3,2,1,0:T(8,128)(2,1)} %bitcast.6.back, bf16[8,512,128]{2,1,0:T(8,128)(2,1)} %all-to-all-done.tok, bf16[512,512]{1,0:T(8,128)(2,1)S(1)} %copy-done, f32[8,512]{1,0:T(8,128)S(1)} %copy-done.1, ...), custom_call_target="tpu_custom_call" | custom-call | flops 99999997952 | bytes 1 | tf_op jit(solution)/shard_map/third/pallas_call | solution.py:249
  143.9 0.0 collective-permute-done.10.rest_4_
  143.9 0.1 collective-permute-start.12
  144.0 0.0 collective-permute-done.11.rest_5_
  144.0 0.5 collective-permute-start.13
  144.5 0.0 collective-permute-done.7.rest_1_
  144.5 5.5 %more.1.before = f32[512,1024]{1,0:T(8,128)S(1)} custom-call(f32[512,1024]{1,0:T(8,128)S(1)} %get-tuple-element.20.before, bf16[512,1024]{1,0:T(8,128)(2,1)S(1)} %get-tuple-element.21.normed, bf16[2,1536,512]{2,1,0:T(8,128)(2,1)} %collective-permute-done.4.rest_0_, bf16[2,1536,512]{2,1,0:T(8,128)(2,1)S(1)} %collective-permute-done.7.rest_1_), custom_call_target="tpu_custom_call" | custom-call | flops 99999997952 | bytes 1 | tf_op jit(solution)/shard_map/more/pallas_call | solution.py:249
  150.0 0.0 collective-permute-done.8.rest_2_
  150.0 0.0 collective-permute-done.9.rest_3_
  150.0 0.0 collective-permute-done.12.rest_6_
  150.1 0.0 collective-permute-done.13.rest_7_
  150.1 5.5 %last.1 = bf16[8,512,128]{2,1,0:T(8,128)(2,1)S(1)} custom-call(f32[512,1024]{1,0:T(8,128)S(1)} %more.1.before, bf16[512,1024]{1,0:T(8,128)(2,1)S(1)} %get-tuple-element.21.normed, bf16[1,768,512]{2,1,0:T(8,128)(2,1)} %collective-permute-done.5.rest_0_, bf16[1,768,512]{2,1,0:T(8,128)(2,1)} %collective-permute-done.6.rest_1_, ...), custom_call_target="tpu_custom_call" | custom-call | flops 99999997952 | bytes 1 | tf_op jit(solution)/shard_map/last/pallas_call | solution.py:249
  155.5 19.0 %all_to_all.20 = bf16[8,512,128]{2,1,0:T(8,128)(2,1)S(1)} all-to-all(bf16[8,512,128]{2,1,0:T(8,128)(2,1)S(1)} %last.1), channel_id=1, replica_groups=mesh['seq'=32,'chan'=8] {'chan'}, dimensions={0} | all-to-all | bytes 2097152 | tf_op jit(solution)/shard_map/all_to_all | solution.py:272
  174.5 1.0 copy.15
Async XLA Ops:
  0.0 7.4 %copy-start.3 = (bf16[1024,512]{1,0:T(8,128)(2,1)S(1)}, bf16[1024,512]{1,0:T(8,128)(2,1)}, u32[]{:S(2)}) copy-start(bf16[1024,512]{1,0:T(8,128)(2,1)} %param.23) | copy-start | bytes 3145732
  0.0 21.9 %all-to-all-start = ((bf16[8,512,128]{2,1,0:T(8,128)(2,1)}), bf16[8,512,128]{2,1,0:T(8,128)(2,1)}, u32[]{:S(2)}, u32[]{:S(2)}) async-start(bf16[8,512,128]{2,1,0:T(8,128)(2,1)} %bitcast.14), calls=%async_computation | async-start | bytes 2097152 | tf_op jit(solution)/shard_map/all_to_all | solution.py:199
  6.0 1.5 copy-start.4
  21.9 52.2 %collective-permute-start = (bf16[2,1536,512]{2,1,0:T(8,128)(2,1)S(1)}, bf16[2,1536,512]{2,1,0:T(8,128)(2,1)}, u32[]{:S(2)}, u32[]{:S(2)}) collective-permute-start(bf16[2,1536,512]{2,1,0:T(8,128)(2,1)S(1)} %pad_maximum_fusion.rest_0_), channel_id=1, source_target_pairs={{0,1},{1,2},{2,3},{3,0},{4,5},{5,6},{6,7},{7,4},{8,11},{9,8},{10,9... | collective-permute-start | bytes 9437192 | tf_op jit(solution)/shard_map/ppermute | solution.py:210
  25.5 48.6 %all-to-all-start.1 = ((bf16[256,16,128]{2,1,0:T(8,128)(2,1)}), bf16[256,16,128]{2,1,0:T(8,128)(2,1)}, u32[]{:S(2)}, u32[]{:S(2)}) async-start(bf16[256,16,128]{2,1,0:T(8,128)(2,1)} %bitcast.12), calls=%async_computation.1 | async-start | bytes 2097152 | tf_op jit(solution)/shard_map/all_to_all | solution.py:223
  41.5 30.2 %collective-permute-start.1 = (bf16[1,1536,512]{2,1,0:T(8,128)(2,1)S(1)}, bf16[1,1536,512]{2,1,0:T(8,128)(2,1)}, u32[]{:S(2)}, u32[]{:S(2)}) collective-permute-start(bf16[1,1536,512]{2,1,0:T(8,128)(2,1)S(1)} %constant_dynamic-slice_fusion.3), channel_id=1, source_target_pairs={{0,4},{1,5},{2,6},{3,7},{4,128},{5,129},{6,130},{7,131},{8,140},{9... | collective-permute-start | bytes 4718600 | tf_op jit(solution)/shard_map/ppermute | solution.py:210
  74.1 51.3 %collective-permute-start.4 = (bf16[2,1536,512]{2,1,0:T(8,128)(2,1)}, bf16[2,1536,512]{2,1,0:T(8,128)(2,1)}, u32[]{:S(2)}, u32[]{:S(2)}) collective-permute-start(bf16[2,1536,512]{2,1,0:T(8,128)(2,1)} %collective-permute-done.rest_1_), channel_id=1, source_target_pairs={{0,4},{1,5},{2,6},{3,7},{4,128},{5,129},{6,130},{7,131},{8,140},{9... | collective-permute-start | bytes 9437192 | tf_op jit(solution)/shard_map/ppermute | solution.py:210
  74.8 56.1 %collective-permute-start.2 = (bf16[2,1536,512]{2,1,0:T(8,128)(2,1)}, bf16[2,1536,512]{2,1,0:T(8,128)(2,1)}, u32[]{:S(2)}, u32[]{:S(2)}) collective-permute-start(bf16[2,1536,512]{2,1,0:T(8,128)(2,1)} %collective-permute-done.rest_1_), channel_id=1, source_target_pairs={{0,8},{1,9},{2,10},{3,11},{4,12},{5,13},{6,14},{7,15},{8,0},{9,1},... | collective-permute-start | bytes 9437192 | tf_op jit(solution)/shard_map/ppermute | solution.py:210
  80.1 51.6 %copy-start.1 = (f32[8,512]{1,0:T(8,128)S(1)}, f32[8,512]{1,0:T(8,128)}, u32[]{:S(2)}) copy-start(f32[8,512]{1,0:T(8,128)} %tw.3) | copy-start | bytes 49156
  80.1 51.6 %copy-start.2 = (f32[1024]{0:T(1024)S(1)}, f32[1024]{0:T(1024)}, u32[]{:S(2)}) copy-start(f32[1024]{0:T(1024)} %param.22) | copy-start | bytes 12292
  80.1 44.7 %all-to-all-start.2 = ((bf16[256,16,128]{2,1,0:T(8,128)(2,1)}), bf16[256,16,128]{2,1,0:T(8,128)(2,1)}, u32[]{:S(2)}, u32[]{:S(2)}) async-start(bf16[256,16,128]{2,1,0:T(8,128)(2,1)} %middle.1), calls=%async_computation.2 | async-start | bytes 2097152 | tf_op jit(solution)/shard_map/all_to_all | solution.py:238
  92.9 37.4 %collective-permute-start.3 = (bf16[1,1536,512]{2,1,0:T(8,128)(2,1)}, bf16[1,1536,512]{2,1,0:T(8,128)(2,1)}, u32[]{:S(2)}, u32[]{:S(2)}) collective-permute-start(bf16[1,1536,512]{2,1,0:T(8,128)(2,1)} %collective-permute-done.1.rest_3_), channel_id=1, source_target_pairs={{0,8},{1,9},{2,10},{3,11},{4,12},{5,13},{6,14},{7,15},{8,0},{9,1},... | collective-permute-start | bytes 4718600 | tf_op jit(solution)/shard_map/ppermute | solution.py:210
  98.0 26.8 %collective-permute-start.5 = (bf16[1,768,512]{2,1,0:T(8,128)(2,1)}, bf16[1,768,512]{2,1,0:T(8,128)(2,1)}, u32[]{:S(2)}, u32[]{:S(2)}) collective-permute-start(bf16[1,768,512]{2,1,0:T(8,128)(2,1)} %get-tuple-element.26), channel_id=1, source_target_pairs={{0,1},{1,2},{2,3},{3,0},{4,5},{5,6},{6,7},{7,4},{8,11},{9,8},{10,9... | collective-permute-start | bytes 2359304 | tf_op jit(solution)/shard_map/ppermute | solution.py:210
  98.8 26.6 %collective-permute-start.6 = (bf16[1,768,512]{2,1,0:T(8,128)(2,1)}, bf16[1,768,512]{2,1,0:T(8,128)(2,1)}, u32[]{:S(2)}, u32[]{:S(2)}) collective-permute-start(bf16[1,768,512]{2,1,0:T(8,128)(2,1)} %get-tuple-element.25), channel_id=1, source_target_pairs={{0,1},{1,2},{2,3},{3,0},{4,5},{5,6},{6,7},{7,4},{8,11},{9,8},{10,9... | collective-permute-start | bytes 2359304 | tf_op jit(solution)/shard_map/ppermute | solution.py:210
  125.4 24.7 %collective-permute-start.8 = (bf16[1,768,512]{2,1,0:T(8,128)(2,1)}, bf16[1,768,512]{2,1,0:T(8,128)(2,1)}, u32[]{:S(2)}, u32[]{:S(2)}) collective-permute-start(bf16[1,768,512]{2,1,0:T(8,128)(2,1)} %collective-permute-done.5.rest_0_), channel_id=1, source_target_pairs={{0,8},{1,9},{2,10},{3,11},{4,12},{5,13},{6,14},{7,15},{8,0},{9,1},... | collective-permute-start | bytes 2359304 | tf_op jit(solution)/shard_map/ppermute | solution.py:210
  127.5 16.5 %collective-permute-start.10 = (bf16[1,768,512]{2,1,0:T(8,128)(2,1)}, bf16[1,768,512]{2,1,0:T(8,128)(2,1)S(1)}, u32[]{:S(2)}, u32[]{:S(2)}) collective-permute-start(bf16[1,768,512]{2,1,0:T(8,128)(2,1)} %collective-permute-done.5.rest_0_), channel_id=1, source_target_pairs={{0,4},{1,5},{2,6},{3,7},{4,128},{5,129},{6,130},{7,131},{8,140},{9... | collective-permute-start | bytes 2359304 | tf_op jit(solution)/shard_map/ppermute | solution.py:210
  129.1 15.4 %collective-permute-start.7 = (bf16[2,1536,512]{2,1,0:T(8,128)(2,1)}, bf16[2,1536,512]{2,1,0:T(8,128)(2,1)S(1)}, u32[]{:S(2)}, u32[]{:S(2)}) collective-permute-start(bf16[2,1536,512]{2,1,0:T(8,128)(2,1)} %collective-permute-done.4.rest_0_), channel_id=1, source_target_pairs={{0,8},{1,9},{2,10},{3,11},{4,12},{5,13},{6,14},{7,15},{8,0},{9,1},... | collective-permute-start | bytes 9437192 | tf_op jit(solution)/shard_map/ppermute | solution.py:210
  130.3 19.7 %collective-permute-start.9 = (bf16[1,768,512]{2,1,0:T(8,128)(2,1)}, bf16[1,768,512]{2,1,0:T(8,128)(2,1)}, u32[]{:S(2)}, u32[]{:S(2)}) collective-permute-start(bf16[1,768,512]{2,1,0:T(8,128)(2,1)} %collective-permute-done.6.rest_1_), channel_id=1, source_target_pairs={{0,8},{1,9},{2,10},{3,11},{4,12},{5,13},{6,14},{7,15},{8,0},{9,1},... | collective-permute-start | bytes 2359304 | tf_op jit(solution)/shard_map/ppermute | solution.py:210
  130.9 13.1 %collective-permute-start.11 = (bf16[1,768,512]{2,1,0:T(8,128)(2,1)S(1)}, bf16[1,768,512]{2,1,0:T(8,128)(2,1)S(1)}, u32[]{:S(2)}, u32[]{:S(2)}) collective-permute-start(bf16[1,768,512]{2,1,0:T(8,128)(2,1)S(1)} %constant_dynamic-slice_fusion), channel_id=1, source_target_pairs={{0,1},{1,2},{2,3},{3,0},{4,5},{5,6},{6,7},{7,4},{8,11},{9,8},{10,9... | collective-permute-start | bytes 2359304 | tf_op jit(solution)/shard_map/ppermute | solution.py:210
  131.7 1.0 copy-start
  143.9 6.1 %collective-permute-start.12 = (bf16[1,768,512]{2,1,0:T(8,128)(2,1)S(1)}, bf16[1,768,512]{2,1,0:T(8,128)(2,1)S(1)}, u32[]{:S(2)}, u32[]{:S(2)}) collective-permute-start(bf16[1,768,512]{2,1,0:T(8,128)(2,1)S(1)} %collective-permute-done.10.rest_4_), channel_id=1, source_target_pairs={{0,8},{1,9},{2,10},{3,11},{4,12},{5,13},{6,14},{7,15},{8,0},{9,1},... | collective-permute-start | bytes 2359304 | tf_op jit(solution)/shard_map/ppermute | solution.py:210
  144.0 6.0 %collective-permute-start.13 = (bf16[1,768,512]{2,1,0:T(8,128)(2,1)S(1)}, bf16[1,768,512]{2,1,0:T(8,128)(2,1)S(1)}, u32[]{:S(2)}, u32[]{:S(2)}) collective-permute-start(bf16[1,768,512]{2,1,0:T(8,128)(2,1)S(1)} %collective-permute-done.11.rest_5_), channel_id=1, source_target_pairs={{0,8},{1,9},{2,10},{3,11},{4,12},{5,13},{6,14},{7,15},{8,0},{9,1},... | collective-permute-start | bytes 2359304 | tf_op jit(solution)/shard_map/ppermute | solution.py:210

commit v3 on v1

--- a/solution.py
+++ b/solution.py
@@ -80,43 +80,86 @@
     out[...] = flat[...].reshape(blocks, inner, width).astype(BF)
 
 
-def last_kernel(count, place, back, tok, right, tw, gain, *rest):
-    packs, out = rest[:count], rest[count]
-    weights, acc, normed, sems = rest[count + 1 :]
+def mlp_over(packs, weights, sems, first, second, normed, acc, prepare):
+    full = normed.shape[1]
+    hid, half = weights.shape[2] // 2, full // 2
+    count = weights.shape[0]
+    slots = [[] for _ in range(count)]
+    at = 0
+    tall = weights.shape[1]
+    for pack, (done, stop) in packs:
+        while done < stop:
+            i, row = at // tall, at % tall
+            rows = min(stop - done, tall - row)
+            sem = sems.at[sum(map(len, slots))]
+            piece = pack.at[0, pl.ds(done, rows)]
+            slots[i].append(pltpu.make_async_copy(piece, weights.at[i, pl.ds(row, rows)], sem))
+            slots[i][-1].start()
+            at, done = at + rows, done + rows
+    prepare()
+
+    def up_to(i, to):
+        for copy in slots[i]:
+            copy.wait()
+        to[...] = jnp.dot(normed[...], weights[i, :full, :], preferred_element_type=F32)
+
+    def down_from(i, both):
+        gate, up = both[:, :hid], both[:, hid:]
+        hidden = (gate * up / (1.0 + jnp.exp(-gate))).astype(BF)
+        for k in range(2):
+            down = weights[i, full + k * hid : full + (k + 1) * hid, :]
+            acc[:, k * half : (k + 1) * half] += jnp.dot(hidden, down, preferred_element_type=F32)
+
+    held = (first, second)
+    up_to(0, first)
     for i in range(count):
-        pltpu.make_async_copy(packs[i], weights.at[i], sems.at[i]).start()
+        if i + 1 < count:
+            up_to(i + 1, held[(i + 1) % 2])
+        down_from(i, held[i % 2])
+
+
+def third_kernel(place, back, tok, right_hbm, tw, gain, stream, normed, acc, right, sem):
+    load = pltpu.make_async_copy(right_hbm, right, sem)
+    load.start()
     groups, rows, width = tok.shape
-    full = groups * width
     turned = tw[...].T
     lane = lax.broadcasted_iota(jnp.int32, turned.shape, 1)
     twiddle = jnp.sum(jnp.where(lane == place[0], turned, 0.0), axis=1, keepdims=True)
     energy = jnp.zeros((rows, 1), F32)
+    load.wait()
     for g in range(0, groups, 2):
         pair = [back[:, g + k].reshape(rows, width) for k in range(2)]
         mixed = jnp.dot(right[...], jnp.concatenate(pair, axis=1), preferred_element_type=F32)
         mixed = mixed * twiddle
         for k in range(2):
             at = pl.ds((g + k) * width, width)
-            s = (tok[g + k].astype(F32) + mixed[:, k * width : (k + 1) * width]).astype(BF).astype(F32)
+            s = tok[g + k].astype(F32) + mixed[:, k * width : (k + 1) * width]
+            stream[:, at] = s.astype(BF)
+            s = s.astype(BF).astype(F32)
             acc[:, at] = s
             energy = energy + jnp.sum(s * s, axis=1, keepdims=True)
-    scale = lax.rsqrt(energy / full + EPS)
+    scale = lax.rsqrt(energy / (groups * width) + EPS)
     normed[...] = (acc[...] * scale * gain[...]).astype(BF)
-    hid = weights.shape[2] // 2
-
-    @pl.loop(0, count)
-    def _(i):
-        pltpu.make_async_copy(packs[0], weights.at[i], sems.at[i]).wait()
-        both = jnp.dot(normed[...], weights[i, :full, :], preferred_element_type=F32)
-        gate, up = both[:, :hid], both[:, hid:]
-        hidden = (gate * up / (1.0 + jnp.exp(-gate))).astype(BF)
-        half = full // 2
-        for k in range(2):
-            down = weights[i, full + k * hid : full + (k + 1) * hid, :]
-            acc[:, k * half : (k + 1) * half] += jnp.dot(hidden, down, preferred_element_type=F32)
-
+
+
+def mlp_kernel(spans, begun, normed, before, *rest):
+    packs, (out, *spare, weights, sems, one, two) = rest[: len(spans)], rest[len(spans) :]
+    packs = list(zip(packs, spans))
+    acc = spare[0] if spare else out
+
+    def prepare():
+        acc[...] = before[...].astype(F32) if begun else jnp.zeros_like(acc)
+
+    mlp_over(packs, weights, sems, one, two, normed, acc, prepare)
+    if spare:
+        out[...] = acc[...].astype(out.dtype)
+
+
+def sum_kernel(a, b, out):
+    groups, _, width = out.shape
     for g in range(groups):
-        out[g] = acc[:, g * width : (g + 1) * width].astype(BF)
+        at = slice(g * width, (g + 1) * width)
+        out[g] = (a[:, at].astype(F32) + b[:, at].astype(F32)).astype(BF)
 
 
 def local(tokens, gain_in, right_in, twiddle_in, left_in, kernel, left_out, right_out, twiddle_out, gain_mlp, w_gate, w_up, w_down):
@@ -134,62 +177,102 @@
     vmem = pl.BlockSpec(memory_space=pltpu.VMEM)
     smem = pl.BlockSpec(memory_space=pltpu.SMEM)
     any_ = pl.BlockSpec(memory_space=pl.ANY)
+    hbm = pl.BlockSpec(memory_space=pltpu.HBM)
 
     tok = lax.all_to_all(tokens.reshape(n_chan, inner, own), "chan", 0, 0, tiled=True)
 
     def pack(side):
-        at = side * hid
-        cut = lambda w, axis: lax.dynamic_slice_in_dim(w, at, hid, axis)
+        cut = lambda w, axis: lax.dynamic_slice_in_dim(w, side * hid, hid, axis)
         d = cut(w_down, 0)
         up = jnp.concatenate([cut(w_gate, 1), cut(w_up, 1)], axis=1)
         return jnp.concatenate([up, d[:, : full // 2], d[:, full // 2 :]], axis=0)
 
-    mine, other = pack(core), pack(1 - core)
-    mine, tok = lax.optimization_barrier((mine, tok))
-    fwd, bwd, yy, swap = along_x(1), along_x(-1), route(along_y), route(other_core)
+    own_half, other_half = pack(core), pack(1 - core)
+    tall = own_half.shape[0]
+    cut = tall // 2
+    most = jnp.concatenate([other_half, own_half[:cut]])[None]
+    q0, q1 = own_half[None, :cut], own_half[None, cut:]
+    most, q0, q1, tok = lax.optimization_barrier((most, q0, q1, tok))
+    fwd, yy, swap = along_x(1), route(along_y), route(other_core)
     go = lambda x, pairs: lax.ppermute(x, BOTH, pairs)
-    a, b, y = go(mine, fwd), go(mine, bwd), go(mine, yy)
-    aa, ya, yb = go(a, fwd), go(a, yy), go(b, yy)
-    yaa = go(aa, yy)
-    got = [y, a, b, ya, yb, aa, yaa]
-    packs = [mine, other] + got + [go(g, swap) for g in got]
+    a_most, a1, y0, y1 = go(most, fwd), go(q1, fwd), go(q0, yy), go(q1, yy)
 
     f1 = pl.pallas_call(
         first_kernel,
         out_shape=jax.ShapeDtypeStruct((n_seq, n_chan, r_own, own), BF),
         in_specs=[smem] + [vmem] * 3,
         out_specs=vmem,
-        compiler_params=pltpu.CompilerParams(vmem_limit_bytes=32 << 20),
+        compiler_params=pltpu.CompilerParams(vmem_limit_bytes=60 << 20),
+        cost_estimate=pl.CostEstimate(flops=1, bytes_accessed=1, transcendentals=0),
         name="first",
     )(place, tok, right_in, twiddle_in)
     col = lax.all_to_all(f1.reshape(n_seq * n_chan, r_own, own), BOTH, 0, 0, tiled=True)
+    a_most, a1, y0, y1, col = lax.optimization_barrier((a_most, a1, y0, y1, col))
+    ya_most, ay1 = go(a_most, yy), go(y1, fwd)
+    aa0, aa1 = go(a_most[:, tall:], fwd), go(a1, fwd)
     f3 = pl.pallas_call(
         middle_kernel,
         out_shape=jax.ShapeDtypeStruct((blocks, r_own, own), BF),
         in_specs=[vmem] * 5,
         out_specs=vmem,
         scratch_shapes=[pltpu.VMEM((blocks * r_own, own), F32)] * 2,
-        compiler_params=pltpu.CompilerParams(vmem_limit_bytes=32 << 20),
+        compiler_params=pltpu.CompilerParams(vmem_limit_bytes=44 << 20),
+        cost_estimate=pl.CostEstimate(flops=1, bytes_accessed=1, transcendentals=0),
         name="middle",
     )(col, left_in, left_out, kernel, gain_in[None])
     back = lax.all_to_all(f3, BOTH, 0, 0, tiled=True).reshape(n_seq, n_chan, r_own, own)
-    count = len(packs)
-
-
+    late = [go(aa0, yy), go(ay1, fwd)]
+    shape = (inner, full)
+    rows_f32, rows_bf = jax.ShapeDtypeStruct(shape, F32), jax.ShapeDtypeStruct(shape, BF)
+    room = pltpu.CompilerParams(vmem_limit_bytes=28 << 20)
+    cost = pl.CostEstimate(flops=10**11, bytes_accessed=1, transcendentals=0)
+    stream, normed = pl.pallas_call(
+        third_kernel,
+        out_shape=(rows_bf, rows_bf),
+        in_specs=[smem, vmem, vmem, any_, vmem, vmem],
+        out_specs=(vmem, vmem),
+        scratch_shapes=[pltpu.VMEM(shape, F32), pltpu.VMEM(right_out.shape, BF), pltpu.SemaphoreType.DMA],
+        compiler_params=room,
+        name="third",
+    )(place, back, tok, right_out, twiddle_out, gain_mlp[None])
+
+    def mlp(name, rows, before, begun, packs, out):
+        packs, spans = zip(*packs)
+        count = sum(stop - start for start, stop in spans) // tall
+        pieces = sum(-(-(stop - start) // tall) for start, stop in spans)
+        return pl.pallas_call(
+            functools.partial(mlp_kernel, spans, begun),
+            out_shape=out,
+            in_specs=[vmem, vmem if begun else any_] + [any_] * len(packs),
+            out_specs=vmem,
+            scratch_shapes=([] if out is rows_f32 else [pltpu.VMEM(shape, F32)])
+            + [
+                pltpu.VMEM((count, tall, 2 * hid), BF),
+                pltpu.SemaphoreType.DMA((pieces,)),
+                pltpu.VMEM((inner, 2 * hid), F32),
+                pltpu.VMEM((inner, 2 * hid), F32),
+            ],
+            compiler_params=room,
+            cost_estimate=cost,
+            name=name,
+        )(rows, before, *packs)
+
+    theirs = go(normed, swap)
+    whole = lambda *arrays: [(w, (0, w.shape[1])) for w in arrays]
+    early = whole(q0, q1, a_most, a1, y0, y1) + [(ya_most, (0, tall))]
+    late = [(ya_most, (tall, tall + cut))] + whole(ay1, aa0, aa1, *late)
+    own_sum = mlp("own", normed, stream, True, early, rows_f32)
+    their_sum = mlp("their", theirs, own_sum, False, early, rows_f32)
+    partial = go(mlp("their_late", theirs, their_sum, True, late, rows_bf), swap)
+    own_sum = mlp("own_late", normed, own_sum, True, late, rows_f32)
     done = pl.pallas_call(
-        functools.partial(last_kernel, count),
+        sum_kernel,
         out_shape=jax.ShapeDtypeStruct((n_chan, inner, own), BF),
-        in_specs=[smem] + [vmem] * 5 + [any_] * count,
+        in_specs=[vmem] * 2,
         out_specs=vmem,
-        scratch_shapes=[
-            pltpu.VMEM((count,) + mine.shape, BF),
-            pltpu.VMEM((inner, full), F32),
-            pltpu.VMEM((inner, full), BF),
-            pltpu.SemaphoreType.DMA((count,)),
-        ],
-        compiler_params=pltpu.CompilerParams(vmem_limit_bytes=56 << 20),
-        name="last",
-    )(place, back, tok, right_out, twiddle_out, gain_mlp[None], *packs)
+        compiler_params=room,
+        name="sum",
+    )(own_sum, partial)
     out = lax.all_to_all(done, "chan", 0, 0, tiled=True)
     return out.reshape(tokens.shape)
 

time: 200 us -> 169 us (0.84)
  waiting for transfers between devices: 101 us -> 57.1 us
  starting transfers between devices: 46.9 us -> 52.7 us
  Pallas kernels: 25.6 us -> 29.4 us
  other arithmetic: 2.64 us -> 5.16 us
    all_to_all x1, waiting for transfers between devices: 24.6 us -> 0.01 us  [local(): lax.all_to_all(f1.reshape(n_seq * n_chan, r_own, own), BOTH, 0, 0, tiled=...]
    ppermute x14 -> x12, waiting for transfers between devices: 64.8 us -> 48.1 us  [local(): go = lambda x, pairs: lax.ppermute(x, BOTH, pairs)]
    ppermute x14 -> x12, starting transfers between devices: 15.4 us -> 21.9 us  [local(): go = lambda x, pairs: lax.ppermute(x, BOTH, pairs)]
    broadcast_in_dim x0 -> x2, other arithmetic: none -> 5.16 us  [the longest x1 4.13 us: local(): most = jnp.concatenate([other_half, own_half[:cut]])[None]]
    all_to_all x1, starting transfers between devices: 18.2 us -> 14 us  [local(): lax.all_to_all(f1.reshape(n_seq * n_chan, r_own, own), BOTH, 0, 0, tiled=...]
    all_to_all x1, starting transfers between devices: 7.43 us -> 10.9 us  [local(): lax.all_to_all(f3, BOTH, 0, 0, tiled=True)]
    concatenate x2 -> x0, other arithmetic: 2.64 us -> none  [pack(): return jnp.concatenate([up, d[:, :full // 2], d[:, full // 2:]], axis=0)]
    pallas_call x1 -> x6, Pallas kernels: 20.2 us -> 22.5 us  [the longest x4 20.8 us: mlp(): pl.pallas_call(functools.partial(mlp_kernel, spans, begun), out_shape=out...]
  transfers between devices with their start and end apart: 17 -> 15, of which waited for: 6 -> 5; matrix products, arithmetic and copies ran while one was open for 3% -> 5% of each run, Pallas kernels for 3% -> 15%
where the time goes in v3:
time: 169 us
  waiting for transfers between devices  57.1 us (34%)
  starting transfers between devices  52.7 us (31%)
  Pallas kernels  29.4 us (17%)
  blocking collectives  18.4 us (11%)
  local copies, waits for them, and re-layouts  6.04 us (4%)
  other arithmetic  5.16 us (3%)
    ppermute x12, waiting for transfers between devices, local(): go = lambda x, pairs: lax.ppermute(x, BOTH, pairs)  48.1 us
    ppermute x12, starting transfers between devices, local(): go = lambda x, pairs: lax.ppermute(x, BOTH, pairs)  21.9 us
    pallas_call x4, Pallas kernels, mlp(): pl.pallas_call(functools.partial(mlp_kernel, spans, begun), out_shape=out...  20.8 us
    all_to_all x1, blocking collectives, local(): out = lax.all_to_all(done, 'chan', 0, 0, tiled=True)  18.4 us
    all_to_all x1, starting transfers between devices, local(): lax.all_to_all(f1.reshape(n_seq * n_chan, r_own, own), BOTH, 0, 0, tiled=...  14 us
    all_to_all x1, starting transfers between devices, local(): lax.all_to_all(f3, BOTH, 0, 0, tiled=True)  10.9 us
    all_to_all x1, waiting for transfers between devices, local(): lax.all_to_all(tokens.reshape(n_chan, inner, own), 'chan', 0, 0, tiled=True)  8.97 us
    all_to_all x1, starting transfers between devices, local(): lax.all_to_all(tokens.reshape(n_chan, inner, own), 'chan', 0, 0, tiled=True)  5.99 us
  transfers between devices with their start and end apart: 15, of which 5 were waited for; matrix products, arithmetic and copies ran while one was open for 5% of the time, Pallas kernels for 15%

profile of v3, /device:TPU:1, one launch (start us, length us, event | category | flops | bytes accessed | tf_op | source)
XLA Modules:
  0.0 169.0 jit_solution(17593415156522217670)
XLA Ops:
  0.0 6.0 %all-to-all-start = ((bf16[8,512,128]{2,1,0:T(8,128)(2,1)}), bf16[8,512,128]{2,1,0:T(8,128)(2,1)S(1)}, u32[]{:S(2)}, u32[]{:S(2)}) async-start(bf16[8,512,128]{2,1,0:T(8,128)(2,1)} %bitcast.20), calls=%async_computation | async-start | bytes 2097152 | tf_op jit(solution)/shard_map/all_to_all | solution.py:182
  6.0 1.4 constant_dynamic-slice_fusion.1
  7.4 0.0 copy-done.16
  7.4 0.2 copy-done.17
  7.5 0.1 constant_dynamic-slice_fusion.4
  7.7 1.0 fusion
  8.7 4.1 %maximum_bitcast_fusion = bf16[1,2304,512]{2,1,0:T(8,128)(2,1)} fusion(bf16[768,512]{1,0:T(8,128)(2,1)S(1)} %get-tuple-element.28, bf16[256,512]{1,0:T(8,128)(2,1)S(1)} %get-tuple-element.32, bf16[256,512]{1,0:T(8,128)(2,1)S(1)} %get-tuple-element.30, bf16[1024,256]{1,0:T(8,128)(2,1)S(1)} %get-tuple-element.35, bf16[1024,256]{1,0:T(8,128)(2,1)S(1)} %get-tuple-element.38), kind=kLoop, calls=%fused_computation | loop fusion | flops 11796480 | bytes 4718592 | tf_op jit(solution)/shard_map/broadcast_in_dim | solution.py:193
  12.8 9.0 %all-to-all-done.tok = bf16[8,512,128]{2,1,0:T(8,128)(2,1)S(1)} async-done(((bf16[8,512,128]{2,1,0:T(8,128)(2,1)}), bf16[8,512,128]{2,1,0:T(8,128)(2,1)S(1)}, u32[]{:S(2)}, u32[]{:S(2)}) %all-to-all-start) | async-done | bytes 1048608 | tf_op jit(solution)/shard_map/all_to_all | solution.py:182
  21.8 0.6 collective-permute-start
  22.4 0.3 copy-done
  22.8 3.7 %first.1 = bf16[32,8,16,128]{3,2,1,0:T(8,128)(2,1)} custom-call(s32[1]{0:T(128)} %bitcast.place, bf16[8,512,128]{2,1,0:T(8,128)(2,1)} %copy-done, bf16[512,512]{1,0:T(8,128)(2,1)} %right.1, f32[8,512]{1,0:T(8,128)} %tw.2), custom_call_target="tpu_custom_call" | custom-call | flops 1 | bytes 1 | tf_op jit(solution)/shard_map/first/pallas_call | solution.py:200
  26.5 14.0 %all-to-all-start.1 = ((bf16[256,16,128]{2,1,0:T(8,128)(2,1)}), bf16[256,16,128]{2,1,0:T(8,128)(2,1)S(1)}, u32[]{:S(2)}, u32[]{:S(2)}) async-start(bf16[256,16,128]{2,1,0:T(8,128)(2,1)} %bitcast.18), calls=%async_computation.1 | async-start | bytes 2097152 | tf_op jit(solution)/shard_map/all_to_all | solution.py:209
  40.5 2.7 %collective-permute-start.1 = (bf16[1,768,512]{2,1,0:T(8,128)(2,1)}, bf16[1,768,512]{2,1,0:T(8,128)(2,1)S(1)}, u32[]{:S(2)}, u32[]{:S(2)}) collective-permute-start(bf16[1,768,512]{2,1,0:T(8,128)(2,1)} %get-tuple-element.17.rest_1_), channel_id=1, source_target_pairs={{0,1},{1,2},{2,3},{3,0},{4,5},{5,6},{6,7},{7,4},{8,11},{9,8},{10,9... | collective-permute-start | bytes 2359304 | tf_op jit(solution)/shard_map/ppermute | solution.py:197
  43.1 2.5 %collective-permute-start.2 = (bf16[1,768,512]{2,1,0:T(8,128)(2,1)S(1)}, bf16[1,768,512]{2,1,0:T(8,128)(2,1)S(1)}, u32[]{:S(2)}, u32[]{:S(2)}) collective-permute-start(bf16[1,768,512]{2,1,0:T(8,128)(2,1)S(1)} %bitcast.13), channel_id=1, source_target_pairs={{0,4},{1,5},{2,6},{3,7},{4,128},{5,129},{6,130},{7,131},{8,140},{9... | collective-permute-start | bytes 2359304 | tf_op jit(solution)/shard_map/ppermute | solution.py:197
  45.6 0.5 collective-permute-start.3
  46.1 23.6 %collective-permute-done.1.rest_3_ = bf16[1,768,512]{2,1,0:T(8,128)(2,1)S(1)} collective-permute-done((bf16[1,768,512]{2,1,0:T(8,128)(2,1)}, bf16[1,768,512]{2,1,0:T(8,128)(2,1)S(1)}, u32[]{:S(2)}, u32[]{:S(2)}) %collective-permute-start.1) | collective-permute-done | bytes 786464 | tf_op jit(solution)/shard_map/ppermute | solution.py:197
  69.8 0.0 collective-permute-done.2.rest_4_
  69.8 0.9 copy-done.12
  70.7 1.0 copy-done.14
  71.6 1.1 collective-permute-done.3.rest_5_
  72.7 0.0 all-to-all-done.1.col
  72.7 0.0 collective-permute-done.rest_2_
  72.7 2.8 %collective-permute-start.4 = (bf16[1,2304,512]{2,1,0:T(8,128)(2,1)}, bf16[1,2304,512]{2,1,0:T(8,128)(2,1)}, u32[]{:S(2)}, u32[]{:S(2)}) collective-permute-start(bf16[1,2304,512]{2,1,0:T(8,128)(2,1)} %collective-permute-done.rest_2_), channel_id=1, source_target_pairs={{0,4},{1,5},{2,6},{3,7},{4,128},{5,129},{6,130},{7,131},{8,140},{9... | collective-permute-start | bytes 7077896 | tf_op jit(solution)/shard_map/ppermute | solution.py:197
  75.6 0.0 copy-done.2
  75.6 0.0 copy-done.5
  75.6 0.0 copy-done.6
  75.6 0.0 copy-done.9
  75.6 3.2 %middle.1 = bf16[256,16,128]{2,1,0:T(8,128)(2,1)} custom-call(bf16[256,16,128]{2,1,0:T(8,128)(2,1)S(1)} %all-to-all-done.1.col, bf16[256,256]{1,0:T(8,128)(2,1)S(1)} %copy-done.5, bf16[256,256]{1,0:T(8,128)(2,1)S(1)} %copy-done.6, bf16[256,16,128]{2,1,0:T(8,128)(2,1)S(1)} %copy-done.2, f32[1,128]{1,0:T(1,128)S(1)} %bitcast.17), custom_call_target="tpu_custom_call" | custom-call | flops 1 | bytes 1 | tf_op jit(solution)/shard_map/middle/pallas_call | solution.py:213
  78.8 10.9 %all-to-all-start.2 = ((bf16[256,16,128]{2,1,0:T(8,128)(2,1)}), bf16[256,16,128]{2,1,0:T(8,128)(2,1)S(1)}, u32[]{:S(2)}, u32[]{:S(2)}) async-start(bf16[256,16,128]{2,1,0:T(8,128)(2,1)} %middle.1), calls=%async_computation.2 | async-start | bytes 2097152 | tf_op jit(solution)/shard_map/all_to_all | solution.py:223
  89.7 1.2 slice.28
  90.9 2.7 %collective-permute-start.6 = (bf16[1,768,512]{2,1,0:T(8,128)(2,1)S(1)}, bf16[1,768,512]{2,1,0:T(8,128)(2,1)}, u32[]{:S(2)}, u32[]{:S(2)}) collective-permute-start(bf16[1,768,512]{2,1,0:T(8,128)(2,1)S(1)} %slice.28), channel_id=1, source_target_pairs={{0,1},{1,2},{2,3},{3,0},{4,5},{5,6},{6,7},{7,4},{8,11},{9,8},{10,9... | collective-permute-start | bytes 2359304 | tf_op jit(solution)/shard_map/ppermute | solution.py:197
  93.6 0.6 collective-permute-start.5
  94.2 0.3 collective-permute-start.7
  94.5 14.5 %collective-permute-done.6.rest_2_ = bf16[1,768,512]{2,1,0:T(8,128)(2,1)} collective-permute-done((bf16[1,768,512]{2,1,0:T(8,128)(2,1)S(1)}, bf16[1,768,512]{2,1,0:T(8,128)(2,1)}, u32[]{:S(2)}, u32[]{:S(2)}) %collective-permute-start.6) | collective-permute-done | bytes 786464 | tf_op jit(solution)/shard_map/ppermute | solution.py:197
  109.0 2.3 %collective-permute-start.8 = (bf16[1,768,512]{2,1,0:T(8,128)(2,1)}, bf16[1,768,512]{2,1,0:T(8,128)(2,1)}, u32[]{:S(2)}, u32[]{:S(2)}) collective-permute-start(bf16[1,768,512]{2,1,0:T(8,128)(2,1)} %collective-permute-done.6.rest_2_), channel_id=1, source_target_pairs={{0,4},{1,5},{2,6},{3,7},{4,128},{5,129},{6,130},{7,131},{8,140},{9... | collective-permute-start | bytes 2359304 | tf_op jit(solution)/shard_map/ppermute | solution.py:197
  111.3 8.8 %collective-permute-done.5.rest_1_ = bf16[1,768,512]{2,1,0:T(8,128)(2,1)} collective-permute-done((bf16[1,768,512]{2,1,0:T(8,128)(2,1)}, bf16[1,768,512]{2,1,0:T(8,128)(2,1)}, u32[]{:S(2)}, u32[]{:S(2)}) %collective-permute-start.5) | collective-permute-done | bytes 786464 | tf_op jit(solution)/shard_map/ppermute | solution.py:197
  120.1 3.3 %collective-permute-start.9 = (bf16[1,768,512]{2,1,0:T(8,128)(2,1)}, bf16[1,768,512]{2,1,0:T(8,128)(2,1)}, u32[]{:S(2)}, u32[]{:S(2)}) collective-permute-start(bf16[1,768,512]{2,1,0:T(8,128)(2,1)} %collective-permute-done.5.rest_1_), channel_id=1, source_target_pairs={{0,1},{1,2},{2,3},{3,0},{4,5},{5,6},{6,7},{7,4},{8,11},{9,8},{10,9... | collective-permute-start | bytes 2359304 | tf_op jit(solution)/shard_map/ppermute | solution.py:197
  123.4 0.0 all-to-all-done.2
  123.4 0.0 copy-done.1
  123.5 0.0 copy-done.4
  123.5 0.0 copy-done.7
  123.5 0.0 copy-done.8
  123.5 1.4 third.1
  124.9 0.0 copy-start.10
  124.9 0.4 collective-permute-start.10
  125.3 0.0 collective-permute-done.4.rest_6_.rest_0_
  125.3 0.0 copy-done.3
  125.3 0.0 copy-done.13
  125.3 0.0 copy-done.15
  125.3 5.9 %own.1.before = f32[512,1024]{1,0:T(8,128)S(1)} custom-call(bf16[512,1024]{1,0:T(8,128)(2,1)S(1)} %get-tuple-element.21.normed, bf16[512,1024]{1,0:T(8,128)(2,1)S(1)} %get-tuple-element.22.before, bf16[1,768,512]{2,1,0:T(8,128)(2,1)S(1)} %bitcast.14, bf16[1,768,512]{2,1,0:T(8,128)(2,1)S(1)} %copy-done.3, bf16[1,2304,512]{2,1,0:T(8,128)(2,1)} %collective-permute-done.rest_2_, ...), custom_call_target="tpu_custom_call" | custom-call | flops 99999997952 | bytes 1 | tf_op jit(solution)/shard_map/own/pallas_call | solution.py:243
  131.2 0.0 copy-done.10
  131.3 0.0 collective-permute-done.10.normed
  131.3 5.9 %their.1.before = f32[512,1024]{1,0:T(8,128)S(1)} custom-call(bf16[512,1024]{1,0:T(8,128)(2,1)S(1)} %collective-permute-done.10.normed, f32[512,1024]{1,0:T(8,128)S(1)} %own.1.before, bf16[1,768,512]{2,1,0:T(8,128)(2,1)S(1)} %bitcast.15, bf16[1,768,512]{2,1,0:T(8,128)(2,1)S(1)} %copy-done.3, bf16[1,2304,512]{2,1,0:T(8,128)(2,1)} %collective-permute-done.rest_2_, ...), custom_call_target="tpu_custom_call" | custom-call | flops 99999997952 | bytes 1 | tf_op jit(solution)/shard_map/their/pallas_call | solution.py:243
  137.2 0.0 copy-start.11
  137.2 0.0 collective-permute-done.7.rest_3_
  137.2 0.0 collective-permute-done.8.rest_4_
  137.2 0.0 collective-permute-done.9.rest_5_
  137.2 4.5 %their_late.1 = bf16[512,1024]{1,0:T(8,128)(2,1)S(1)} custom-call(bf16[512,1024]{1,0:T(8,128)(2,1)S(1)} %collective-permute-done.10.normed, f32[512,1024]{1,0:T(8,128)S(1)} %their.1.before, bf16[1,2304,512]{2,1,0:T(8,128)(2,1)} %collective-permute-done.4.rest_6_.rest_0_, bf16[1,768,512]{2,1,0:T(8,128)(2,1)} %collective-permute-done.5.rest_1_, ...), custom_call_target="tpu_custom_call" | custom-call | flops 99999997952 | bytes 1 | tf_op jit(solution)/shard_map/their_late/pallas_call | solution.py:243
  141.8 3.1 %collective-permute-start.11 = (bf16[512,1024]{1,0:T(8,128)(2,1)S(1)}, bf16[512,1024]{1,0:T(8,128)(2,1)S(1)}, u32[]{:S(2)}, u32[]{:S(2)}) collective-permute-start(bf16[512,1024]{1,0:T(8,128)(2,1)S(1)} %their_late.1), channel_id=1, source_target_pairs={{0,8},{1,9},{2,10},{3,11},{4,12},{5,13},{6,14},{7,15},{8,0},{9,1},... | collective-permute-start | bytes 3145736 | tf_op jit(solution)/shard_map/ppermute | solution.py:197
  144.9 4.5 %own_late.1.a = f32[512,1024]{1,0:T(8,128)S(1)} custom-call(bf16[512,1024]{1,0:T(8,128)(2,1)S(1)} %copy-done.11, f32[512,1024]{1,0:T(8,128)S(1)} %own.1.before, bf16[1,2304,512]{2,1,0:T(8,128)(2,1)} %collective-permute-done.4.rest_6_.rest_0_, bf16[1,768,512]{2,1,0:T(8,128)(2,1)} %collective-permute-done.5.rest_1_, ...), custom_call_target="tpu_custom_call" | custom-call | flops 99999997952 | bytes 1 | tf_op jit(solution)/shard_map/own_late/pallas_call | solution.py:243
  149.4 0.0 collective-permute-done.11.b
  149.4 0.3 sum.1
  149.7 18.4 %all_to_all.20 = bf16[8,512,128]{2,1,0:T(8,128)(2,1)S(1)} all-to-all(bf16[8,512,128]{2,1,0:T(8,128)(2,1)S(1)} %sum.1), channel_id=1, replica_groups=mesh['seq'=32,'chan'=8] {'chan'}, dimensions={0} | all-to-all | bytes 2097152 | tf_op jit(solution)/shard_map/all_to_all | solution.py:276
  168.1 1.0 copy.15
  (17 shorter events, 0.0 us)
Async XLA Ops:
  0.0 7.4 %copy-start.16 = (bf16[1024,512]{1,0:T(8,128)(2,1)S(1)}, bf16[1024,512]{1,0:T(8,128)(2,1)}, u32[]{:S(2)}) copy-start(bf16[1024,512]{1,0:T(8,128)(2,1)} %param.24) | copy-start | bytes 3145732
  0.0 21.8 %all-to-all-start = ((bf16[8,512,128]{2,1,0:T(8,128)(2,1)}), bf16[8,512,128]{2,1,0:T(8,128)(2,1)S(1)}, u32[]{:S(2)}, u32[]{:S(2)}) async-start(bf16[8,512,128]{2,1,0:T(8,128)(2,1)} %bitcast.20), calls=%async_computation | async-start | bytes 2097152 | tf_op jit(solution)/shard_map/all_to_all | solution.py:182
  6.0 1.5 copy-start.17
  21.8 1.0 copy-start
  21.8 50.9 %collective-permute-start = (bf16[1,2304,512]{2,1,0:T(8,128)(2,1)}, bf16[1,2304,512]{2,1,0:T(8,128)(2,1)}, u32[]{:S(2)}, u32[]{:S(2)}) collective-permute-start(bf16[1,2304,512]{2,1,0:T(8,128)(2,1)} %maximum_bitcast_fusion), channel_id=1, source_target_pairs={{0,1},{1,2},{2,3},{3,0},{4,5},{5,6},{6,7},{7,4},{8,11},{9,8},{10,9... | collective-permute-start | bytes 7077896 | tf_op jit(solution)/shard_map/ppermute | solution.py:197
  22.8 52.8 %copy-start.2 = (bf16[256,16,128]{2,1,0:T(8,128)(2,1)S(1)}, bf16[256,16,128]{2,1,0:T(8,128)(2,1)}, u32[]{:S(2)}) copy-start(bf16[256,16,128]{2,1,0:T(8,128)(2,1)} %kern.1) | copy-start | bytes 3145732
  22.8 52.8 %copy-start.5 = (bf16[256,256]{1,0:T(8,128)(2,1)S(1)}, bf16[256,256]{1,0:T(8,128)(2,1)}, u32[]{:S(2)}) copy-start(bf16[256,256]{1,0:T(8,128)(2,1)} %left_in.1) | copy-start | bytes 393220
  22.8 52.8 %copy-start.6 = (bf16[256,256]{1,0:T(8,128)(2,1)S(1)}, bf16[256,256]{1,0:T(8,128)(2,1)}, u32[]{:S(2)}) copy-start(bf16[256,256]{1,0:T(8,128)(2,1)} %left_out.1) | copy-start | bytes 393220
  22.8 52.8 %copy-start.9 = (f32[128]{0:T(128)S(1)}, f32[128]{0:T(128)}, u32[]{:S(2)}) copy-start(f32[128]{0:T(128)} %param.14) | copy-start | bytes 1540
  26.5 46.2 %all-to-all-start.1 = ((bf16[256,16,128]{2,1,0:T(8,128)(2,1)}), bf16[256,16,128]{2,1,0:T(8,128)(2,1)S(1)}, u32[]{:S(2)}, u32[]{:S(2)}) async-start(bf16[256,16,128]{2,1,0:T(8,128)(2,1)} %bitcast.18), calls=%async_computation.1 | async-start | bytes 2097152 | tf_op jit(solution)/shard_map/all_to_all | solution.py:209
  40.5 29.3 %collective-permute-start.1 = (bf16[1,768,512]{2,1,0:T(8,128)(2,1)}, bf16[1,768,512]{2,1,0:T(8,128)(2,1)S(1)}, u32[]{:S(2)}, u32[]{:S(2)}) collective-permute-start(bf16[1,768,512]{2,1,0:T(8,128)(2,1)} %get-tuple-element.17.rest_1_), channel_id=1, source_target_pairs={{0,1},{1,2},{2,3},{3,0},{4,5},{5,6},{6,7},{7,4},{8,11},{9,8},{10,9... | collective-permute-start | bytes 2359304 | tf_op jit(solution)/shard_map/ppermute | solution.py:197
  43.1 26.7 %collective-permute-start.2 = (bf16[1,768,512]{2,1,0:T(8,128)(2,1)S(1)}, bf16[1,768,512]{2,1,0:T(8,128)(2,1)S(1)}, u32[]{:S(2)}, u32[]{:S(2)}) collective-permute-start(bf16[1,768,512]{2,1,0:T(8,128)(2,1)S(1)} %bitcast.13), channel_id=1, source_target_pairs={{0,4},{1,5},{2,6},{3,7},{4,128},{5,129},{6,130},{7,131},{8,140},{9... | collective-permute-start | bytes 2359304 | tf_op jit(solution)/shard_map/ppermute | solution.py:197
  45.6 27.1 %collective-permute-start.3 = (bf16[1,768,512]{2,1,0:T(8,128)(2,1)}, bf16[1,768,512]{2,1,0:T(8,128)(2,1)}, u32[]{:S(2)}, u32[]{:S(2)}) collective-permute-start(bf16[1,768,512]{2,1,0:T(8,128)(2,1)} %get-tuple-element.17.rest_1_), channel_id=1, source_target_pairs={{0,4},{1,5},{2,6},{3,7},{4,128},{5,129},{6,130},{7,131},{8,140},{9... | collective-permute-start | bytes 2359304 | tf_op jit(solution)/shard_map/ppermute | solution.py:197
  69.8 0.9 copy-start.12
  70.7 1.0 copy-start.14
  72.7 52.6 %collective-permute-start.4 = (bf16[1,2304,512]{2,1,0:T(8,128)(2,1)}, bf16[1,2304,512]{2,1,0:T(8,128)(2,1)}, u32[]{:S(2)}, u32[]{:S(2)}) collective-permute-start(bf16[1,2304,512]{2,1,0:T(8,128)(2,1)} %collective-permute-done.rest_2_), channel_id=1, source_target_pairs={{0,4},{1,5},{2,6},{3,7},{4,128},{5,129},{6,130},{7,131},{8,140},{9... | collective-permute-start | bytes 7077896 | tf_op jit(solution)/shard_map/ppermute | solution.py:197
  78.8 44.6 %copy-start.1 = (bf16[8,512,128]{2,1,0:T(8,128)(2,1)S(1)}, bf16[8,512,128]{2,1,0:T(8,128)(2,1)}, u32[]{:S(2)}) copy-start(bf16[8,512,128]{2,1,0:T(8,128)(2,1)} %copy-done) | copy-start | bytes 3145732
  78.8 44.6 %copy-start.4 = (bf16[512,512]{1,0:T(8,128)(2,1)S(1)}, bf16[512,512]{1,0:T(8,128)(2,1)}, u32[]{:S(2)}) copy-start(bf16[512,512]{1,0:T(8,128)(2,1)} %right_hbm.1) | copy-start | bytes 1572868
  78.8 44.7 %copy-start.7 = (f32[8,512]{1,0:T(8,128)S(1)}, f32[8,512]{1,0:T(8,128)}, u32[]{:S(2)}) copy-start(f32[8,512]{1,0:T(8,128)} %tw.3) | copy-start | bytes 49156
  78.8 44.7 %copy-start.8 = (f32[1024]{0:T(1024)S(1)}, f32[1024]{0:T(1024)}, u32[]{:S(2)}) copy-start(f32[1024]{0:T(1024)} %param.22) | copy-start | bytes 12292
  78.8 44.6 %all-to-all-start.2 = ((bf16[256,16,128]{2,1,0:T(8,128)(2,1)}), bf16[256,16,128]{2,1,0:T(8,128)(2,1)S(1)}, u32[]{:S(2)}, u32[]{:S(2)}) async-start(bf16[256,16,128]{2,1,0:T(8,128)(2,1)} %middle.1), calls=%async_computation.2 | async-start | bytes 2097152 | tf_op jit(solution)/shard_map/all_to_all | solution.py:223
  90.9 18.1 %collective-permute-start.6 = (bf16[1,768,512]{2,1,0:T(8,128)(2,1)S(1)}, bf16[1,768,512]{2,1,0:T(8,128)(2,1)}, u32[]{:S(2)}, u32[]{:S(2)}) collective-permute-start(bf16[1,768,512]{2,1,0:T(8,128)(2,1)S(1)} %slice.28), channel_id=1, source_target_pairs={{0,1},{1,2},{2,3},{3,0},{4,5},{5,6},{6,7},{7,4},{8,11},{9,8},{10,9... | collective-permute-start | bytes 2359304 | tf_op jit(solution)/shard_map/ppermute | solution.py:197
  93.6 26.5 %collective-permute-start.5 = (bf16[1,768,512]{2,1,0:T(8,128)(2,1)}, bf16[1,768,512]{2,1,0:T(8,128)(2,1)}, u32[]{:S(2)}, u32[]{:S(2)}) collective-permute-start(bf16[1,768,512]{2,1,0:T(8,128)(2,1)} %collective-permute-done.3.rest_5_), channel_id=1, source_target_pairs={{0,1},{1,2},{2,3},{3,0},{4,5},{5,6},{6,7},{7,4},{8,11},{9,8},{10,9... | collective-permute-start | bytes 2359304 | tf_op jit(solution)/shard_map/ppermute | solution.py:197
  94.2 43.0 %collective-permute-start.7 = (bf16[1,768,512]{2,1,0:T(8,128)(2,1)}, bf16[1,768,512]{2,1,0:T(8,128)(2,1)}, u32[]{:S(2)}, u32[]{:S(2)}) collective-permute-start(bf16[1,768,512]{2,1,0:T(8,128)(2,1)} %copy-done.12), channel_id=1, source_target_pairs={{0,1},{1,2},{2,3},{3,0},{4,5},{5,6},{6,7},{7,4},{8,11},{9,8},{10,9... | collective-permute-start | bytes 2359304 | tf_op jit(solution)/shard_map/ppermute | solution.py:197
  109.0 28.2 %collective-permute-start.8 = (bf16[1,768,512]{2,1,0:T(8,128)(2,1)}, bf16[1,768,512]{2,1,0:T(8,128)(2,1)}, u32[]{:S(2)}, u32[]{:S(2)}) collective-permute-start(bf16[1,768,512]{2,1,0:T(8,128)(2,1)} %collective-permute-done.6.rest_2_), channel_id=1, source_target_pairs={{0,4},{1,5},{2,6},{3,7},{4,128},{5,129},{6,130},{7,131},{8,140},{9... | collective-permute-start | bytes 2359304 | tf_op jit(solution)/shard_map/ppermute | solution.py:197
  120.1 17.1 %collective-permute-start.9 = (bf16[1,768,512]{2,1,0:T(8,128)(2,1)}, bf16[1,768,512]{2,1,0:T(8,128)(2,1)}, u32[]{:S(2)}, u32[]{:S(2)}) collective-permute-start(bf16[1,768,512]{2,1,0:T(8,128)(2,1)} %collective-permute-done.5.rest_1_), channel_id=1, source_target_pairs={{0,1},{1,2},{2,3},{3,0},{4,5},{5,6},{6,7},{7,4},{8,11},{9,8},{10,9... | collective-permute-start | bytes 2359304 | tf_op jit(solution)/shard_map/ppermute | solution.py:197
  123.4 1.9 %copy-start.3 = (bf16[1,768,512]{2,1,0:T(8,128)(2,1)S(1)}, bf16[1,768,512]{2,1,0:T(8,128)(2,1)}, u32[]{:S(2)}) copy-start(bf16[1,768,512]{2,1,0:T(8,128)(2,1)} %get-tuple-element.17.rest_1_) | copy-start | bytes 2359300
  123.4 1.9 %copy-start.13 = (bf16[1,768,512]{2,1,0:T(8,128)(2,1)S(1)}, bf16[1,768,512]{2,1,0:T(8,128)(2,1)}, u32[]{:S(2)}) copy-start(bf16[1,768,512]{2,1,0:T(8,128)(2,1)} %copy-done.12) | copy-start | bytes 2359300
  123.4 1.9 %copy-start.15 = (bf16[1,768,512]{2,1,0:T(8,128)(2,1)S(1)}, bf16[1,768,512]{2,1,0:T(8,128)(2,1)}, u32[]{:S(2)}) copy-start(bf16[1,768,512]{2,1,0:T(8,128)(2,1)} %copy-done.14) | copy-start | bytes 2359300
  124.9 6.3 %copy-start.10 = (bf16[512,1024]{1,0:T(8,128)(2,1)}, bf16[512,1024]{1,0:T(8,128)(2,1)S(1)}, u32[]{:S(2)}) copy-start(bf16[512,1024]{1,0:T(8,128)(2,1)S(1)} %get-tuple-element.21.normed) | copy-start | bytes 3145732
  124.9 6.3 %collective-permute-start.10 = (bf16[512,1024]{1,0:T(8,128)(2,1)S(1)}, bf16[512,1024]{1,0:T(8,128)(2,1)S(1)}, u32[]{:S(2)}, u32[]{:S(2)}) collective-permute-start(bf16[512,1024]{1,0:T(8,128)(2,1)S(1)} %get-tuple-element.21.normed), channel_id=1, source_target_pairs={{0,8},{1,9},{2,10},{3,11},{4,12},{5,13},{6,14},{7,15},{8,0},{9,1},... | collective-permute-start | bytes 3145736 | tf_op jit(solution)/shard_map/ppermute | solution.py:197
  137.2 7.7 %copy-start.11 = (bf16[512,1024]{1,0:T(8,128)(2,1)S(1)}, bf16[512,1024]{1,0:T(8,128)(2,1)}, u32[]{:S(2)}) copy-start(bf16[512,1024]{1,0:T(8,128)(2,1)} %copy-done.10) | copy-start | bytes 3145732
  141.8 7.6 %collective-permute-start.11 = (bf16[512,1024]{1,0:T(8,128)(2,1)S(1)}, bf16[512,1024]{1,0:T(8,128)(2,1)S(1)}, u32[]{:S(2)}, u32[]{:S(2)}) collective-permute-start(bf16[512,1024]{1,0:T(8,128)(2,1)S(1)} %their_late.1), channel_id=1, source_target_pairs={{0,8},{1,9},{2,10},{3,11},{4,12},{5,13},{6,14},{7,15},{8,0},{9,1},... | collective-permute-start | bytes 3145736 | tf_op jit(solution)/shard_map/ppermute | solution.py:197

commit v4 on v3

--- a/solution.py
+++ b/solution.py
@@ -80,7 +80,7 @@
     out[...] = flat[...].reshape(blocks, inner, width).astype(BF)
 
 
-def mlp_over(packs, weights, sems, first, second, normed, acc, prepare):
+def mlp_over(packs, weights, sems, first, second, normed, acc, base):
     full = normed.shape[1]
     hid, half = weights.shape[2] // 2, full // 2
     count = weights.shape[0]
@@ -94,13 +94,17 @@
             sem = sems.at[sum(map(len, slots))]
             piece = pack.at[0, pl.ds(done, rows)]
             slots[i].append(pltpu.make_async_copy(piece, weights.at[i, pl.ds(row, rows)], sem))
-            slots[i][-1].start()
             at, done = at + rows, done + rows
-    prepare()
+    for i in range(min(2, count)):
+        for copy in slots[i]:
+            copy.start()
 
     def up_to(i, to):
         for copy in slots[i]:
             copy.wait()
+        if i + 2 < count:
+            for copy in slots[i + 2]:
+                copy.start()
         to[...] = jnp.dot(normed[...], weights[i, :full, :], preferred_element_type=F32)
 
     def down_from(i, both):
@@ -108,7 +112,13 @@
         hidden = (gate * up / (1.0 + jnp.exp(-gate))).astype(BF)
         for k in range(2):
             down = weights[i, full + k * hid : full + (k + 1) * hid, :]
-            acc[:, k * half : (k + 1) * half] += jnp.dot(hidden, down, preferred_element_type=F32)
+            at = slice(k * half, (k + 1) * half)
+            part = jnp.dot(hidden, down, preferred_element_type=F32)
+            if i > 0:
+                part = part + acc[:, at]
+            elif base is not None:
+                part = part + base[:, at].astype(F32)
+            acc[:, at] = part
 
     held = (first, second)
     up_to(0, first)
@@ -147,10 +157,7 @@
     packs = list(zip(packs, spans))
     acc = spare[0] if spare else out
 
-    def prepare():
-        acc[...] = before[...].astype(F32) if begun else jnp.zeros_like(acc)
-
-    mlp_over(packs, weights, sems, one, two, normed, acc, prepare)
+    mlp_over(packs, weights, sems, one, two, normed, acc, before if begun else None)
     if spare:
         out[...] = acc[...].astype(out.dtype)
 
@@ -259,8 +266,8 @@
 
     theirs = go(normed, swap)
     whole = lambda *arrays: [(w, (0, w.shape[1])) for w in arrays]
-    early = whole(q0, q1, a_most, a1, y0, y1) + [(ya_most, (0, tall))]
-    late = [(ya_most, (tall, tall + cut))] + whole(ay1, aa0, aa1, *late)
+    early = whole(q0, q1, a_most, a1, y0, y1, ya_most, ay1)
+    late = whole(aa0, aa1, *late)
     own_sum = mlp("own", normed, stream, True, early, rows_f32)
     their_sum = mlp("their", theirs, own_sum, False, early, rows_f32)
     partial = go(mlp("their_late", theirs, their_sum, True, late, rows_bf), swap)

time: 169 us -> 167 us (0.988)
  starting transfers between devices: 52.7 us -> 50.5 us
    ppermute x12, starting transfers between devices: 21.9 us -> 19.8 us  [local(): go = lambda x, pairs: lax.ppermute(x, BOTH, pairs)]
where the time goes in v4:
time: 167 us; the launch traced here: 166 us
  waiting for transfers between devices  57.1 us (34%)
  starting transfers between devices  50.5 us (30%)
  Pallas kernels  29.6 us (18%)
  blocking collectives  17.9 us (11%)
  local copies, waits for them, and re-layouts  5.96 us (4%)
  other arithmetic  5.16 us (3%)
    ppermute x12, waiting for transfers between devices, local(): go = lambda x, pairs: lax.ppermute(x, BOTH, pairs)  48.2 us
    pallas_call x4, Pallas kernels, mlp(): pl.pallas_call(functools.partial(mlp_kernel, spans, begun), out_shape=out...  20.9 us
    ppermute x12, starting transfers between devices, local(): go = lambda x, pairs: lax.ppermute(x, BOTH, pairs)  19.8 us
    all_to_all x1, blocking collectives, local(): out = lax.all_to_all(done, 'chan', 0, 0, tiled=True)  17.9 us
    all_to_all x1, starting transfers between devices, local(): lax.all_to_all(f1.reshape(n_seq * n_chan, r_own, own), BOTH, 0, 0, tiled=...  14 us
    all_to_all x1, starting transfers between devices, local(): lax.all_to_all(f3, BOTH, 0, 0, tiled=True)  10.8 us
    all_to_all x1, waiting for transfers between devices, local(): lax.all_to_all(tokens.reshape(n_chan, inner, own), 'chan', 0, 0, tiled=True)  8.97 us
    all_to_all x1, starting transfers between devices, local(): lax.all_to_all(tokens.reshape(n_chan, inner, own), 'chan', 0, 0, tiled=True)  5.99 us
  transfers between devices with their start and end apart: 15, of which 5 were waited for; matrix products, arithmetic and copies ran while one was open for 5% of the time, Pallas kernels for 15%

profile of v4, /device:TPU:1, one launch (start us, length us, event | category | flops | bytes accessed | tf_op | source)
XLA Modules:
  0.0 166.5 jit_solution(11027479202957624605)
XLA Ops:
  0.0 6.0 %all-to-all-start = ((bf16[8,512,128]{2,1,0:T(8,128)(2,1)}), bf16[8,512,128]{2,1,0:T(8,128)(2,1)S(1)}, u32[]{:S(2)}, u32[]{:S(2)}) async-start(bf16[8,512,128]{2,1,0:T(8,128)(2,1)} %bitcast.20), calls=%async_computation | async-start | bytes 2097152 | tf_op jit(solution)/shard_map/all_to_all | solution.py:189
  6.0 1.4 constant_dynamic-slice_fusion.1
  7.4 0.0 copy-done.16
  7.4 0.2 copy-done.17
  7.5 0.1 constant_dynamic-slice_fusion.4
  7.7 1.0 fusion
  8.7 4.1 %maximum_bitcast_fusion = bf16[1,2304,512]{2,1,0:T(8,128)(2,1)} fusion(bf16[768,512]{1,0:T(8,128)(2,1)S(1)} %get-tuple-element.28, bf16[256,512]{1,0:T(8,128)(2,1)S(1)} %get-tuple-element.32, bf16[256,512]{1,0:T(8,128)(2,1)S(1)} %get-tuple-element.30, bf16[1024,256]{1,0:T(8,128)(2,1)S(1)} %get-tuple-element.35, bf16[1024,256]{1,0:T(8,128)(2,1)S(1)} %get-tuple-element.38), kind=kLoop, calls=%fused_computation | loop fusion | flops 11796480 | bytes 4718592 | tf_op jit(solution)/shard_map/broadcast_in_dim | solution.py:200
  12.8 9.0 %all-to-all-done.tok = bf16[8,512,128]{2,1,0:T(8,128)(2,1)S(1)} async-done(((bf16[8,512,128]{2,1,0:T(8,128)(2,1)}), bf16[8,512,128]{2,1,0:T(8,128)(2,1)S(1)}, u32[]{:S(2)}, u32[]{:S(2)}) %all-to-all-start) | async-done | bytes 1048608 | tf_op jit(solution)/shard_map/all_to_all | solution.py:189
  21.8 0.6 collective-permute-start
  22.4 0.3 copy-done
  22.8 3.7 %first.1 = bf16[32,8,16,128]{3,2,1,0:T(8,128)(2,1)} custom-call(s32[1]{0:T(128)} %bitcast.place, bf16[8,512,128]{2,1,0:T(8,128)(2,1)} %copy-done, bf16[512,512]{1,0:T(8,128)(2,1)} %right.1, f32[8,512]{1,0:T(8,128)} %tw.2), custom_call_target="tpu_custom_call" | custom-call | flops 1 | bytes 1 | tf_op jit(solution)/shard_map/first/pallas_call | solution.py:207
  26.5 14.0 %all-to-all-start.1 = ((bf16[256,16,128]{2,1,0:T(8,128)(2,1)}), bf16[256,16,128]{2,1,0:T(8,128)(2,1)S(1)}, u32[]{:S(2)}, u32[]{:S(2)}) async-start(bf16[256,16,128]{2,1,0:T(8,128)(2,1)} %bitcast.18), calls=%async_computation.1 | async-start | bytes 2097152 | tf_op jit(solution)/shard_map/all_to_all | solution.py:216
  40.5 2.7 %collective-permute-start.1 = (bf16[1,768,512]{2,1,0:T(8,128)(2,1)}, bf16[1,768,512]{2,1,0:T(8,128)(2,1)S(1)}, u32[]{:S(2)}, u32[]{:S(2)}) collective-permute-start(bf16[1,768,512]{2,1,0:T(8,128)(2,1)} %get-tuple-element.17.rest_1_), channel_id=1, source_target_pairs={{0,1},{1,2},{2,3},{3,0},{4,5},{5,6},{6,7},{7,4},{8,11},{9,8},{10,9... | collective-permute-start | bytes 2359304 | tf_op jit(solution)/shard_map/ppermute | solution.py:204
  43.1 2.5 %collective-permute-start.2 = (bf16[1,768,512]{2,1,0:T(8,128)(2,1)S(1)}, bf16[1,768,512]{2,1,0:T(8,128)(2,1)S(1)}, u32[]{:S(2)}, u32[]{:S(2)}) collective-permute-start(bf16[1,768,512]{2,1,0:T(8,128)(2,1)S(1)} %bitcast.13), channel_id=1, source_target_pairs={{0,4},{1,5},{2,6},{3,7},{4,128},{5,129},{6,130},{7,131},{8,140},{9... | collective-permute-start | bytes 2359304 | tf_op jit(solution)/shard_map/ppermute | solution.py:204
  45.6 0.5 collective-permute-start.3
  46.1 23.6 %collective-permute-done.1.rest_3_ = bf16[1,768,512]{2,1,0:T(8,128)(2,1)S(1)} collective-permute-done((bf16[1,768,512]{2,1,0:T(8,128)(2,1)}, bf16[1,768,512]{2,1,0:T(8,128)(2,1)S(1)}, u32[]{:S(2)}, u32[]{:S(2)}) %collective-permute-start.1) | collective-permute-done | bytes 786464 | tf_op jit(solution)/shard_map/ppermute | solution.py:204
  69.8 0.0 collective-permute-done.2.rest_4_
  69.8 0.9 copy-done.12
  70.7 0.9 copy-done.14
  71.5 1.2 collective-permute-done.3.rest_5_
  72.7 0.0 all-to-all-done.1.col
  72.7 0.0 collective-permute-done.rest_2_
  72.7 2.8 %collective-permute-start.4 = (bf16[1,2304,512]{2,1,0:T(8,128)(2,1)}, bf16[1,2304,512]{2,1,0:T(8,128)(2,1)}, u32[]{:S(2)}, u32[]{:S(2)}) collective-permute-start(bf16[1,2304,512]{2,1,0:T(8,128)(2,1)} %collective-permute-done.rest_2_), channel_id=1, source_target_pairs={{0,4},{1,5},{2,6},{3,7},{4,128},{5,129},{6,130},{7,131},{8,140},{9... | collective-permute-start | bytes 7077896 | tf_op jit(solution)/shard_map/ppermute | solution.py:204
  75.6 0.0 copy-done.2
  75.6 0.0 copy-done.5
  75.6 0.0 copy-done.6
  75.6 0.0 copy-done.9
  75.6 3.2 %middle.1 = bf16[256,16,128]{2,1,0:T(8,128)(2,1)} custom-call(bf16[256,16,128]{2,1,0:T(8,128)(2,1)S(1)} %all-to-all-done.1.col, bf16[256,256]{1,0:T(8,128)(2,1)S(1)} %copy-done.5, bf16[256,256]{1,0:T(8,128)(2,1)S(1)} %copy-done.6, bf16[256,16,128]{2,1,0:T(8,128)(2,1)S(1)} %copy-done.2, f32[1,128]{1,0:T(1,128)S(1)} %bitcast.17), custom_call_target="tpu_custom_call" | custom-call | flops 1 | bytes 1 | tf_op jit(solution)/shard_map/middle/pallas_call | solution.py:220
  78.8 10.8 %all-to-all-start.2 = ((bf16[256,16,128]{2,1,0:T(8,128)(2,1)}), bf16[256,16,128]{2,1,0:T(8,128)(2,1)S(1)}, u32[]{:S(2)}, u32[]{:S(2)}) async-start(bf16[256,16,128]{2,1,0:T(8,128)(2,1)} %middle.1), calls=%async_computation.2 | async-start | bytes 2097152 | tf_op jit(solution)/shard_map/all_to_all | solution.py:230
  89.7 1.2 slice.28
  90.8 2.7 %collective-permute-start.6 = (bf16[1,768,512]{2,1,0:T(8,128)(2,1)S(1)}, bf16[1,768,512]{2,1,0:T(8,128)(2,1)}, u32[]{:S(2)}, u32[]{:S(2)}) collective-permute-start(bf16[1,768,512]{2,1,0:T(8,128)(2,1)S(1)} %slice.28), channel_id=1, source_target_pairs={{0,1},{1,2},{2,3},{3,0},{4,5},{5,6},{6,7},{7,4},{8,11},{9,8},{10,9... | collective-permute-start | bytes 2359304 | tf_op jit(solution)/shard_map/ppermute | solution.py:204
  93.5 0.6 collective-permute-start.5
  94.1 0.3 collective-permute-start.7
  94.4 14.5 %collective-permute-done.6.rest_0_ = bf16[1,768,512]{2,1,0:T(8,128)(2,1)} collective-permute-done((bf16[1,768,512]{2,1,0:T(8,128)(2,1)S(1)}, bf16[1,768,512]{2,1,0:T(8,128)(2,1)}, u32[]{:S(2)}, u32[]{:S(2)}) %collective-permute-start.6) | collective-permute-done | bytes 786464 | tf_op jit(solution)/shard_map/ppermute | solution.py:204
  108.9 2.3 %collective-permute-start.8 = (bf16[1,768,512]{2,1,0:T(8,128)(2,1)}, bf16[1,768,512]{2,1,0:T(8,128)(2,1)}, u32[]{:S(2)}, u32[]{:S(2)}) collective-permute-start(bf16[1,768,512]{2,1,0:T(8,128)(2,1)} %collective-permute-done.6.rest_0_), channel_id=1, source_target_pairs={{0,4},{1,5},{2,6},{3,7},{4,128},{5,129},{6,130},{7,131},{8,140},{9... | collective-permute-start | bytes 2359304 | tf_op jit(solution)/shard_map/ppermute | solution.py:204
  111.2 8.8 %collective-permute-done.5.rest_7_ = bf16[1,768,512]{2,1,0:T(8,128)(2,1)} collective-permute-done((bf16[1,768,512]{2,1,0:T(8,128)(2,1)}, bf16[1,768,512]{2,1,0:T(8,128)(2,1)}, u32[]{:S(2)}, u32[]{:S(2)}) %collective-permute-start.5) | collective-permute-done | bytes 786464 | tf_op jit(solution)/shard_map/ppermute | solution.py:204
  120.0 3.3 %collective-permute-start.9 = (bf16[1,768,512]{2,1,0:T(8,128)(2,1)}, bf16[1,768,512]{2,1,0:T(8,128)(2,1)}, u32[]{:S(2)}, u32[]{:S(2)}) collective-permute-start(bf16[1,768,512]{2,1,0:T(8,128)(2,1)} %collective-permute-done.5.rest_7_), channel_id=1, source_target_pairs={{0,1},{1,2},{2,3},{3,0},{4,5},{5,6},{6,7},{7,4},{8,11},{9,8},{10,9... | collective-permute-start | bytes 2359304 | tf_op jit(solution)/shard_map/ppermute | solution.py:204
  123.3 0.0 all-to-all-done.2
  123.4 0.0 copy-done.1
  123.4 0.0 copy-done.4
  123.4 0.0 copy-done.7
  123.4 0.0 copy-done.8
  123.4 1.4 third.1
  124.8 0.0 copy-start.10
  124.8 0.4 collective-permute-start.10
  125.2 0.0 collective-permute-done.4.rest_6_
  125.2 0.0 copy-done.3
  125.2 0.0 copy-done.13
  125.2 0.0 copy-done.15
  125.3 7.0 %own.1.before = f32[512,1024]{1,0:T(8,128)S(1)} custom-call(bf16[512,1024]{1,0:T(8,128)(2,1)S(1)} %get-tuple-element.21.normed, bf16[512,1024]{1,0:T(8,128)(2,1)S(1)} %get-tuple-element.22.before, bf16[1,768,512]{2,1,0:T(8,128)(2,1)S(1)} %bitcast.14, bf16[1,768,512]{2,1,0:T(8,128)(2,1)S(1)} %copy-done.3, bf16[1,2304,512]{2,1,0:T(8,128)(2,1)} %collective-permute-done.rest_2_, ...), custom_call_target="tpu_custom_call" | custom-call | flops 99999997952 | bytes 1 | tf_op jit(solution)/shard_map/own/pallas_call | solution.py:250
  132.2 0.0 copy-done.10
  132.2 0.0 collective-permute-done.10.normed
  132.2 7.0 %their.1.before = f32[512,1024]{1,0:T(8,128)S(1)} custom-call(bf16[512,1024]{1,0:T(8,128)(2,1)S(1)} %collective-permute-done.10.normed, f32[512,1024]{1,0:T(8,128)S(1)} %own.1.before, bf16[1,768,512]{2,1,0:T(8,128)(2,1)S(1)} %bitcast.15, bf16[1,768,512]{2,1,0:T(8,128)(2,1)S(1)} %copy-done.3, bf16[1,2304,512]{2,1,0:T(8,128)(2,1)} %collective-permute-done.rest_2_, ...), custom_call_target="tpu_custom_call" | custom-call | flops 99999997952 | bytes 1 | tf_op jit(solution)/shard_map/their/pallas_call | solution.py:250
  139.2 0.0 copy-start.11
  139.2 0.0 collective-permute-done.7.rest_1_
  139.2 0.0 collective-permute-done.8.rest_2_
  139.2 0.0 collective-permute-done.9.rest_3_
  139.3 3.6 %their_late.1 = bf16[512,1024]{1,0:T(8,128)(2,1)S(1)} custom-call(bf16[512,1024]{1,0:T(8,128)(2,1)S(1)} %collective-permute-done.10.normed, f32[512,1024]{1,0:T(8,128)S(1)} %their.1.before, bf16[1,768,512]{2,1,0:T(8,128)(2,1)} %collective-permute-done.6.rest_0_, bf16[1,768,512]{2,1,0:T(8,128)(2,1)} %collective-permute-done.7.rest_1_, ...), custom_call_target="tpu_custom_call" | custom-call | flops 99999997952 | bytes 1 | tf_op jit(solution)/shard_map/their_late/pallas_call | solution.py:250
  142.8 1.0 collective-permute-start.11
  143.8 3.5 %own_late.1.a = f32[512,1024]{1,0:T(8,128)S(1)} custom-call(bf16[512,1024]{1,0:T(8,128)(2,1)S(1)} %copy-done.11, f32[512,1024]{1,0:T(8,128)S(1)} %own.1.before, bf16[1,768,512]{2,1,0:T(8,128)(2,1)} %collective-permute-done.6.rest_0_, bf16[1,768,512]{2,1,0:T(8,128)(2,1)} %collective-permute-done.7.rest_1_, ...), custom_call_target="tpu_custom_call" | custom-call | flops 99999997952 | bytes 1 | tf_op jit(solution)/shard_map/own_late/pallas_call | solution.py:250
  147.3 0.0 collective-permute-done.11.b
  147.3 0.3 sum.1
  147.6 17.9 %all_to_all.20 = bf16[8,512,128]{2,1,0:T(8,128)(2,1)S(1)} all-to-all(bf16[8,512,128]{2,1,0:T(8,128)(2,1)S(1)} %sum.1), channel_id=1, replica_groups=mesh['seq'=32,'chan'=8] {'chan'}, dimensions={0} | all-to-all | bytes 2097152 | tf_op jit(solution)/shard_map/all_to_all | solution.py:283
  165.5 1.0 copy.15
  (17 shorter events, 0.0 us)
Async XLA Ops:
  0.0 7.4 %copy-start.16 = (bf16[1024,512]{1,0:T(8,128)(2,1)S(1)}, bf16[1024,512]{1,0:T(8,128)(2,1)}, u32[]{:S(2)}) copy-start(bf16[1024,512]{1,0:T(8,128)(2,1)} %param.24) | copy-start | bytes 3145732
  0.0 21.8 %all-to-all-start = ((bf16[8,512,128]{2,1,0:T(8,128)(2,1)}), bf16[8,512,128]{2,1,0:T(8,128)(2,1)S(1)}, u32[]{:S(2)}, u32[]{:S(2)}) async-start(bf16[8,512,128]{2,1,0:T(8,128)(2,1)} %bitcast.20), calls=%async_computation | async-start | bytes 2097152 | tf_op jit(solution)/shard_map/all_to_all | solution.py:189
  6.0 1.5 copy-start.17
  21.8 1.0 copy-start
  21.8 50.9 %collective-permute-start = (bf16[1,2304,512]{2,1,0:T(8,128)(2,1)}, bf16[1,2304,512]{2,1,0:T(8,128)(2,1)}, u32[]{:S(2)}, u32[]{:S(2)}) collective-permute-start(bf16[1,2304,512]{2,1,0:T(8,128)(2,1)} %maximum_bitcast_fusion), channel_id=1, source_target_pairs={{0,1},{1,2},{2,3},{3,0},{4,5},{5,6},{6,7},{7,4},{8,11},{9,8},{10,9... | collective-permute-start | bytes 7077896 | tf_op jit(solution)/shard_map/ppermute | solution.py:204
  22.8 52.8 %copy-start.2 = (bf16[256,16,128]{2,1,0:T(8,128)(2,1)S(1)}, bf16[256,16,128]{2,1,0:T(8,128)(2,1)}, u32[]{:S(2)}) copy-start(bf16[256,16,128]{2,1,0:T(8,128)(2,1)} %kern.1) | copy-start | bytes 3145732
  22.8 52.8 %copy-start.5 = (bf16[256,256]{1,0:T(8,128)(2,1)S(1)}, bf16[256,256]{1,0:T(8,128)(2,1)}, u32[]{:S(2)}) copy-start(bf16[256,256]{1,0:T(8,128)(2,1)} %left_in.1) | copy-start | bytes 393220
  22.8 52.8 %copy-start.6 = (bf16[256,256]{1,0:T(8,128)(2,1)S(1)}, bf16[256,256]{1,0:T(8,128)(2,1)}, u32[]{:S(2)}) copy-start(bf16[256,256]{1,0:T(8,128)(2,1)} %left_out.1) | copy-start | bytes 393220
  22.8 52.8 %copy-start.9 = (f32[128]{0:T(128)S(1)}, f32[128]{0:T(128)}, u32[]{:S(2)}) copy-start(f32[128]{0:T(128)} %param.14) | copy-start | bytes 1540
  26.5 46.2 %all-to-all-start.1 = ((bf16[256,16,128]{2,1,0:T(8,128)(2,1)}), bf16[256,16,128]{2,1,0:T(8,128)(2,1)S(1)}, u32[]{:S(2)}, u32[]{:S(2)}) async-start(bf16[256,16,128]{2,1,0:T(8,128)(2,1)} %bitcast.18), calls=%async_computation.1 | async-start | bytes 2097152 | tf_op jit(solution)/shard_map/all_to_all | solution.py:216
  40.5 29.3 %collective-permute-start.1 = (bf16[1,768,512]{2,1,0:T(8,128)(2,1)}, bf16[1,768,512]{2,1,0:T(8,128)(2,1)S(1)}, u32[]{:S(2)}, u32[]{:S(2)}) collective-permute-start(bf16[1,768,512]{2,1,0:T(8,128)(2,1)} %get-tuple-element.17.rest_1_), channel_id=1, source_target_pairs={{0,1},{1,2},{2,3},{3,0},{4,5},{5,6},{6,7},{7,4},{8,11},{9,8},{10,9... | collective-permute-start | bytes 2359304 | tf_op jit(solution)/shard_map/ppermute | solution.py:204
  43.1 26.7 %collective-permute-start.2 = (bf16[1,768,512]{2,1,0:T(8,128)(2,1)S(1)}, bf16[1,768,512]{2,1,0:T(8,128)(2,1)S(1)}, u32[]{:S(2)}, u32[]{:S(2)}) collective-permute-start(bf16[1,768,512]{2,1,0:T(8,128)(2,1)S(1)} %bitcast.13), channel_id=1, source_target_pairs={{0,4},{1,5},{2,6},{3,7},{4,128},{5,129},{6,130},{7,131},{8,140},{9... | collective-permute-start | bytes 2359304 | tf_op jit(solution)/shard_map/ppermute | solution.py:204
  45.6 27.1 %collective-permute-start.3 = (bf16[1,768,512]{2,1,0:T(8,128)(2,1)}, bf16[1,768,512]{2,1,0:T(8,128)(2,1)}, u32[]{:S(2)}, u32[]{:S(2)}) collective-permute-start(bf16[1,768,512]{2,1,0:T(8,128)(2,1)} %get-tuple-element.17.rest_1_), channel_id=1, source_target_pairs={{0,4},{1,5},{2,6},{3,7},{4,128},{5,129},{6,130},{7,131},{8,140},{9... | collective-permute-start | bytes 2359304 | tf_op jit(solution)/shard_map/ppermute | solution.py:204
  69.8 0.9 copy-start.12
  70.7 0.9 copy-start.14
  72.7 52.5 %collective-permute-start.4 = (bf16[1,2304,512]{2,1,0:T(8,128)(2,1)}, bf16[1,2304,512]{2,1,0:T(8,128)(2,1)}, u32[]{:S(2)}, u32[]{:S(2)}) collective-permute-start(bf16[1,2304,512]{2,1,0:T(8,128)(2,1)} %collective-permute-done.rest_2_), channel_id=1, source_target_pairs={{0,4},{1,5},{2,6},{3,7},{4,128},{5,129},{6,130},{7,131},{8,140},{9... | collective-permute-start | bytes 7077896 | tf_op jit(solution)/shard_map/ppermute | solution.py:204
  78.8 44.6 %copy-start.1 = (bf16[8,512,128]{2,1,0:T(8,128)(2,1)S(1)}, bf16[8,512,128]{2,1,0:T(8,128)(2,1)}, u32[]{:S(2)}) copy-start(bf16[8,512,128]{2,1,0:T(8,128)(2,1)} %copy-done) | copy-start | bytes 3145732
  78.8 44.6 %copy-start.4 = (bf16[512,512]{1,0:T(8,128)(2,1)S(1)}, bf16[512,512]{1,0:T(8,128)(2,1)}, u32[]{:S(2)}) copy-start(bf16[512,512]{1,0:T(8,128)(2,1)} %right_hbm.1) | copy-start | bytes 1572868
  78.8 44.6 %copy-start.7 = (f32[8,512]{1,0:T(8,128)S(1)}, f32[8,512]{1,0:T(8,128)}, u32[]{:S(2)}) copy-start(f32[8,512]{1,0:T(8,128)} %tw.3) | copy-start | bytes 49156
  78.8 44.6 %copy-start.8 = (f32[1024]{0:T(1024)S(1)}, f32[1024]{0:T(1024)}, u32[]{:S(2)}) copy-start(f32[1024]{0:T(1024)} %param.22) | copy-start | bytes 12292
  78.8 44.5 %all-to-all-start.2 = ((bf16[256,16,128]{2,1,0:T(8,128)(2,1)}), bf16[256,16,128]{2,1,0:T(8,128)(2,1)S(1)}, u32[]{:S(2)}, u32[]{:S(2)}) async-start(bf16[256,16,128]{2,1,0:T(8,128)(2,1)} %middle.1), calls=%async_computation.2 | async-start | bytes 2097152 | tf_op jit(solution)/shard_map/all_to_all | solution.py:230
  90.8 18.1 %collective-permute-start.6 = (bf16[1,768,512]{2,1,0:T(8,128)(2,1)S(1)}, bf16[1,768,512]{2,1,0:T(8,128)(2,1)}, u32[]{:S(2)}, u32[]{:S(2)}) collective-permute-start(bf16[1,768,512]{2,1,0:T(8,128)(2,1)S(1)} %slice.28), channel_id=1, source_target_pairs={{0,1},{1,2},{2,3},{3,0},{4,5},{5,6},{6,7},{7,4},{8,11},{9,8},{10,9... | collective-permute-start | bytes 2359304 | tf_op jit(solution)/shard_map/ppermute | solution.py:204
  93.5 26.5 %collective-permute-start.5 = (bf16[1,768,512]{2,1,0:T(8,128)(2,1)}, bf16[1,768,512]{2,1,0:T(8,128)(2,1)}, u32[]{:S(2)}, u32[]{:S(2)}) collective-permute-start(bf16[1,768,512]{2,1,0:T(8,128)(2,1)} %collective-permute-done.3.rest_5_), channel_id=1, source_target_pairs={{0,1},{1,2},{2,3},{3,0},{4,5},{5,6},{6,7},{7,4},{8,11},{9,8},{10,9... | collective-permute-start | bytes 2359304 | tf_op jit(solution)/shard_map/ppermute | solution.py:204
  94.1 45.1 %collective-permute-start.7 = (bf16[1,768,512]{2,1,0:T(8,128)(2,1)}, bf16[1,768,512]{2,1,0:T(8,128)(2,1)}, u32[]{:S(2)}, u32[]{:S(2)}) collective-permute-start(bf16[1,768,512]{2,1,0:T(8,128)(2,1)} %copy-done.12), channel_id=1, source_target_pairs={{0,1},{1,2},{2,3},{3,0},{4,5},{5,6},{6,7},{7,4},{8,11},{9,8},{10,9... | collective-permute-start | bytes 2359304 | tf_op jit(solution)/shard_map/ppermute | solution.py:204
  108.9 30.3 %collective-permute-start.8 = (bf16[1,768,512]{2,1,0:T(8,128)(2,1)}, bf16[1,768,512]{2,1,0:T(8,128)(2,1)}, u32[]{:S(2)}, u32[]{:S(2)}) collective-permute-start(bf16[1,768,512]{2,1,0:T(8,128)(2,1)} %collective-permute-done.6.rest_0_), channel_id=1, source_target_pairs={{0,4},{1,5},{2,6},{3,7},{4,128},{5,129},{6,130},{7,131},{8,140},{9... | collective-permute-start | bytes 2359304 | tf_op jit(solution)/shard_map/ppermute | solution.py:204
  120.0 19.2 %collective-permute-start.9 = (bf16[1,768,512]{2,1,0:T(8,128)(2,1)}, bf16[1,768,512]{2,1,0:T(8,128)(2,1)}, u32[]{:S(2)}, u32[]{:S(2)}) collective-permute-start(bf16[1,768,512]{2,1,0:T(8,128)(2,1)} %collective-permute-done.5.rest_7_), channel_id=1, source_target_pairs={{0,1},{1,2},{2,3},{3,0},{4,5},{5,6},{6,7},{7,4},{8,11},{9,8},{10,9... | collective-permute-start | bytes 2359304 | tf_op jit(solution)/shard_map/ppermute | solution.py:204
  123.3 1.9 %copy-start.3 = (bf16[1,768,512]{2,1,0:T(8,128)(2,1)S(1)}, bf16[1,768,512]{2,1,0:T(8,128)(2,1)}, u32[]{:S(2)}) copy-start(bf16[1,768,512]{2,1,0:T(8,128)(2,1)} %get-tuple-element.17.rest_1_) | copy-start | bytes 2359300
  123.4 1.9 %copy-start.13 = (bf16[1,768,512]{2,1,0:T(8,128)(2,1)S(1)}, bf16[1,768,512]{2,1,0:T(8,128)(2,1)}, u32[]{:S(2)}) copy-start(bf16[1,768,512]{2,1,0:T(8,128)(2,1)} %copy-done.12) | copy-start | bytes 2359300
  123.4 1.9 %copy-start.15 = (bf16[1,768,512]{2,1,0:T(8,128)(2,1)S(1)}, bf16[1,768,512]{2,1,0:T(8,128)(2,1)}, u32[]{:S(2)}) copy-start(bf16[1,768,512]{2,1,0:T(8,128)(2,1)} %copy-done.14) | copy-start | bytes 2359300
  124.8 7.4 %copy-start.10 = (bf16[512,1024]{1,0:T(8,128)(2,1)}, bf16[512,1024]{1,0:T(8,128)(2,1)S(1)}, u32[]{:S(2)}) copy-start(bf16[512,1024]{1,0:T(8,128)(2,1)S(1)} %get-tuple-element.21.normed) | copy-start | bytes 3145732
  124.8 7.4 %collective-permute-start.10 = (bf16[512,1024]{1,0:T(8,128)(2,1)S(1)}, bf16[512,1024]{1,0:T(8,128)(2,1)S(1)}, u32[]{:S(2)}, u32[]{:S(2)}) collective-permute-start(bf16[512,1024]{1,0:T(8,128)(2,1)S(1)} %get-tuple-element.21.normed), channel_id=1, source_target_pairs={{0,8},{1,9},{2,10},{3,11},{4,12},{5,13},{6,14},{7,15},{8,0},{9,1},... | collective-permute-start | bytes 3145736 | tf_op jit(solution)/shard_map/ppermute | solution.py:204
  139.2 4.6 %copy-start.11 = (bf16[512,1024]{1,0:T(8,128)(2,1)S(1)}, bf16[512,1024]{1,0:T(8,128)(2,1)}, u32[]{:S(2)}) copy-start(bf16[512,1024]{1,0:T(8,128)(2,1)} %copy-done.10) | copy-start | bytes 3145732
  142.8 4.5 %collective-permute-start.11 = (bf16[512,1024]{1,0:T(8,128)(2,1)S(1)}, bf16[512,1024]{1,0:T(8,128)(2,1)S(1)}, u32[]{:S(2)}, u32[]{:S(2)}) collective-permute-start(bf16[512,1024]{1,0:T(8,128)(2,1)S(1)} %their_late.1), channel_id=1, source_target_pairs={{0,8},{1,9},{2,10},{3,11},{4,12},{5,13},{6,14},{7,15},{8,0},{9,1},... | collective-permute-start | bytes 3145736 | tf_op jit(solution)/shard_map/ppermute | solution.py:204

commit v5 on v4

--- a/solution.py
+++ b/solution.py
@@ -214,7 +214,7 @@
         name="first",
     )(place, tok, right_in, twiddle_in)
     col = lax.all_to_all(f1.reshape(n_seq * n_chan, r_own, own), BOTH, 0, 0, tiled=True)
-    a_most, a1, y0, y1, col = lax.optimization_barrier((a_most, a1, y0, y1, col))
+    a_most, col = lax.optimization_barrier((a_most, col))
     ya_most, ay1 = go(a_most, yy), go(y1, fwd)
     aa0, aa1 = go(a_most[:, tall:], fwd), go(a1, fwd)
     f3 = pl.pallas_call(

time: 167 us -> 188 us (1.13)
  blocking collectives: 17.9 us -> 62.3 us
  starting transfers between devices: 50.5 us -> 36.5 us
  waiting for transfers between devices: 57.1 us -> 49.7 us
    all_to_all x0 -> x1, blocking collectives: none -> 44 us  [local(): lax.all_to_all(f1.reshape(n_seq * n_chan, r_own, own), BOTH, 0, 0, tiled=...]
    all_to_all x1 -> x0, starting transfers between devices: 14 us -> none  [local(): lax.all_to_all(f1.reshape(n_seq * n_chan, r_own, own), BOTH, 0, 0, tiled=...]
    ppermute x12, waiting for transfers between devices: 48.2 us -> 40.7 us  [local(): go = lambda x, pairs: lax.ppermute(x, BOTH, pairs)]
    all_to_all x1, starting transfers between devices: 10.8 us -> 6.25 us  [local(): lax.all_to_all(f3, BOTH, 0, 0, tiled=True)]
    ppermute x12, starting transfers between devices: 19.8 us -> 24.3 us  [local(): go = lambda x, pairs: lax.ppermute(x, BOTH, pairs)]
  transfers between devices with their start and end apart: 15 -> 14, of which waited for: 5 -> 4; matrix products, arithmetic and copies ran while one was open for 5% -> 4% of each run, Pallas kernels for 15% -> 14%
where the time goes in v5:
time: 188 us
  blocking collectives  62.3 us (33%)
  waiting for transfers between devices  49.7 us (26%)
  starting transfers between devices  36.5 us (19%)
  Pallas kernels  29.5 us (16%)
  other arithmetic  5.17 us (3%)
  local copies, waits for them, and re-layouts  4.21 us (2%)
    all_to_all x1, blocking collectives, local(): lax.all_to_all(f1.reshape(n_seq * n_chan, r_own, own), BOTH, 0, 0, tiled=...  44 us
    ppermute x12, waiting for transfers between devices, local(): go = lambda x, pairs: lax.ppermute(x, BOTH, pairs)  40.7 us
    ppermute x12, starting transfers between devices, local(): go = lambda x, pairs: lax.ppermute(x, BOTH, pairs)  24.3 us
    pallas_call x4, Pallas kernels, mlp(): pl.pallas_call(functools.partial(mlp_kernel, spans, begun), out_shape=out...  20.9 us
    all_to_all x1, blocking collectives, local(): out = lax.all_to_all(done, 'chan', 0, 0, tiled=True)  18.4 us
    all_to_all x1, waiting for transfers between devices, local(): lax.all_to_all(tokens.reshape(n_chan, inner, own), 'chan', 0, 0, tiled=True)  8.97 us
    all_to_all x1, starting transfers between devices, local(): lax.all_to_all(f3, BOTH, 0, 0, tiled=True)  6.25 us
    all_to_all x1, starting transfers between devices, local(): lax.all_to_all(tokens.reshape(n_chan, inner, own), 'chan', 0, 0, tiled=True)  5.99 us
  transfers between devices with their start and end apart: 14, of which 4 were waited for; matrix products, arithmetic and copies ran while one was open for 4% of the time, Pallas kernels for 14%

profile of v5, /device:TPU:1, one launch (start us, length us, event | category | flops | bytes accessed | tf_op | source)
XLA Modules:
  0.0 187.7 jit_solution(2969091005311693226)
XLA Ops:
  0.0 0.0 copy-start.14
  0.0 6.0 %all-to-all-start = ((bf16[8,512,128]{2,1,0:T(8,128)(2,1)}), bf16[8,512,128]{2,1,0:T(8,128)(2,1)S(1)}, u32[]{:S(2)}, u32[]{:S(2)}) async-start(bf16[8,512,128]{2,1,0:T(8,128)(2,1)} %bitcast.20), calls=%async_computation | async-start | bytes 2097152 | tf_op jit(solution)/shard_map/all_to_all | solution.py:189
  6.0 0.0 copy-start.15
  6.0 1.4 constant_dynamic-slice_fusion.1
  7.4 0.0 copy-done.14
  7.4 0.2 copy-done.15
  7.5 0.1 constant_dynamic-slice_fusion.4
  7.7 1.0 fusion
  8.7 4.2 %maximum_bitcast_fusion = bf16[1,2304,512]{2,1,0:T(8,128)(2,1)} fusion(bf16[768,512]{1,0:T(8,128)(2,1)S(1)} %get-tuple-element.22, bf16[256,512]{1,0:T(8,128)(2,1)S(1)} %get-tuple-element.26, bf16[256,512]{1,0:T(8,128)(2,1)S(1)} %get-tuple-element.24, bf16[1024,256]{1,0:T(8,128)(2,1)S(1)} %get-tuple-element.29, bf16[1024,256]{1,0:T(8,128)(2,1)S(1)} %get-tuple-element.32), kind=kLoop, calls=%fused_computation | loop fusion | flops 11796480 | bytes 4718592 | tf_op jit(solution)/shard_map/broadcast_in_dim | solution.py:200
  12.8 9.0 %all-to-all-done.tok = bf16[8,512,128]{2,1,0:T(8,128)(2,1)S(1)} async-done(((bf16[8,512,128]{2,1,0:T(8,128)(2,1)}), bf16[8,512,128]{2,1,0:T(8,128)(2,1)S(1)}, u32[]{:S(2)}, u32[]{:S(2)}) %all-to-all-start) | async-done | bytes 1048608 | tf_op jit(solution)/shard_map/all_to_all | solution.py:189
  21.8 0.6 collective-permute-start
  22.4 0.3 copy-done
  22.8 3.7 %first.1 = bf16[32,8,16,128]{3,2,1,0:T(8,128)(2,1)} custom-call(s32[1]{0:T(128)} %bitcast.place, bf16[8,512,128]{2,1,0:T(8,128)(2,1)} %copy-done, bf16[512,512]{1,0:T(8,128)(2,1)} %right.1, f32[8,512]{1,0:T(8,128)} %tw.2), custom_call_target="tpu_custom_call" | custom-call | flops 1 | bytes 1 | tf_op jit(solution)/shard_map/first/pallas_call | solution.py:207
  26.5 44.0 %all_to_all.20.col = bf16[256,16,128]{2,1,0:T(8,128)(2,1)S(1)} all-to-all(bf16[256,16,128]{2,1,0:T(8,128)(2,1)} %bitcast.19), channel_id=1, replica_groups=mesh['seq'=32,'chan'=8] {'seq','chan'}, dimensions={0} | all-to-all | bytes 2097152 | tf_op jit(solution)/shard_map/all_to_all | solution.py:216
  70.4 0.0 collective-permute-done.rest_2_
  70.4 3.0 %collective-permute-start.4 = (bf16[1,2304,512]{2,1,0:T(8,128)(2,1)}, bf16[1,2304,512]{2,1,0:T(8,128)(2,1)}, u32[]{:S(2)}, u32[]{:S(2)}) collective-permute-start(bf16[1,2304,512]{2,1,0:T(8,128)(2,1)} %collective-permute-done.rest_2_), channel_id=1, source_target_pairs={{0,4},{1,5},{2,6},{3,7},{4,128},{5,129},{6,130},{7,131},{8,140},{9... | collective-permute-start | bytes 7077896 | tf_op jit(solution)/shard_map/ppermute | solution.py:204
  73.4 0.0 copy-done.2
  73.4 0.0 copy-done.5
  73.4 0.0 copy-done.6
  73.4 0.0 copy-done.9
  73.4 3.2 %middle.1 = bf16[256,16,128]{2,1,0:T(8,128)(2,1)} custom-call(bf16[256,16,128]{2,1,0:T(8,128)(2,1)S(1)} %all_to_all.20.col, bf16[256,256]{1,0:T(8,128)(2,1)S(1)} %copy-done.5, bf16[256,256]{1,0:T(8,128)(2,1)S(1)} %copy-done.6, bf16[256,16,128]{2,1,0:T(8,128)(2,1)S(1)} %copy-done.2, f32[1,128]{1,0:T(1,128)S(1)} %bitcast.17), custom_call_target="tpu_custom_call" | custom-call | flops 1 | bytes 1 | tf_op jit(solution)/shard_map/middle/pallas_call | solution.py:220
  76.7 6.3 %all-to-all-start.2 = ((bf16[256,16,128]{2,1,0:T(8,128)(2,1)}), bf16[256,16,128]{2,1,0:T(8,128)(2,1)S(1)}, u32[]{:S(2)}, u32[]{:S(2)}) async-start(bf16[256,16,128]{2,1,0:T(8,128)(2,1)} %middle.1), calls=%async_computation.2 | async-start | bytes 2097152 | tf_op jit(solution)/shard_map/all_to_all | solution.py:230
  82.9 2.7 %collective-permute-start.3 = (bf16[1,768,512]{2,1,0:T(8,128)(2,1)}, bf16[1,768,512]{2,1,0:T(8,128)(2,1)S(1)}, u32[]{:S(2)}, u32[]{:S(2)}) collective-permute-start(bf16[1,768,512]{2,1,0:T(8,128)(2,1)} %get-tuple-element.19.rest_1_), channel_id=1, source_target_pairs={{0,4},{1,5},{2,6},{3,7},{4,128},{5,129},{6,130},{7,131},{8,140},{9... | collective-permute-start | bytes 2359304 | tf_op jit(solution)/shard_map/ppermute | solution.py:204
  85.7 2.4 %collective-permute-start.1 = (bf16[1,768,512]{2,1,0:T(8,128)(2,1)}, bf16[1,768,512]{2,1,0:T(8,128)(2,1)}, u32[]{:S(2)}, u32[]{:S(2)}) collective-permute-start(bf16[1,768,512]{2,1,0:T(8,128)(2,1)} %get-tuple-element.19.rest_1_), channel_id=1, source_target_pairs={{0,1},{1,2},{2,3},{3,0},{4,5},{5,6},{6,7},{7,4},{8,11},{9,8},{10,9... | collective-permute-start | bytes 2359304 | tf_op jit(solution)/shard_map/ppermute | solution.py:204
  88.1 31.1 %collective-permute-done.3.rest_5_ = bf16[1,768,512]{2,1,0:T(8,128)(2,1)S(1)} collective-permute-done((bf16[1,768,512]{2,1,0:T(8,128)(2,1)}, bf16[1,768,512]{2,1,0:T(8,128)(2,1)S(1)}, u32[]{:S(2)}, u32[]{:S(2)}) %collective-permute-start.3) | collective-permute-done | bytes 786464 | tf_op jit(solution)/shard_map/ppermute | solution.py:204
  119.2 2.2 %collective-permute-start.5 = (bf16[1,768,512]{2,1,0:T(8,128)(2,1)S(1)}, bf16[1,768,512]{2,1,0:T(8,128)(2,1)}, u32[]{:S(2)}, u32[]{:S(2)}) collective-permute-start(bf16[1,768,512]{2,1,0:T(8,128)(2,1)S(1)} %collective-permute-done.3.rest_5_), channel_id=1, source_target_pairs={{0,1},{1,2},{2,3},{3,0},{4,5},{5,6},{6,7},{7,4},{8,11},{9,8},{10,9... | collective-permute-start | bytes 2359304 | tf_op jit(solution)/shard_map/ppermute | solution.py:204
  121.4 1.2 slice.28
  122.6 0.4 collective-permute-start.6
  122.9 1.8 collective-permute-start.2
  124.7 0.0 collective-permute-done.1.rest_3_
  124.7 1.2 collective-permute-start.7
  125.9 4.6 %collective-permute-done.5.rest_7_ = bf16[1,768,512]{2,1,0:T(8,128)(2,1)} collective-permute-done((bf16[1,768,512]{2,1,0:T(8,128)(2,1)S(1)}, bf16[1,768,512]{2,1,0:T(8,128)(2,1)}, u32[]{:S(2)}, u32[]{:S(2)}) %collective-permute-start.5) | collective-permute-done | bytes 786464 | tf_op jit(solution)/shard_map/ppermute | solution.py:204
  130.4 3.4 %collective-permute-start.9 = (bf16[1,768,512]{2,1,0:T(8,128)(2,1)}, bf16[1,768,512]{2,1,0:T(8,128)(2,1)}, u32[]{:S(2)}, u32[]{:S(2)}) collective-permute-start(bf16[1,768,512]{2,1,0:T(8,128)(2,1)} %collective-permute-done.5.rest_7_), channel_id=1, source_target_pairs={{0,1},{1,2},{2,3},{3,0},{4,5},{5,6},{6,7},{7,4},{8,11},{9,8},{10,9... | collective-permute-start | bytes 2359304 | tf_op jit(solution)/shard_map/ppermute | solution.py:204
  133.8 5.0 %collective-permute-done.6.rest_0_ = bf16[1,768,512]{2,1,0:T(8,128)(2,1)} collective-permute-done((bf16[1,768,512]{2,1,0:T(8,128)(2,1)S(1)}, bf16[1,768,512]{2,1,0:T(8,128)(2,1)}, u32[]{:S(2)}, u32[]{:S(2)}) %collective-permute-start.6) | collective-permute-done | bytes 786464 | tf_op jit(solution)/shard_map/ppermute | solution.py:204
  138.9 0.0 copy-done.12
  138.9 3.0 %collective-permute-start.8 = (bf16[1,768,512]{2,1,0:T(8,128)(2,1)}, bf16[1,768,512]{2,1,0:T(8,128)(2,1)}, u32[]{:S(2)}, u32[]{:S(2)}) collective-permute-start(bf16[1,768,512]{2,1,0:T(8,128)(2,1)} %collective-permute-done.6.rest_0_), channel_id=1, source_target_pairs={{0,4},{1,5},{2,6},{3,7},{4,128},{5,129},{6,130},{7,131},{8,140},{9... | collective-permute-start | bytes 2359304 | tf_op jit(solution)/shard_map/ppermute | solution.py:204
  141.9 0.0 all-to-all-done.2
  141.9 0.0 copy-done.1
  141.9 0.0 copy-done.4
  141.9 0.0 copy-done.7
  141.9 0.0 copy-done.8
  141.9 1.4 third.1
  143.4 0.0 copy-start.10
  143.4 0.0 collective-permute-done.2.rest_4_
  143.4 2.6 %collective-permute-start.10 = (bf16[512,1024]{1,0:T(8,128)(2,1)S(1)}, bf16[512,1024]{1,0:T(8,128)(2,1)S(1)}, u32[]{:S(2)}, u32[]{:S(2)}) collective-permute-start(bf16[512,1024]{1,0:T(8,128)(2,1)S(1)} %get-tuple-element.16.normed), channel_id=1, source_target_pairs={{0,8},{1,9},{2,10},{3,11},{4,12},{5,13},{6,14},{7,15},{8,0},{9,1},... | collective-permute-start | bytes 3145736 | tf_op jit(solution)/shard_map/ppermute | solution.py:204
  146.0 0.0 collective-permute-done.4.rest_6_
  146.0 0.0 copy-done.3
  146.0 0.0 copy-done.13
  146.0 7.0 %own.1.before = f32[512,1024]{1,0:T(8,128)S(1)} custom-call(bf16[512,1024]{1,0:T(8,128)(2,1)S(1)} %get-tuple-element.16.normed, bf16[512,1024]{1,0:T(8,128)(2,1)S(1)} %get-tuple-element.17.before, bf16[1,768,512]{2,1,0:T(8,128)(2,1)S(1)} %bitcast.14, bf16[1,768,512]{2,1,0:T(8,128)(2,1)S(1)} %copy-done.3, bf16[1,2304,512]{2,1,0:T(8,128)(2,1)} %collective-permute-done.rest_2_, ...), custom_call_target="tpu_custom_call" | custom-call | flops 99999997952 | bytes 1 | tf_op jit(solution)/shard_map/own/pallas_call | solution.py:250
  153.0 0.0 copy-done.10
  153.0 0.0 collective-permute-done.10.normed
  153.0 7.0 %their.1.before = f32[512,1024]{1,0:T(8,128)S(1)} custom-call(bf16[512,1024]{1,0:T(8,128)(2,1)S(1)} %collective-permute-done.10.normed, f32[512,1024]{1,0:T(8,128)S(1)} %own.1.before, bf16[1,768,512]{2,1,0:T(8,128)(2,1)S(1)} %bitcast.15, bf16[1,768,512]{2,1,0:T(8,128)(2,1)S(1)} %copy-done.3, bf16[1,2304,512]{2,1,0:T(8,128)(2,1)} %collective-permute-done.rest_2_, ...), custom_call_target="tpu_custom_call" | custom-call | flops 99999997952 | bytes 1 | tf_op jit(solution)/shard_map/their/pallas_call | solution.py:250
  160.0 0.0 copy-start.11
  160.0 0.0 collective-permute-done.7.rest_1_
  160.0 0.0 collective-permute-done.9.rest_3_
  160.0 0.0 collective-permute-done.8.rest_2_
  160.0 3.6 %their_late.1 = bf16[512,1024]{1,0:T(8,128)(2,1)S(1)} custom-call(bf16[512,1024]{1,0:T(8,128)(2,1)S(1)} %collective-permute-done.10.normed, f32[512,1024]{1,0:T(8,128)S(1)} %their.1.before, bf16[1,768,512]{2,1,0:T(8,128)(2,1)} %collective-permute-done.6.rest_0_, bf16[1,768,512]{2,1,0:T(8,128)(2,1)} %collective-permute-done.7.rest_1_, ...), custom_call_target="tpu_custom_call" | custom-call | flops 99999997952 | bytes 1 | tf_op jit(solution)/shard_map/their_late/pallas_call | solution.py:250
  163.6 1.0 collective-permute-start.11
  164.6 0.0 copy-done.11
  164.6 3.5 %own_late.1.a = f32[512,1024]{1,0:T(8,128)S(1)} custom-call(bf16[512,1024]{1,0:T(8,128)(2,1)S(1)} %copy-done.11, f32[512,1024]{1,0:T(8,128)S(1)} %own.1.before, bf16[1,768,512]{2,1,0:T(8,128)(2,1)} %collective-permute-done.6.rest_0_, bf16[1,768,512]{2,1,0:T(8,128)(2,1)} %collective-permute-done.7.rest_1_, ...), custom_call_target="tpu_custom_call" | custom-call | flops 99999997952 | bytes 1 | tf_op jit(solution)/shard_map/own_late/pallas_call | solution.py:250
  168.1 0.0 collective-permute-done.11.b
  168.1 0.3 sum.1
  168.4 18.4 %all_to_all.21 = bf16[8,512,128]{2,1,0:T(8,128)(2,1)S(1)} all-to-all(bf16[8,512,128]{2,1,0:T(8,128)(2,1)S(1)} %sum.1), channel_id=1, replica_groups=mesh['seq'=32,'chan'=8] {'chan'}, dimensions={0} | all-to-all | bytes 2097152 | tf_op jit(solution)/shard_map/all_to_all | solution.py:283
  186.7 1.0 copy.15
  (12 shorter events, 0.0 us)
Async XLA Ops:
  0.0 7.4 %copy-start.14 = (bf16[1024,512]{1,0:T(8,128)(2,1)S(1)}, bf16[1024,512]{1,0:T(8,128)(2,1)}, u32[]{:S(2)}) copy-start(bf16[1024,512]{1,0:T(8,128)(2,1)} %param.24) | copy-start | bytes 3145732
  0.0 21.8 %all-to-all-start = ((bf16[8,512,128]{2,1,0:T(8,128)(2,1)}), bf16[8,512,128]{2,1,0:T(8,128)(2,1)S(1)}, u32[]{:S(2)}, u32[]{:S(2)}) async-start(bf16[8,512,128]{2,1,0:T(8,128)(2,1)} %bitcast.20), calls=%async_computation | async-start | bytes 2097152 | tf_op jit(solution)/shard_map/all_to_all | solution.py:189
  6.0 1.5 copy-start.15
  21.8 1.0 copy-start
  21.8 48.6 %collective-permute-start = (bf16[1,2304,512]{2,1,0:T(8,128)(2,1)}, bf16[1,2304,512]{2,1,0:T(8,128)(2,1)}, u32[]{:S(2)}, u32[]{:S(2)}) collective-permute-start(bf16[1,2304,512]{2,1,0:T(8,128)(2,1)} %maximum_bitcast_fusion), channel_id=1, source_target_pairs={{0,1},{1,2},{2,3},{3,0},{4,5},{5,6},{6,7},{7,4},{8,11},{9,8},{10,9... | collective-permute-start | bytes 7077896 | tf_op jit(solution)/shard_map/ppermute | solution.py:204
  22.8 50.7 %copy-start.2 = (bf16[256,16,128]{2,1,0:T(8,128)(2,1)S(1)}, bf16[256,16,128]{2,1,0:T(8,128)(2,1)}, u32[]{:S(2)}) copy-start(bf16[256,16,128]{2,1,0:T(8,128)(2,1)} %kern.1) | copy-start | bytes 3145732
  22.8 50.7 %copy-start.5 = (bf16[256,256]{1,0:T(8,128)(2,1)S(1)}, bf16[256,256]{1,0:T(8,128)(2,1)}, u32[]{:S(2)}) copy-start(bf16[256,256]{1,0:T(8,128)(2,1)} %left_in.1) | copy-start | bytes 393220
  22.8 50.7 %copy-start.6 = (bf16[256,256]{1,0:T(8,128)(2,1)S(1)}, bf16[256,256]{1,0:T(8,128)(2,1)}, u32[]{:S(2)}) copy-start(bf16[256,256]{1,0:T(8,128)(2,1)} %left_out.1) | copy-start | bytes 393220
  22.8 50.7 %copy-start.9 = (f32[128]{0:T(128)S(1)}, f32[128]{0:T(128)}, u32[]{:S(2)}) copy-start(f32[128]{0:T(128)} %param.14) | copy-start | bytes 1540
  70.4 75.5 %collective-permute-start.4 = (bf16[1,2304,512]{2,1,0:T(8,128)(2,1)}, bf16[1,2304,512]{2,1,0:T(8,128)(2,1)}, u32[]{:S(2)}, u32[]{:S(2)}) collective-permute-start(bf16[1,2304,512]{2,1,0:T(8,128)(2,1)} %collective-permute-done.rest_2_), channel_id=1, source_target_pairs={{0,4},{1,5},{2,6},{3,7},{4,128},{5,129},{6,130},{7,131},{8,140},{9... | collective-permute-start | bytes 7077896 | tf_op jit(solution)/shard_map/ppermute | solution.py:204
  76.7 65.2 %copy-start.1 = (bf16[8,512,128]{2,1,0:T(8,128)(2,1)S(1)}, bf16[8,512,128]{2,1,0:T(8,128)(2,1)}, u32[]{:S(2)}) copy-start(bf16[8,512,128]{2,1,0:T(8,128)(2,1)} %copy-done) | copy-start | bytes 3145732
  76.7 65.2 %copy-start.4 = (bf16[512,512]{1,0:T(8,128)(2,1)S(1)}, bf16[512,512]{1,0:T(8,128)(2,1)}, u32[]{:S(2)}) copy-start(bf16[512,512]{1,0:T(8,128)(2,1)} %right_hbm.1) | copy-start | bytes 1572868
  76.7 65.2 %copy-start.7 = (f32[8,512]{1,0:T(8,128)S(1)}, f32[8,512]{1,0:T(8,128)}, u32[]{:S(2)}) copy-start(f32[8,512]{1,0:T(8,128)} %tw.3) | copy-start | bytes 49156
  76.7 65.3 %copy-start.8 = (f32[1024]{0:T(1024)S(1)}, f32[1024]{0:T(1024)}, u32[]{:S(2)}) copy-start(f32[1024]{0:T(1024)} %param.22) | copy-start | bytes 12292
  76.7 65.2 %all-to-all-start.2 = ((bf16[256,16,128]{2,1,0:T(8,128)(2,1)}), bf16[256,16,128]{2,1,0:T(8,128)(2,1)S(1)}, u32[]{:S(2)}, u32[]{:S(2)}) async-start(bf16[256,16,128]{2,1,0:T(8,128)(2,1)} %middle.1), calls=%async_computation.2 | async-start | bytes 2097152 | tf_op jit(solution)/shard_map/all_to_all | solution.py:230
  82.9 36.3 %collective-permute-start.3 = (bf16[1,768,512]{2,1,0:T(8,128)(2,1)}, bf16[1,768,512]{2,1,0:T(8,128)(2,1)S(1)}, u32[]{:S(2)}, u32[]{:S(2)}) collective-permute-start(bf16[1,768,512]{2,1,0:T(8,128)(2,1)} %get-tuple-element.19.rest_1_), channel_id=1, source_target_pairs={{0,4},{1,5},{2,6},{3,7},{4,128},{5,129},{6,130},{7,131},{8,140},{9... | collective-permute-start | bytes 2359304 | tf_op jit(solution)/shard_map/ppermute | solution.py:204
  85.7 39.0 %collective-permute-start.1 = (bf16[1,768,512]{2,1,0:T(8,128)(2,1)}, bf16[1,768,512]{2,1,0:T(8,128)(2,1)}, u32[]{:S(2)}, u32[]{:S(2)}) collective-permute-start(bf16[1,768,512]{2,1,0:T(8,128)(2,1)} %get-tuple-element.19.rest_1_), channel_id=1, source_target_pairs={{0,1},{1,2},{2,3},{3,0},{4,5},{5,6},{6,7},{7,4},{8,11},{9,8},{10,9... | collective-permute-start | bytes 2359304 | tf_op jit(solution)/shard_map/ppermute | solution.py:204
  119.2 19.7 %copy-start.12 = (bf16[1,768,512]{2,1,0:T(8,128)(2,1)}, bf16[1,768,512]{2,1,0:T(8,128)(2,1)S(1)}, u32[]{:S(2)}) copy-start(bf16[1,768,512]{2,1,0:T(8,128)(2,1)S(1)} %collective-permute-done.3.rest_5_) | copy-start | bytes 2359300
  119.2 11.2 %collective-permute-start.5 = (bf16[1,768,512]{2,1,0:T(8,128)(2,1)S(1)}, bf16[1,768,512]{2,1,0:T(8,128)(2,1)}, u32[]{:S(2)}, u32[]{:S(2)}) collective-permute-start(bf16[1,768,512]{2,1,0:T(8,128)(2,1)S(1)} %collective-permute-done.3.rest_5_), channel_id=1, source_target_pairs={{0,1},{1,2},{2,3},{3,0},{4,5},{5,6},{6,7},{7,4},{8,11},{9,8},{10,9... | collective-permute-start | bytes 2359304 | tf_op jit(solution)/shard_map/ppermute | solution.py:204
  122.6 16.3 %collective-permute-start.6 = (bf16[1,768,512]{2,1,0:T(8,128)(2,1)S(1)}, bf16[1,768,512]{2,1,0:T(8,128)(2,1)}, u32[]{:S(2)}, u32[]{:S(2)}) collective-permute-start(bf16[1,768,512]{2,1,0:T(8,128)(2,1)S(1)} %slice.28), channel_id=1, source_target_pairs={{0,1},{1,2},{2,3},{3,0},{4,5},{5,6},{6,7},{7,4},{8,11},{9,8},{10,9... | collective-permute-start | bytes 2359304 | tf_op jit(solution)/shard_map/ppermute | solution.py:204
  122.9 20.4 %collective-permute-start.2 = (bf16[1,768,512]{2,1,0:T(8,128)(2,1)S(1)}, bf16[1,768,512]{2,1,0:T(8,128)(2,1)}, u32[]{:S(2)}, u32[]{:S(2)}) collective-permute-start(bf16[1,768,512]{2,1,0:T(8,128)(2,1)S(1)} %bitcast.13), channel_id=1, source_target_pairs={{0,4},{1,5},{2,6},{3,7},{4,128},{5,129},{6,130},{7,131},{8,140},{9... | collective-permute-start | bytes 2359304 | tf_op jit(solution)/shard_map/ppermute | solution.py:204
  124.7 35.3 %collective-permute-start.7 = (bf16[1,768,512]{2,1,0:T(8,128)(2,1)}, bf16[1,768,512]{2,1,0:T(8,128)(2,1)}, u32[]{:S(2)}, u32[]{:S(2)}) collective-permute-start(bf16[1,768,512]{2,1,0:T(8,128)(2,1)} %collective-permute-done.1.rest_3_), channel_id=1, source_target_pairs={{0,1},{1,2},{2,3},{3,0},{4,5},{5,6},{6,7},{7,4},{8,11},{9,8},{10,9... | collective-permute-start | bytes 2359304 | tf_op jit(solution)/shard_map/ppermute | solution.py:204
  130.4 29.5 %collective-permute-start.9 = (bf16[1,768,512]{2,1,0:T(8,128)(2,1)}, bf16[1,768,512]{2,1,0:T(8,128)(2,1)}, u32[]{:S(2)}, u32[]{:S(2)}) collective-permute-start(bf16[1,768,512]{2,1,0:T(8,128)(2,1)} %collective-permute-done.5.rest_7_), channel_id=1, source_target_pairs={{0,1},{1,2},{2,3},{3,0},{4,5},{5,6},{6,7},{7,4},{8,11},{9,8},{10,9... | collective-permute-start | bytes 2359304 | tf_op jit(solution)/shard_map/ppermute | solution.py:204
  138.9 21.1 %collective-permute-start.8 = (bf16[1,768,512]{2,1,0:T(8,128)(2,1)}, bf16[1,768,512]{2,1,0:T(8,128)(2,1)}, u32[]{:S(2)}, u32[]{:S(2)}) collective-permute-start(bf16[1,768,512]{2,1,0:T(8,128)(2,1)} %collective-permute-done.6.rest_0_), channel_id=1, source_target_pairs={{0,4},{1,5},{2,6},{3,7},{4,128},{5,129},{6,130},{7,131},{8,140},{9... | collective-permute-start | bytes 2359304 | tf_op jit(solution)/shard_map/ppermute | solution.py:204
  141.9 4.1 %copy-start.3 = (bf16[1,768,512]{2,1,0:T(8,128)(2,1)S(1)}, bf16[1,768,512]{2,1,0:T(8,128)(2,1)}, u32[]{:S(2)}) copy-start(bf16[1,768,512]{2,1,0:T(8,128)(2,1)} %get-tuple-element.19.rest_1_) | copy-start | bytes 2359300
  141.9 4.1 %copy-start.13 = (bf16[1,768,512]{2,1,0:T(8,128)(2,1)S(1)}, bf16[1,768,512]{2,1,0:T(8,128)(2,1)}, u32[]{:S(2)}) copy-start(bf16[1,768,512]{2,1,0:T(8,128)(2,1)} %copy-done.12) | copy-start | bytes 2359300
  143.4 9.6 %copy-start.10 = (bf16[512,1024]{1,0:T(8,128)(2,1)}, bf16[512,1024]{1,0:T(8,128)(2,1)S(1)}, u32[]{:S(2)}) copy-start(bf16[512,1024]{1,0:T(8,128)(2,1)S(1)} %get-tuple-element.16.normed) | copy-start | bytes 3145732
  143.4 9.6 %collective-permute-start.10 = (bf16[512,1024]{1,0:T(8,128)(2,1)S(1)}, bf16[512,1024]{1,0:T(8,128)(2,1)S(1)}, u32[]{:S(2)}, u32[]{:S(2)}) collective-permute-start(bf16[512,1024]{1,0:T(8,128)(2,1)S(1)} %get-tuple-element.16.normed), channel_id=1, source_target_pairs={{0,8},{1,9},{2,10},{3,11},{4,12},{5,13},{6,14},{7,15},{8,0},{9,1},... | collective-permute-start | bytes 3145736 | tf_op jit(solution)/shard_map/ppermute | solution.py:204
  160.0 4.6 %copy-start.11 = (bf16[512,1024]{1,0:T(8,128)(2,1)S(1)}, bf16[512,1024]{1,0:T(8,128)(2,1)}, u32[]{:S(2)}) copy-start(bf16[512,1024]{1,0:T(8,128)(2,1)} %copy-done.10) | copy-start | bytes 3145732
  163.6 4.5 %collective-permute-start.11 = (bf16[512,1024]{1,0:T(8,128)(2,1)S(1)}, bf16[512,1024]{1,0:T(8,128)(2,1)S(1)}, u32[]{:S(2)}, u32[]{:S(2)}) collective-permute-start(bf16[512,1024]{1,0:T(8,128)(2,1)S(1)} %their_late.1), channel_id=1, source_target_pairs={{0,8},{1,9},{2,10},{3,11},{4,12},{5,13},{6,14},{7,15},{8,0},{9,1},... | collective-permute-start | bytes 3145736 | tf_op jit(solution)/shard_map/ppermute | solution.py:204
